TPU v7x, 768 devices: a whole 4x8x12 slice. The times are simulated.
768 devices in a mesh: owner: 48 (over z, x), reader: 16 (over y, core).
Axes of the slice: x: 4, y: 8, z: 12, core: 2. Of those that a mesh axis runs over, the one named last changes fastest.
Arguments:
- table: float32 [49152, 128], P('owner'), may hold values from -3 to 3
- accum: float32 [49152], P('owner'), may hold values from 0.001 to 0.1
- serve: int32 [48, 16, 48, 128], P('owner', 'reader'), may hold values from 0 to 1023, as said below
- counts: int32 [48, 16, 48], P('owner', 'reader'), may hold values from 16 to 128, as said below
- slot_map: int32 [48, 16, 6144], P('owner', 'reader'), may hold values from 0 to 6143, each once within a row
- bag_rows: int32 [196608, 4, 8], P(('owner', 'reader')), may hold values from 0 to 6143
- bag_len: int32 [196608, 4], P(('owner', 'reader')), may hold values from 1 to 8
- labels: int32 [196608], P(('owner', 'reader')), may hold values 0 or 1
- w1: bfloat16 [512, 1024], replicated, may hold values from -0.25 to 0.25
- b1: float32 [1024], replicated, may hold values from -3 to 3
- w2: bfloat16 [1024], replicated, may hold values from -0.1875 to 0.1875
Outputs:
- new_table: float32 [49152, 128], P('owner')
- new_accum: float32 [49152], P('owner')
- row_grad: float32 [49152, 128], P('owner')
- w1_grad: float32 [512, 1024], replicated
- w2_grad: float32 [1024], replicated
- logits: float32 [196608], P(('owner', 'reader'))
Inputs may be any that keep to these rules, and one draw needn't show every extreme that they name: serve[o, r, p, s] is a row number of owner index o, 0 to 1023, and equal for r and r + 1 with r even. counts are equal for r and r + 1 with r even; each (o, r) has some p with a full block. Each slot_map[p, r] is a permutation of 0 to 6143.
All inputs are finite; a program needn't handle non-finite values. No bound on the sum of `labels` on one device may be relied on, other than what follows from the above.
Results may differ from a plain program's by a relative error of at most 0.0043.
Values may be sent and summed in bfloat16 or wider, within the bound.
No kernel may reach another device: no remote copies, remote signals or barrier semaphores. Data moves between devices by JAX's collectives and lax.ppermute only.
A program may use at most 64 MiB of HBM per device.

v0:
```python
import jax
import jax.numpy as jnp
from jax import lax
from jax.sharding import PartitionSpec as P

LEARN_RATE = 0.05


def partner(shard, axis, stride):
    return lax.ppermute(shard, axis, [(i, i ^ 1 << stride) for i in range(lax.axis_size(axis))])


def on_device(table, accum, serve, counts, slot_map, bag_rows, bag_len, labels, w1, b1, w2):
    lists = serve[0, 0]
    limits = counts[0, 0]
    n_peers, slots = lists.shape
    width = table.shape[1]
    half = slots // 2
    parity = lax.axis_index("reader") % 2
    valid = jnp.arange(slots, dtype=jnp.int32)[None, :] < limits[:, None]
    own_lists = lax.dynamic_slice_in_dim(lists, parity * half, half, 1)
    own_valid = lax.dynamic_slice_in_dim(valid, parity * half, half, 1)
    picked = jnp.where(valid[:, :, None], table[lists], 0.0).astype(jnp.bfloat16)
    cache_rows = lax.all_to_all(picked, "owner", split_axis=0, concat_axis=0, tiled=True)
    cache_size = n_peers * slots
    flat_rows = cache_rows.reshape(cache_size, width)
    places = slot_map[0, 0]
    source = (
        jnp.zeros((cache_size,), jnp.int32).at[places].set(jnp.arange(cache_size, dtype=jnp.int32))
    )
    entries = source[bag_rows]
    batch, feats, depth = bag_rows.shape
    inside = jnp.arange(depth, dtype=jnp.int32)[None, None, :] < bag_len[:, :, None]
    pooled_sum = jnp.zeros((batch, feats, width), jnp.float32)
    for level in range(depth):
        rows_here = flat_rows[entries[:, :, level]]
        pooled_sum = pooled_sum + jnp.where(
            inside[:, :, level, None], rows_here.astype(jnp.float32), 0.0
        )
    pooled = pooled_sum.reshape(batch, feats * width).astype(jnp.bfloat16)
    pre = jnp.dot(pooled, w1, preferred_element_type=jnp.float32) + b1
    sig_pre = jax.nn.sigmoid(pre)
    active = pre * sig_pre
    w2_wide = w2.astype(jnp.float32)
    logits = jnp.dot(active, w2_wide, precision=lax.Precision.HIGHEST)
    error = jax.nn.sigmoid(logits) - labels.astype(jnp.float32)
    part_w2 = jnp.dot(error, active, precision=lax.Precision.HIGHEST)
    slope = sig_pre * (1.0 + pre * (1.0 - sig_pre))
    grad_pre = (error[:, None] * w2_wide[None, :] * slope).astype(jnp.bfloat16)
    part_w1 = lax.dot_general(
        pooled, grad_pre, (((0,), (0,)), ((), ())), preferred_element_type=jnp.float32
    )
    grad_pooled = lax.dot_general(
        grad_pre, w1, (((1,), (1,)), ((), ())), preferred_element_type=jnp.float32
    )
    w1_grad, w2_grad = lax.psum((part_w1, part_w2), ("owner", "reader"))
    grad_three = grad_pooled.reshape(batch, feats, width)
    slot_grad = jnp.zeros((cache_size, width), jnp.float32)
    for level in range(depth):
        level_terms = jnp.where(inside[:, :, level, None], grad_three, 0.0).reshape(-1, width)
        slot_grad = slot_grad.at[entries[:, :, level].reshape(-1)].add(level_terms)
    slot_grad = slot_grad.reshape(n_peers, slots, width)
    keeping = lax.dynamic_slice_in_dim(slot_grad, parity * half, half, 1)
    giving = lax.dynamic_slice_in_dim(slot_grad, (1 - parity) * half, half, 1)
    summed = keeping + partner(giving, "reader", 0)
    returned = lax.all_to_all(summed, "owner", split_axis=0, concat_axis=0, tiled=True)
    returned = jnp.where(own_valid[:, :, None], returned, 0.0)
    local_grad = jax.ops.segment_sum(
        returned.reshape(-1, width), own_lists.reshape(-1), num_segments=table.shape[0]
    )
    row_grad = lax.psum(local_grad, "reader")
    new_accum = accum + jnp.mean(row_grad * row_grad, axis=1)
    new_table = table - LEARN_RATE * row_grad / jnp.sqrt(new_accum)[:, None]
    return (new_table, new_accum, row_grad, w1_grad, w2_grad, logits)


def solution(mesh):
    return jax.shard_map(
        on_device,
        mesh=mesh,
        in_specs=(
            P("owner", None),
            P("owner"),
            P("owner", "reader", None, None),
            P("owner", "reader", None),
            P("owner", "reader", None),
            P(("owner", "reader"), None, None),
            P(("owner", "reader"), None),
            P(("owner", "reader")),
            P(),
            P(),
            P(),
        ),
        out_specs=(
            P("owner", None),
            P("owner"),
            P("owner", None),
            P(),
            P(),
            P(("owner", "reader")),
        ),
        check_vma=False,
    )
```

profile of v0, /device:TPU:1, one launch (start us, length us, event | category | flops | bytes accessed | tf_op | source)
XLA Modules:
  0.0 1070.0 jit_solution(7731664489802856359)
XLA Ops:
  8.8 17.5 %gather_fusion.1 = bf16[6144,128]{1,0:T(8,128)(2,1)S(1)} fusion(f32[1024,128]{1,0:T(8,128)} %param.11, s32[6144]{0:T(1024)S(1)} %fusion.62), kind=kCustom, calls=%fused_computation.1 | custom fusion | bytes 3170304 | tf_op jit(solution)/shard_map/gather | solution.py:23
  28.7 19.2 %all-to-all-start = ((bf16[48,128,128]{2,1,0:T(8,128)(2,1)}), bf16[48,128,128]{2,1,0:T(8,128)(2,1)}, u32[]{:S(2)}, u32[]{:S(2)}) async-start(bf16[48,128,128]{2,1,0:T(8,128)(2,1)} %select_convert_fusion), calls=%async_computation | async-start | bytes 3145728 | tf_op jit(solution)/shard_map/all_to_all | solution.py:24
  56.6 23.0 %scatter_custom_fusion = s32[6144]{0:T(1024)S(1)} fusion(s32[6144]{0:T(1024)S(1)} %bitcast.100, s32[6144]{0:T(1024)S(1)} %iota.15, s32[]{:T(128)} %constant.13.clone.1), kind=kCustom, calls=%fused_computation.127 | custom fusion | bytes 24580 | tf_op jit(solution)/shard_map/scatter | solution.py:29
  79.6 45.5 %gather_fusion = s32[8192]{0:T(1024)S(1)} fusion(s32[6144]{0:T(1024)S(1)} %scatter_custom_fusion, s32[8192]{0:T(1024)S(1)} %broadcast_clamp_fusion), kind=kCustom, calls=%fused_computation | custom fusion | bytes 98304 | tf_op jit(solution)/shard_map/gather | solution.py:31
  125.8 100.3 %slice_reduce_fusion = (s32[256,4]{1,0:T(8,128)}, s32[256,4]{1,0:T(8,128)S(1)}, s32[256,4]{1,0:T(8,128)S(1)}, s32[256,4]{1,0:T(8,128)S(1)}, s32[256,4]{1,0:T(8,1...) fusion(s32[256,4,8]{2,1,0:T(4,128)S(1)} %reshape.420), kind=kLoop, calls=%fused_computation.79 | loop fusion | flops 24576 | bytes 98304 | tf_op jit(solution)/shard_map/slice | solution.py:36
  232.7 4.5 gather_fusion.9
  237.2 4.5 gather_fusion.8
  241.7 4.5 gather_fusion.7
  246.2 4.5 gather_fusion.6
  250.7 4.5 gather_fusion.5
  255.3 4.5 gather_fusion.4
  259.8 4.5 gather_fusion.3
  264.3 4.5 gather_fusion.2
  268.8 4.6 fusion.12
  275.6 8.6 scatter_custom_fusion.1
  284.2 9.7 scatter_custom_fusion.2
  293.9 9.9 scatter_custom_fusion.3
  303.8 9.7 scatter_custom_fusion.4
  313.5 9.7 scatter_custom_fusion.5
  323.2 9.7 scatter_custom_fusion.6
  332.9 9.6 scatter_custom_fusion.7
  342.5 9.8 scatter_custom_fusion.8
  355.0 2.9 collective-permute-start
  357.9 3.2 collective-permute-done
  363.9 12.1 %all-to-all-start.1 = ((f32[48,64,128]{2,1,0:T(8,128)}), f32[48,64,128]{2,1,0:T(8,128)S(1)}, u32[]{:S(2)}, u32[]{:S(2)}) async-start(f32[48,64,128]{2,1,0:T(8,128)} %dynamic-slice_add_fusion), calls=%async_computation.1 | async-start | bytes 3145728 | tf_op jit(solution)/shard_map/all_to_all | solution.py:66
  376.3 55.7 %all-to-all-done.1 = f32[48,64,128]{2,1,0:T(8,128)S(1)} async-done(((f32[48,64,128]{2,1,0:T(8,128)}), f32[48,64,128]{2,1,0:T(8,128)S(1)}, u32[]{:S(2)}, u32[]{:S(2)}) %all-to-all-start.1) | async-done | bytes 1572896 | tf_op jit(solution)/shard_map/all_to_all | solution.py:66
  433.4 18.0 %scatter_custom_fusion.9 = f32[1024,128]{1,0:T(8,128)} fusion(s32[3072]{0:T(1024)S(1)} %reshape.573, f32[3072,128]{1,0:T(8,128)} %bitcast.89, f32[]{:T(128)} %constant.12.clone.1), kind=kCustom, calls=%fused_computation.90 | custom fusion | flops 393216 | bytes 524800 | tf_op jit(solution)/shard_map/scatter-add | solution.py:68
  451.5 3.4 fusion.34
  455.7 108.6 %psum.23 = f32[1024]{0:T(1024)} all-reduce(f32[1024]{0:T(1024)S(1)} %bitcast.109), channel_id=1, replica_groups=mesh['owner'=48,'reader'=16] {'owner','reader'}, use_global_device_ids=true, to_apply=%region_13.14 | all-reduce | flops 1024 | bytes 8192 | tf_op jit(solution)/shard_map/psum | solution.py:56
  564.3 5.5 all-reduce.3.cloned.1.call-done
  573.7 484.0 %all-reduce.5.cloned.1.call-done = f32[512,1024]{1,0:T(8,128)} async-done(((f32[512,1024]{1,0:T(8,128)}), f32[512,1024]{1,0:T(8,128)}) %all-reduce.5.cloned.1.call-update) | async-done | bytes 2097168 | tf_op jit(solution)/shard_map/psum | solution.py:56
  1059.5 3.2 copy.39
  (134 shorter events, 35.8 us)
Async XLA Ops:
  7.2 266.3 %copy-start = (bf16[512,1024]{1,0:T(8,128)(2,1)S(1)}, bf16[512,1024]{1,0:T(8,128)(2,1)}, u32[]{:S(2)}) copy-start(bf16[512,1024]{1,0:T(8,128)(2,1)} %param.19) | copy-start | bytes 3145732
  8.0 18.3 %copy-start.9 = (pred[48,128]{1,0:T(8,128)(4,1)}, pred[48,128]{1,0:T(8,128)(4,1)S(1)}, u32[]{:S(2)}) copy-start(pred[48,128]{1,0:T(8,128)(4,1)S(1)} %iota_compare_fusion.1) | copy-start | bytes 18436
  26.3 21.6 %copy-start.12 = (s32[1,1,6144]{2,1,0:T(1,128)S(1)}, s32[1,1,6144]{2,1,0:T(1,128)}, u32[]{:S(2)}) copy-start(s32[1,1,6144]{2,1,0:T(1,128)} %param.15) | copy-start | bytes 73732
  26.3 21.6 %copy-start.23 = (s32[256,4]{0,1:T(4,128)S(1)}, s32[256,4]{0,1:T(4,128)}, u32[]{:S(2)}) copy-start(s32[256,4]{0,1:T(4,128)} %param.17) | copy-start | bytes 12292
  26.3 22.7 %copy-start.13 = (bf16[1024]{0:T(1024)(128)(2,1)S(1)}, bf16[1024]{0:T(1024)(128)(2,1)}, u32[]{:S(2)}) copy-start(bf16[1024]{0:T(1024)(128)(2,1)} %param.21) | copy-start | bytes 6148
  28.7 27.1 %copy-start.11 = (s32[256,4,8]{0,2,1:T(8,128)S(1)}, s32[256,4,8]{0,2,1:T(8,128)}, u32[]{:S(2)}) copy-start(s32[256,4,8]{0,2,1:T(8,128)} %param.16) | copy-start | bytes 98308
  28.7 204.0 %all-to-all-start = ((bf16[48,128,128]{2,1,0:T(8,128)(2,1)}), bf16[48,128,128]{2,1,0:T(8,128)(2,1)}, u32[]{:S(2)}, u32[]{:S(2)}) async-start(bf16[48,128,128]{2,1,0:T(8,128)(2,1)} %select_convert_fusion), calls=%async_computation | async-start | bytes 3145728 | tf_op jit(solution)/shard_map/all_to_all | solution.py:24
  255.2 13.6 %copy-start.4 = (pred[256,4]{1,0:T(8,128)(4,1)S(1)}, pred[256,4]{1,0:T(8,128)(4,1)}, u32[]{:S(2)}) copy-start(pred[256,4]{1,0:T(8,128)(4,1)} %get-tuple-element.25) | copy-start | bytes 3076
  255.2 13.6 %copy-start.5 = (pred[256,4]{1,0:T(8,128)(4,1)S(1)}, pred[256,4]{1,0:T(8,128)(4,1)}, u32[]{:S(2)}) copy-start(pred[256,4]{1,0:T(8,128)(4,1)} %get-tuple-element.26) | copy-start | bytes 3076
  255.2 13.6 %copy-start.6 = (pred[256,4]{1,0:T(8,128)(4,1)S(1)}, pred[256,4]{1,0:T(8,128)(4,1)}, u32[]{:S(2)}) copy-start(pred[256,4]{1,0:T(8,128)(4,1)} %get-tuple-element.27) | copy-start | bytes 3076
  255.2 13.6 %copy-start.7 = (pred[256,4]{1,0:T(8,128)(4,1)S(1)}, pred[256,4]{1,0:T(8,128)(4,1)}, u32[]{:S(2)}) copy-start(pred[256,4]{1,0:T(8,128)(4,1)} %get-tuple-element.28) | copy-start | bytes 3076
  264.3 9.2 copy-start.14
  264.3 9.7 copy-start.25
  273.5 1.3 copy-start.27
  273.5 1.5 copy-start.24
  274.0 1.0 copy-start.2
  275.6 8.6 copy-start.21
  275.6 18.3 %copy-start.20 = (pred[1024]{0:T(1024)(128)(4,1)S(1)}, pred[1024]{0:T(1024)(128)(4,1)}, u32[]{:S(2)}) copy-start(pred[1024]{0:T(1024)(128)(4,1)} %broadcast_in_dim.221) | copy-start | bytes 3076
  284.2 19.6 %copy-start.19 = (pred[1024]{0:T(1024)(128)(4,1)S(1)}, pred[1024]{0:T(1024)(128)(4,1)}, u32[]{:S(2)}) copy-start(pred[1024]{0:T(1024)(128)(4,1)} %broadcast_in_dim.223) | copy-start | bytes 3076
  293.9 19.6 %copy-start.18 = (pred[1024]{0:T(1024)(128)(4,1)S(1)}, pred[1024]{0:T(1024)(128)(4,1)}, u32[]{:S(2)}) copy-start(pred[1024]{0:T(1024)(128)(4,1)} %broadcast_in_dim.225) | copy-start | bytes 3076
  303.8 19.4 %copy-start.17 = (pred[1024]{0:T(1024)(128)(4,1)S(1)}, pred[1024]{0:T(1024)(128)(4,1)}, u32[]{:S(2)}) copy-start(pred[1024]{0:T(1024)(128)(4,1)} %broadcast_in_dim.227) | copy-start | bytes 3076
  313.5 19.4 %copy-start.16 = (pred[1024]{0:T(1024)(128)(4,1)S(1)}, pred[1024]{0:T(1024)(128)(4,1)}, u32[]{:S(2)}) copy-start(pred[1024]{0:T(1024)(128)(4,1)} %broadcast_in_dim.229) | copy-start | bytes 3076
  323.2 19.3 %copy-start.15 = (pred[1024]{0:T(1024)(128)(4,1)S(1)}, pred[1024]{0:T(1024)(128)(4,1)}, u32[]{:S(2)}) copy-start(pred[1024]{0:T(1024)(128)(4,1)} %broadcast_in_dim.231) | copy-start | bytes 3076
  355.0 6.1 collective-permute-start
  357.9 18.2 %copy-start.8 = (s32[1,1,48,128]{3,2,1,0:T(8,128)S(1)}, s32[1,1,48,128]{3,2,1,0:T(8,128)}, u32[]{:S(2)}) copy-start(s32[1,1,48,128]{3,2,1,0:T(8,128)} %param.13) | copy-start | bytes 73732
  357.9 18.3 %copy-start.10 = (pred[48,128]{1,0:T(8,128)(4,1)S(1)}, pred[48,128]{1,0:T(8,128)(4,1)}, u32[]{:S(2)}) copy-start(pred[48,128]{1,0:T(8,128)(4,1)} %copy-done.9) | copy-start | bytes 18436
  363.9 68.1 %all-to-all-start.1 = ((f32[48,64,128]{2,1,0:T(8,128)}), f32[48,64,128]{2,1,0:T(8,128)S(1)}, u32[]{:S(2)}, u32[]{:S(2)}) async-start(f32[48,64,128]{2,1,0:T(8,128)} %dynamic-slice_add_fusion), calls=%async_computation.1 | async-start | bytes 3145728 | tf_op jit(solution)/shard_map/all_to_all | solution.py:66
  376.0 193.8 %all-reduce.3.cloned.1.call-start = ((), (), s32[]{:S(2)}) async-start(), calls=%async_computation.2 | async-start | bytes 1048576 | tf_op jit(solution)/shard_map/psum | solution.py:71
  451.4 3.5 copy-start.3
  451.4 606.2 %all-reduce.5.cloned.1.call-start = ((), (), s32[]{:S(2)}) async-start(), calls=%async_computation.3 | async-start | bytes 4194304 | tf_op jit(solution)/shard_map/psum | solution.py:56
  454.9 116.2 %copy-start.26 = (f32[1024]{0:T(1024)S(1)}, f32[1024]{0:T(1024)}, u32[]{:S(2)}) copy-start(f32[1024]{0:T(1024)} %param.12) | copy-start | bytes 12292
  454.9 116.8 %copy-start.1 = (f32[1024,128]{1,0:T(8,128)S(1)}, f32[1024,128]{1,0:T(8,128)}, u32[]{:S(2)}) copy-start(f32[1024,128]{1,0:T(8,128)} %param.11) | copy-start | bytes 1572868
  (2 other events, 1.5 us)
Sparse Core Ops, SparseCore 0:
  451.6 118.1 all-reduce.2
  576.7 480.9 all-reduce.4
where the time goes:
time: 1080 us; the launch traced here: 1070 us
  waiting for transfers between devices  548 us (51%)
  other arithmetic  216 us (20%)
  local copies, waits for them, and re-layouts  142 us (13%)
  blocking collectives  109 us (10%)
  starting transfers between devices  34.2 us (3%)
  between operations  15.1 us (1%)
    psum x1, waiting for transfers between devices, on_device(): w1_grad, w2_grad = lax.psum((part_w1, part_w2), ('owner', 'reader'))  484 us
    psum x1, blocking collectives, on_device(): w1_grad, w2_grad = lax.psum((part_w1, part_w2), ('owner', 'reader'))  109 us
    slice x1, other arithmetic, on_device(): rows_here = flat_rows[entries[:, :, level]]  100 us
    scatter-add x8, other arithmetic, on_device(): slot_grad = slot_grad.at[entries[:, :, level].reshape(-1)].add(level_terms)  76.6 us
    all_to_all x1, waiting for transfers between devices, on_device(): lax.all_to_all(summed, 'owner', split_axis=0, concat_axis=0, tiled=True)  55.7 us
    gather x2, local copies, waits for them, and re-layouts, on_device(): entries = source[bag_rows]  46.2 us
    gather x8, local copies, waits for them, and re-layouts, on_device(): rows_here = flat_rows[entries[:, :, level]]  35.9 us
    scatter x1, local copies, waits for them, and re-layouts, on_device(): jnp.zeros((cache_size,), jnp.int32).at[places]  23 us
  transfers between devices with their start and end apart: 5, of which 4 were waited for; matrix products, arithmetic and copies ran while one was open for 18% of the time, Pallas kernels for 0%

commit v1 on v0

v1 whole, which is shorter than its diff:
```python
import functools

import jax
import jax.numpy as jnp
from jax import lax
from jax.experimental import pallas as pl
from jax.experimental.pallas import tpu as pltpu
from jax.sharding import PartitionSpec as P

LEARN_RATE = 0.05
LANES = 128
bf16 = jnp.bfloat16
f32 = jnp.float32
VMEM = pl.BlockSpec(memory_space=pltpu.VMEM)
PARAMS = pltpu.CompilerParams(vmem_limit_bytes=48 * 1024 * 1024)


def fetch_kernel(slot_ref, table_ref, out_ref):
    table = table_ref[...].astype(bf16)
    rows = lax.broadcasted_iota(jnp.int32, (LANES, table.shape[0]), 1)
    for k in range(slot_ref.shape[1]):
        hot = jnp.where(slot_ref[:, k : k + 1] == rows, 1.0, 0.0).astype(bf16)
        picked = jnp.dot(hot, table, preferred_element_type=f32)
        out_ref[k * LANES : (k + 1) * LANES, :] = picked.astype(bf16)


def fetch(slot_cols, table):
    slots = slot_cols.shape[1] * LANES
    return pl.pallas_call(
        fetch_kernel,
        out_shape=jax.ShapeDtypeStruct((slots, table.shape[1]), bf16),
        in_specs=[VMEM] * 2,
        out_specs=VMEM,
        compiler_params=PARAMS,
        name="fetch",
    )(slot_cols, table)


def row_sum_kernel(slot_ref, value_ref, out_ref):
    n = out_ref.shape[0]
    iota = lax.broadcasted_iota(jnp.int32, (n, LANES), 0)
    total = jnp.zeros(out_ref.shape, f32)
    for k in range(0, slot_ref.shape[0], 2):
        hot = jnp.concatenate(
            [jnp.where(slot_ref[j : j + 1, :] == iota, 1.0, 0.0).astype(bf16) for j in (k, k + 1)],
            axis=1,
        )
        values = value_ref[k * LANES : (k + 2) * LANES, :]
        total = total + jnp.dot(hot, values, preferred_element_type=f32)
    out_ref[...] = total.astype(out_ref.dtype)


def row_sum(slot_rows, values, n):
    return pl.pallas_call(
        row_sum_kernel,
        out_shape=jax.ShapeDtypeStruct((n, values.shape[1]), bf16),
        in_specs=[VMEM] * 2,
        out_specs=VMEM,
        compiler_params=PARAMS,
        name="row_sum",
    )(slot_rows, values)


def count_kernel(bag_ref, place_ref, out_ref):
    group = 16
    one, zero = jnp.ones((), bf16), jnp.zeros((), bf16)

    def step(g, carry):
        rows = pl.ds(pl.multiple_of(g * group, group), group)
        bags = bag_ref[rows, :]
        names = [
            jnp.broadcast_to(bags[:, l : l + 1], (group, LANES)).astype(jnp.int16)
            for l in range(bags.shape[1])
        ]
        for t in range(out_ref.shape[1] // LANES):
            cols = slice(t * LANES, (t + 1) * LANES)
            place = jnp.broadcast_to(place_ref[0, :, cols], (group, LANES)).astype(jnp.int16)
            total = jnp.zeros((group, LANES), bf16)
            for name in names:
                total = total + jnp.where(name == place, one, zero)
            out_ref[rows, cols] = total
        return carry

    lax.fori_loop(0, out_ref.shape[0] // group, step, 0)


def count(bags, places):
    n_bags, depth = bags.shape
    sides, _, slots = places.shape
    block = 128
    per = n_bags // sides // block
    return pl.pallas_call(
        count_kernel,
        grid=(n_bags // block,),
        out_shape=jax.ShapeDtypeStruct((n_bags, slots), bf16),
        in_specs=[
            pl.BlockSpec((block, depth), lambda i: (i, 0)),
            pl.BlockSpec((1, 1, slots), lambda i: (i // per, 0, 0)),
        ],
        out_specs=pl.BlockSpec((block, slots), lambda i: (i, 0)),
        compiler_params=PARAMS,
        cost_estimate=pl.CostEstimate(
            flops=n_bags * slots * depth * 2,
            bytes_accessed=n_bags * slots * 2,
            transcendentals=0,
        ),
        name="count",
    )(bags, places)


def top_kernel(own_ref, got_ref, w1_ref, b1_ref, w2_ref, label_ref, logit_ref, part_ref, g_ref):
    batch = label_ref.shape[0]
    feats = own_ref.shape[0] // batch
    spans = [slice(f * batch, (f + 1) * batch) for f in range(feats)]
    pooled = jnp.concatenate([(own_ref[s, :] + got_ref[s, :]).astype(bf16) for s in spans], axis=1)
    w1 = w1_ref[...]
    pre = jnp.dot(pooled, w1, preferred_element_type=f32) + b1_ref[...]
    sig_pre = jax.nn.sigmoid(pre)
    active = pre * sig_pre
    w2 = w2_ref[...].astype(f32)
    logits = jnp.sum(active * w2, axis=1, keepdims=True)
    logit_ref[...] = logits
    error = jax.nn.sigmoid(logits) - label_ref[...].astype(f32)
    part_w2 = jnp.sum(error * active, axis=0, keepdims=True)
    slope = sig_pre * (1.0 + pre * (1.0 - sig_pre))
    grad_pre = (error * w2 * slope).astype(bf16)
    grad_pooled = lax.dot_general(
        grad_pre, w1, (((1,), (1,)), ((), ())), preferred_element_type=f32
    )
    for f, s in enumerate(spans):
        g_ref[s, :] = grad_pooled[:, f * LANES : (f + 1) * LANES].astype(bf16)
    part_w1 = lax.dot_general(
        pooled, grad_pre, (((0,), (0,)), ((), ())), preferred_element_type=f32
    )
    chunks = part_ref.shape[0]
    depth, blocks = part_w1.shape[0] // chunks, part_w1.shape[1] // LANES
    for j in range(blocks):
        block = part_w1[:, j * LANES : (j + 1) * LANES].astype(bf16)
        part_ref[:, j * depth : (j + 1) * depth, :] = block.reshape(chunks, depth, LANES)
    part_ref[:, blocks * depth :, :] = jnp.zeros((chunks, 16, LANES), bf16)
    tail = [part_w2[:, j * LANES : (j + 1) * LANES] for j in range(blocks)]
    tail = jnp.concatenate(tail + [jnp.zeros((16 - blocks, LANES), f32)], axis=0)
    part_ref[0, blocks * depth :, :] = tail.astype(bf16)


def top(own, got, w1, b1, w2, labels, chunks):
    batch = labels.shape[0]
    depth = w1.size // chunks // LANES + 16
    return pl.pallas_call(
        top_kernel,
        out_shape=(
            jax.ShapeDtypeStruct((batch, 1), f32),
            jax.ShapeDtypeStruct((chunks, depth, LANES), bf16),
            jax.ShapeDtypeStruct(own.shape, bf16),
        ),
        in_specs=[VMEM] * 6,
        out_specs=(VMEM,) * 3,
        compiler_params=PARAMS,
        name="top",
    )(own, got, w1, b1, w2, labels)


def partner(shard):
    return lax.ppermute(shard, "reader", [(i, i ^ 1) for i in range(lax.axis_size("reader"))])


def exchange(blocks, axis):
    return lax.all_to_all(blocks, axis, split_axis=0, concat_axis=0, tiled=True)


def on_device(table, accum, serve, counts, slot_map, bag_rows, bag_len, labels, w1, b1, w2):
    lists = serve[0, 0]
    limits = counts[0, 0]
    n_peers, slots = lists.shape
    rows, width = table.shape
    half = slots // 2
    readers = lax.axis_size("reader")
    parity = lax.axis_index("reader") % 2
    own_lists = lax.dynamic_slice_in_dim(lists, parity * half, half, 1)
    own_slots = jnp.arange(half, dtype=jnp.int32)[None, :] + parity * half
    own_lists = jnp.where(own_slots < limits[:, None], own_lists, -1)
    slot_rows = own_lists.reshape(-1, LANES)
    picked = fetch(slot_rows.T, table)
    fetched = exchange(picked.reshape(n_peers, half, width), "owner").reshape(-1, width)

    batch, feats, depth = bag_rows.shape
    inside = jnp.arange(depth, dtype=jnp.int32)[None, None, :] < bag_len[:, :, None]
    bags = jnp.where(inside, bag_rows, -1).transpose(1, 0, 2).reshape(-1, depth)
    places = slot_map.reshape(n_peers, 2, half)
    own_places = lax.dynamic_slice_in_dim(places, parity, 1, 1).reshape(-1)
    other_places = lax.dynamic_slice_in_dim(places, 1 - parity, 1, 1).reshape(-1)
    sent = jnp.concatenate([bags.reshape(-1), other_places]).reshape(-1, LANES)
    came = partner(sent).reshape(-1)
    came_bags = came[: bags.size].reshape(bags.shape)
    came_places = came[bags.size :]
    counted = count(
        jnp.concatenate([bags, came_bags], axis=0),
        jnp.stack([own_places, came_places])[:, None, :],
    )

    pooled = jnp.dot(counted, fetched, preferred_element_type=f32)
    own_pooled, other_pooled = pooled[: batch * feats], pooled[batch * feats :]
    logits, part, grad_bags = top(
        own_pooled,
        partner(other_pooled),
        w1,
        b1[None, :],
        w2[None, :],
        labels[:, None],
        readers,
    )
    grad_both = jnp.concatenate([grad_bags, partner(grad_bags)], axis=0)
    slot_grad = lax.dot_general(
        counted, grad_both, (((0,), (0,)), ((), ())), preferred_element_type=f32
    ).astype(bf16)

    part = jnp.sum(exchange(part, "reader").astype(f32), axis=0)
    piece = 8
    chunk = jnp.zeros((n_peers * piece, LANES), f32).at[: part.shape[0]].set(part)
    chunk = jnp.sum(exchange(chunk.reshape(n_peers, piece, LANES), "owner"), axis=0)
    chunk = exchange(jnp.broadcast_to(chunk[None], (n_peers, piece, LANES)), "owner")
    chunk = chunk.reshape(-1, LANES)[: part.shape[0]].astype(bf16)

    returned = exchange(slot_grad.reshape(n_peers, half, width), "owner").reshape(-1, width)
    local_grad = row_sum(slot_rows, returned, rows)
    block = exchange(local_grad.reshape(readers, rows // readers, width), "reader")
    block = jnp.sum(block.astype(f32), axis=0)
    row_grad = lax.all_gather(block, "reader", axis=0, tiled=True)
    new_accum = accum + jnp.mean(row_grad * row_grad, axis=1)
    new_table = table - LEARN_RATE * row_grad / jnp.sqrt(new_accum)[:, None]

    every = exchange(jnp.broadcast_to(chunk[None], (readers,) + chunk.shape), "reader")
    hidden = w1.shape[1]
    blocks = hidden // LANES
    w1_grad = every[:, : -16, :].reshape(readers, blocks, -1, LANES).transpose(0, 2, 1, 3)
    w1_grad = w1_grad.reshape(w1.shape).astype(f32)
    w2_grad = every[0, -16 : blocks - 16, :].reshape(-1).astype(f32)
    return (new_table, new_accum, row_grad, w1_grad, w2_grad, logits.reshape(-1))


def solution(mesh):
    return jax.shard_map(
        on_device,
        mesh=mesh,
        in_specs=(
            P("owner", None),
            P("owner"),
            P("owner", "reader", None, None),
            P("owner", "reader", None),
            P("owner", "reader", None),
            P(("owner", "reader"), None, None),
            P(("owner", "reader"), None),
            P(("owner", "reader")),
            P(),
            P(),
            P(),
        ),
        out_specs=(
            P("owner", None),
            P("owner"),
            P("owner", None),
            P(),
            P(),
            P(("owner", "reader")),
        ),
        check_vma=False,
    )
```

time: 1080 us -> 258 us (0.24)
  waiting for transfers between devices: 548 us -> 93.3 us
  other arithmetic: 216 us -> 5.75 us
  local copies, waits for them, and re-layouts: 142 us -> 10.3 us
  blocking collectives: 109 us -> 38.7 us
  starting transfers between devices: 34.2 us -> 63.9 us
  Pallas kernels: 0 us -> 29.5 us
  between operations: 15.1 us -> 1.04 us
    psum x2 -> x0, waiting for transfers between devices: 489 us -> none  [the longest x1 484 us: on_device(): w1_grad, w2_grad = lax.psum((part_w1, part_w2), ('owner', 'reader'))]
    psum x1 -> x0, blocking collectives: 109 us -> none  [on_device(): w1_grad, w2_grad = lax.psum((part_w1, part_w2), ('owner', 'reader'))]
    slice x1 -> x0, other arithmetic: 100 us -> none  [on_device(): rows_here = flat_rows[entries[:, :, level]]]
    gather x11 -> x0, local copies, waits for them, and re-layouts: 99.6 us -> none  [the longest x2 46.2 us: on_device(): entries = source[bag_rows]]
    scatter-add x9 -> x0, other arithmetic: 94.6 us -> none  [the longest x8 76.6 us: on_device(): slot_grad = slot_grad.at[entries[:, :, level].reshape(-1)].add(level_terms)]
    all_gather x0 -> x1, blocking collectives: none -> 38.7 us  [on_device(): row_grad = lax.all_gather(block, 'reader', axis=0, tiled=True)]
    all_to_all x2 -> x7, waiting for transfers between devices: 55.7 us -> 91.2 us  [exchange(): return lax.all_to_all(blocks, axis, split_axis=0, concat_axis=0, tiled=True)]
    pallas_call x0 -> x4, Pallas kernels: none -> 29.5 us  [the longest x1 21.5 us: count(): pl.pallas_call(count_kernel, grid=(n_bags // block,), out_shape=jax.Shape...]
  transfers between devices with their start and end apart: 5 -> 10, of which waited for: 4 -> 8; matrix products, arithmetic and copies ran while one was open for 18% -> 5% of each run, Pallas kernels for 0% -> 9%
where the time goes in v1:
time: 258 us; the launch traced here: 257 us
  waiting for transfers between devices  93.3 us (36%)
  starting transfers between devices  63.9 us (25%)
  blocking collectives  38.7 us (15%)
  Pallas kernels  29.5 us (11%)
  matrix products  14.7 us (6%)
  local copies, waits for them, and re-layouts  10.3 us (4%)
  other arithmetic  5.75 us (2%)
    all_to_all x7, waiting for transfers between devices, exchange(): return lax.all_to_all(blocks, axis, split_axis=0, concat_axis=0, tiled=True)  91.2 us
    all_to_all x7, starting transfers between devices, exchange(): return lax.all_to_all(blocks, axis, split_axis=0, concat_axis=0, tiled=True)  53.9 us
    all_gather x1, blocking collectives, on_device(): row_grad = lax.all_gather(block, 'reader', axis=0, tiled=True)  38.7 us
    pallas_call x1, Pallas kernels, count(): pl.pallas_call(count_kernel, grid=(n_bags // block,), out_shape=jax.Shape...  21.5 us
    ppermute x3, starting transfers between devices, partner(): lax.ppermute(shard, 'reader', [(i, i ^ 1) for i in range(lax.axis_size('r...  10 us
    dot_general x1, matrix products, on_device(): lax.dot_general(counted, grad_both, (((0,), (0,)), ((), ())), preferred_e...  8.3 us
    dot_general x1, matrix products, on_device(): pooled = jnp.dot(counted, fetched, preferred_element_type=f32)  6.4 us
  transfers between devices with their start and end apart: 10, of which 8 were waited for; matrix products, arithmetic and copies ran while one was open for 5% of the time, Pallas kernels for 9%

profile of v1, /device:TPU:1, one launch (start us, length us, event | category | flops | bytes accessed | tf_op | source)
XLA Modules:
  0.0 257.2 jit_solution(8505625819918709928)
XLA Ops:
  1.3 1.3 reduce.13
  3.2 1.0 copy-done.1
  4.2 2.9 %fetch.1 = bf16[3072,128]{1,0:T(8,128)(2,1)} custom-call(s32[128,24]{1,0:T(8,128)S(1)} %copy.41.slot_ref, f32[1024,128]{1,0:T(8,128)S(1)} %copy-done.1), custom_call_target="tpu_custom_call" | custom-call | tf_op jit(solution)/shard_map/fetch/pallas_call | solution.py:29
  7.1 18.8 %all-to-all-start = ((bf16[48,64,128]{2,1,0:T(8,128)(2,1)}), bf16[48,64,128]{2,1,0:T(8,128)(2,1)S(1)}, u32[]{:S(2)}, u32[]{:S(2)}) async-start(bf16[48,64,128]{2,1,0:T(8,128)(2,1)} %bitcast.5), calls=%async_computation | async-start | bytes 1572864 | tf_op jit(solution)/shard_map/all_to_all | solution.py:168
  27.5 2.9 %collective-permute-start = (s32[88,128]{1,0:T(8,128)S(1)}, s32[88,128]{1,0:T(8,128)S(1)}, u32[]{:S(2)}, u32[]{:S(2)}) collective-permute-start(s32[88,128]{1,0:T(8,128)S(1)} %add_bitcast_fusion), channel_id=1, source_target_pairs={{0,1},{1,0},{2,3},{3,2},{4,5},{5,4},{6,7},{7,6},{8,9},{9,8},{10,11... | collective-permute-start | bytes 135176 | tf_op jit(solution)/shard_map/ppermute | solution.py:164
  30.4 0.8 collective-permute-done
  31.6 21.5 %count.1 = bf16[2048,3072]{1,0:T(8,128)(2,1)} custom-call(s32[2048,8]{1,0:T(8,128)S(1)} %pad_add_fusion.bag_ref, s32[2,1,3072]{2,1,0:T(1,128)S(1)} %broadcast_in_dim.39.place_ref), custom_call_target="tpu_custom_call" | custom-call | flops 100663296 | bytes 12582912 | tf_op jit(solution)/shard_map/count/pallas_call | solution.py:92
  53.2 4.4 %all-to-all-done = bf16[48,64,128]{2,1,0:T(8,128)(2,1)S(1)} async-done(((bf16[48,64,128]{2,1,0:T(8,128)(2,1)}), bf16[48,64,128]{2,1,0:T(8,128)(2,1)S(1)}, u32[]{:S(2)}, u32[]{:S(2)}) %all-to-all-start) | async-done | bytes 786464 | tf_op jit(solution)/shard_map/all_to_all | solution.py:168
  57.6 6.4 %fusion.8 = f32[2048,128]{1,0:T(8,128)S(1)} fusion(bf16[2048,3072]{1,0:T(8,128)(2,1)} %count.1, bf16[3072,128]{1,0:T(8,128)(2,1)S(1)} %bitcast.47), kind=kOutput, calls=%fused_computation.29 | convolution fusion | flops 1610612736 | bytes 14417920 | tf_op jit(solution)/shard_map/dot_general | solution.py:201
  64.1 5.1 %collective-permute-start.1 = (f32[1024,128]{1,0:T(8,128)S(1)}, f32[1024,128]{1,0:T(8,128)S(1)}, u32[]{:S(2)}, u32[]{:S(2)}) collective-permute-start(f32[1024,128]{1,0:T(8,128)S(1)} %get-tuple-element.26), channel_id=1, source_target_pairs={{0,1},{1,0},{2,3},{3,2},{4,5},{5,4},{6,7},{7,6},{8,9},{9,8},{10,11... | collective-permute-start | bytes 1572872 | tf_op jit(solution)/shard_map/ppermute | solution.py:164
  69.5 1.3 collective-permute-done.1.got_ref
  70.8 2.6 top.1
  73.4 7.5 %all-to-all-start.3 = ((bf16[16,272,128]{2,1,0:T(8,128)(2,1)}), bf16[16,272,128]{2,1,0:T(8,128)(2,1)S(1)}, u32[]{:S(2)}, u32[]{:S(2)}) async-start(bf16[16,272,128]{2,1,0:T(8,128)(2,1)} %get-tuple-element.22), calls=%async_computation.3 | async-start | bytes 2228224 | tf_op jit(solution)/shard_map/all_to_all | solution.py:168
  80.8 2.0 collective-permute-start.2
  82.9 27.2 %all-to-all-done.3 = bf16[16,272,128]{2,1,0:T(8,128)(2,1)S(1)} async-done(((bf16[16,272,128]{2,1,0:T(8,128)(2,1)}), bf16[16,272,128]{2,1,0:T(8,128)(2,1)S(1)}, u32[]{:S(2)}, u32[]{:S(2)}) %all-to-all-start.3) | async-done | bytes 1114144 | tf_op jit(solution)/shard_map/all_to_all | solution.py:168
  110.9 5.7 %all-to-all-start.4 = ((f32[48,8,128]{2,1,0:T(8,128)}), f32[48,8,128]{2,1,0:T(8,128)S(1)}, u32[]{:S(2)}, u32[]{:S(2)}) async-start(f32[48,8,128]{2,1,0:T(8,128)} %pad_bitcast_fusion), calls=%async_computation.4 | async-start | bytes 393216 | tf_op jit(solution)/shard_map/all_to_all | solution.py:168
  116.6 8.3 %convolution_convert_fusion = bf16[3072,128]{1,0:T(8,128)(2,1)} fusion(bf16[2048,3072]{1,0:T(8,128)(2,1)} %count.1, bf16[1024,128]{1,0:T(8,128)(2,1)S(1)} %collective-permute-done.2, bf16[1024,128]{1,0:T(8,128)(2,1)S(1)} %get-tuple-element.21), kind=kOutput, calls=%fused_computation | convolution fusion | flops 1612054528 | bytes 13893632 | tf_op jit(solution)/shard_map/dot_general | solution.py:213
  124.9 7.2 %all-to-all-done.4 = f32[48,8,128]{2,1,0:T(8,128)S(1)} async-done(((f32[48,8,128]{2,1,0:T(8,128)}), f32[48,8,128]{2,1,0:T(8,128)S(1)}, u32[]{:S(2)}, u32[]{:S(2)}) %all-to-all-start.4) | async-done | bytes 196640 | tf_op jit(solution)/shard_map/all_to_all | solution.py:168
  132.1 4.8 %all-to-all-start.1 = ((bf16[48,64,128]{2,1,0:T(8,128)(2,1)}), bf16[48,64,128]{2,1,0:T(8,128)(2,1)S(1)}, u32[]{:S(2)}, u32[]{:S(2)}) async-start(bf16[48,64,128]{2,1,0:T(8,128)(2,1)} %bitcast.9), calls=%async_computation.1 | async-start | bytes 1572864 | tf_op jit(solution)/shard_map/all_to_all | solution.py:168
  136.9 31.6 %all-to-all-done.1 = bf16[48,64,128]{2,1,0:T(8,128)(2,1)S(1)} async-done(((bf16[48,64,128]{2,1,0:T(8,128)(2,1)}), bf16[48,64,128]{2,1,0:T(8,128)(2,1)S(1)}, u32[]{:S(2)}, u32[]{:S(2)}) %all-to-all-start.1) | async-done | bytes 786464 | tf_op jit(solution)/shard_map/all_to_all | solution.py:168
  169.2 7.5 %all-to-all-start.5 = ((bf16[48,8,128]{2,1,0:T(8,128)(2,1)}), bf16[48,8,128]{2,1,0:T(8,128)(2,1)S(1)}, u32[]{:S(2)}, u32[]{:S(2)}) async-start(bf16[48,8,128]{2,1,0:T(8,128)(2,1)} %broadcast_in_dim.43), calls=%async_computation.5 | async-start | bytes 196608 | tf_op jit(solution)/shard_map/all_to_all | solution.py:168
  176.7 2.5 row_sum.1
  179.2 8.9 %all-to-all-done.5 = bf16[48,8,128]{2,1,0:T(8,128)(2,1)S(1)} async-done(((bf16[48,8,128]{2,1,0:T(8,128)(2,1)}), bf16[48,8,128]{2,1,0:T(8,128)(2,1)S(1)}, u32[]{:S(2)}, u32[]{:S(2)}) %all-to-all-start.5) | async-done | bytes 98336 | tf_op jit(solution)/shard_map/all_to_all | solution.py:168
  188.1 5.9 %all-to-all-start.2 = ((bf16[16,64,128]{2,1,0:T(8,128)(2,1)}), bf16[16,64,128]{2,1,0:T(8,128)(2,1)S(1)}, u32[]{:S(2)}, u32[]{:S(2)}) async-start(bf16[16,64,128]{2,1,0:T(8,128)(2,1)} %bitcast.11), calls=%async_computation.2 | async-start | bytes 524288 | tf_op jit(solution)/shard_map/all_to_all | solution.py:168
  194.0 11.8 %all-to-all-done.2 = bf16[16,64,128]{2,1,0:T(8,128)(2,1)S(1)} async-done(((bf16[16,64,128]{2,1,0:T(8,128)(2,1)}), bf16[16,64,128]{2,1,0:T(8,128)(2,1)S(1)}, u32[]{:S(2)}, u32[]{:S(2)}) %all-to-all-start.2) | async-done | bytes 262176 | tf_op jit(solution)/shard_map/all_to_all | solution.py:168
  205.9 1.1 broadcast_in_dim.44
  207.0 3.7 %all-to-all-start.6 = ((bf16[16,272,128]{2,1,0:T(8,128)(2,1)}), bf16[16,272,128]{2,1,0:T(8,128)(2,1)S(1)}, u32[]{:S(2)}, u32[]{:S(2)}) async-start(bf16[16,272,128]{2,1,0:T(8,128)(2,1)} %broadcast_in_dim.44), calls=%async_computation.6 | async-start | bytes 2228224 | tf_op jit(solution)/shard_map/all_to_all | solution.py:168
  211.5 38.7 %all_gather.3 = f32[1024,128]{1,0:T(8,128)S(1)} all-gather(f32[64,128]{1,0:T(8,128)S(1)} %convert_reduce_fusion.1), channel_id=1, replica_groups=mesh['owner'=48,'reader'=16] {'reader'}, dimensions={0}, use_global_device_ids=true | all-gather | bytes 557056 | tf_op jit(solution)/shard_map/all_gather | solution.py:228
  251.0 1.0 divide_subtract_fusion
  252.4 1.6 copy.43
  254.0 1.8 copy.47
  256.4 0.8 copy.49
  (64 shorter events, 7.4 us)
Async XLA Ops:
  0.6 2.3 copy-start
  0.6 25.3 %copy-start.6 = (s32[1,1,6144]{2,1,0:T(1,128)S(1)}, s32[1,1,6144]{2,1,0:T(1,128)}, u32[]{:S(2)}) copy-start(s32[1,1,6144]{2,1,0:T(1,128)} %param.17) | copy-start | bytes 73732
  0.7 26.3 %copy-start.7 = (s32[256,4]{0,1:T(4,128)S(1)}, s32[256,4]{0,1:T(4,128)}, u32[]{:S(2)}) copy-start(s32[256,4]{0,1:T(4,128)} %param.19) | copy-start | bytes 12292
  0.7 26.3 %copy-start.5 = (s32[256,4,8]{0,2,1:T(8,128)S(1)}, s32[256,4,8]{0,2,1:T(8,128)}, u32[]{:S(2)}) copy-start(s32[256,4,8]{0,2,1:T(8,128)} %param.18) | copy-start | bytes 98308
  3.2 1.0 copy-start.1
  7.1 50.5 %all-to-all-start = ((bf16[48,64,128]{2,1,0:T(8,128)(2,1)}), bf16[48,64,128]{2,1,0:T(8,128)(2,1)S(1)}, u32[]{:S(2)}, u32[]{:S(2)}) async-start(bf16[48,64,128]{2,1,0:T(8,128)(2,1)} %bitcast.5), calls=%async_computation | async-start | bytes 1572864 | tf_op jit(solution)/shard_map/all_to_all | solution.py:168
  27.5 3.7 %collective-permute-start = (s32[88,128]{1,0:T(8,128)S(1)}, s32[88,128]{1,0:T(8,128)S(1)}, u32[]{:S(2)}, u32[]{:S(2)}) collective-permute-start(s32[88,128]{1,0:T(8,128)S(1)} %add_bitcast_fusion), channel_id=1, source_target_pairs={{0,1},{1,0},{2,3},{3,2},{4,5},{5,4},{6,7},{7,6},{8,9},{9,8},{10,11... | collective-permute-start | bytes 135176 | tf_op jit(solution)/shard_map/ppermute | solution.py:164
  64.0 5.3 %copy-start.9 = (bf16[1024]{0:T(1024)(128)(2,1)S(1)}, bf16[1024]{0:T(1024)(128)(2,1)}, u32[]{:S(2)}) copy-start(bf16[1024]{0:T(1024)(128)(2,1)} %param.23) | copy-start | bytes 6148
  64.0 5.3 %copy-start.10 = (s32[256]{0:T(256)S(1)}, s32[256]{0:T(256)}, u32[]{:S(2)}) copy-start(s32[256]{0:T(256)} %param.20) | copy-start | bytes 3076
  64.0 6.8 %copy-start.3 = (bf16[512,1024]{1,0:T(8,128)(2,1)S(1)}, bf16[512,1024]{1,0:T(8,128)(2,1)}, u32[]{:S(2)}) copy-start(bf16[512,1024]{1,0:T(8,128)(2,1)} %w1_ref.1) | copy-start | bytes 3145732
  64.0 6.8 %copy-start.4 = (f32[1024]{0:T(1024)S(1)}, f32[1024]{0:T(1024)}, u32[]{:S(2)}) copy-start(f32[1024]{0:T(1024)} %param.22) | copy-start | bytes 12292
  64.1 6.7 %collective-permute-start.1 = (f32[1024,128]{1,0:T(8,128)S(1)}, f32[1024,128]{1,0:T(8,128)S(1)}, u32[]{:S(2)}, u32[]{:S(2)}) collective-permute-start(f32[1024,128]{1,0:T(8,128)S(1)} %get-tuple-element.26), channel_id=1, source_target_pairs={{0,1},{1,0},{2,3},{3,2},{4,5},{5,4},{6,7},{7,6},{8,9},{9,8},{10,11... | collective-permute-start | bytes 1572872 | tf_op jit(solution)/shard_map/ppermute | solution.py:164
  73.4 36.7 %all-to-all-start.3 = ((bf16[16,272,128]{2,1,0:T(8,128)(2,1)}), bf16[16,272,128]{2,1,0:T(8,128)(2,1)S(1)}, u32[]{:S(2)}, u32[]{:S(2)}) async-start(bf16[16,272,128]{2,1,0:T(8,128)(2,1)} %get-tuple-element.22), calls=%async_computation.3 | async-start | bytes 2228224 | tf_op jit(solution)/shard_map/all_to_all | solution.py:168
  80.8 35.8 %collective-permute-start.2 = (bf16[1024,128]{1,0:T(8,128)(2,1)S(1)}, bf16[1024,128]{1,0:T(8,128)(2,1)S(1)}, u32[]{:S(2)}, u32[]{:S(2)}) collective-permute-start(bf16[1024,128]{1,0:T(8,128)(2,1)S(1)} %get-tuple-element.21), channel_id=1, source_target_pairs={{0,1},{1,0},{2,3},{3,2},{4,5},{5,4},{6,7},{7,6},{8,9},{9,8},{10,11... | collective-permute-start | bytes 786440 | tf_op jit(solution)/shard_map/ppermute | solution.py:164
  110.9 21.1 %all-to-all-start.4 = ((f32[48,8,128]{2,1,0:T(8,128)}), f32[48,8,128]{2,1,0:T(8,128)S(1)}, u32[]{:S(2)}, u32[]{:S(2)}) async-start(f32[48,8,128]{2,1,0:T(8,128)} %pad_bitcast_fusion), calls=%async_computation.4 | async-start | bytes 393216 | tf_op jit(solution)/shard_map/all_to_all | solution.py:168
  132.1 36.5 %all-to-all-start.1 = ((bf16[48,64,128]{2,1,0:T(8,128)(2,1)}), bf16[48,64,128]{2,1,0:T(8,128)(2,1)S(1)}, u32[]{:S(2)}, u32[]{:S(2)}) async-start(bf16[48,64,128]{2,1,0:T(8,128)(2,1)} %bitcast.9), calls=%async_computation.1 | async-start | bytes 1572864 | tf_op jit(solution)/shard_map/all_to_all | solution.py:168
  169.2 18.9 %all-to-all-start.5 = ((bf16[48,8,128]{2,1,0:T(8,128)(2,1)}), bf16[48,8,128]{2,1,0:T(8,128)(2,1)S(1)}, u32[]{:S(2)}, u32[]{:S(2)}) async-start(bf16[48,8,128]{2,1,0:T(8,128)(2,1)} %broadcast_in_dim.43), calls=%async_computation.5 | async-start | bytes 196608 | tf_op jit(solution)/shard_map/all_to_all | solution.py:168
  188.1 17.8 %all-to-all-start.2 = ((bf16[16,64,128]{2,1,0:T(8,128)(2,1)}), bf16[16,64,128]{2,1,0:T(8,128)(2,1)S(1)}, u32[]{:S(2)}, u32[]{:S(2)}) async-start(bf16[16,64,128]{2,1,0:T(8,128)(2,1)} %bitcast.11), calls=%async_computation.2 | async-start | bytes 524288 | tf_op jit(solution)/shard_map/all_to_all | solution.py:168
  207.0 43.4 %copy-start.8 = (f32[1024]{0:T(1024)S(1)}, f32[1024]{0:T(1024)}, u32[]{:S(2)}) copy-start(f32[1024]{0:T(1024)} %param.14) | copy-start | bytes 12292
  207.0 44.0 %copy-start.2 = (f32[1024,128]{1,0:T(8,128)S(1)}, f32[1024,128]{1,0:T(8,128)}, u32[]{:S(2)}) copy-start(f32[1024,128]{1,0:T(8,128)} %table_ref.1) | copy-start | bytes 1572868
  207.0 45.0 %all-to-all-start.6 = ((bf16[16,272,128]{2,1,0:T(8,128)(2,1)}), bf16[16,272,128]{2,1,0:T(8,128)(2,1)S(1)}, u32[]{:S(2)}, u32[]{:S(2)}) async-start(bf16[16,272,128]{2,1,0:T(8,128)(2,1)} %broadcast_in_dim.44), calls=%async_computation.6 | async-start | bytes 2228224 | tf_op jit(solution)/shard_map/all_to_all | solution.py:168

commit v2 on v1

--- a/solution.py
+++ b/solution.py
@@ -36,7 +36,7 @@
     )(slot_cols, table)
 
 
-def row_sum_kernel(slot_ref, value_ref, out_ref):
+def row_sum_kernel(order, slot_ref, value_ref, out_ref):
     n = out_ref.shape[0]
     iota = lax.broadcasted_iota(jnp.int32, (n, LANES), 0)
     total = jnp.zeros(out_ref.shape, f32)
@@ -47,13 +47,16 @@
         )
         values = value_ref[k * LANES : (k + 2) * LANES, :]
         total = total + jnp.dot(hot, values, preferred_element_type=f32)
-    out_ref[...] = total.astype(out_ref.dtype)
-
-
-def row_sum(slot_rows, values, n):
+    blocks = len(order)
+    size = n // blocks
+    for b, place in enumerate(order):
+        out_ref[place * size : (place + 1) * size, :] = total[b * size : (b + 1) * size, :]
+
+
+def row_sum(slot_rows, values, n, order):
     return pl.pallas_call(
-        row_sum_kernel,
-        out_shape=jax.ShapeDtypeStruct((n, values.shape[1]), bf16),
+        functools.partial(row_sum_kernel, order),
+        out_shape=jax.ShapeDtypeStruct((n, values.shape[1]), f32),
         in_specs=[VMEM] * 2,
         out_specs=VMEM,
         compiler_params=PARAMS,
@@ -62,23 +65,29 @@
 
 
 def count_kernel(bag_ref, place_ref, out_ref):
-    group = 16
+    group, part = 32, 16
     one, zero = jnp.ones((), bf16), jnp.zeros((), bf16)
 
     def step(g, carry):
         rows = pl.ds(pl.multiple_of(g * group, group), group)
         bags = bag_ref[rows, :]
         names = [
-            jnp.broadcast_to(bags[:, l : l + 1], (group, LANES)).astype(jnp.int16)
-            for l in range(bags.shape[1])
+            [
+                jnp.broadcast_to(bags[p : p + part, l : l + 1], (part, LANES)).astype(jnp.int16)
+                for l in range(bags.shape[1])
+            ]
+            for p in range(0, group, part)
         ]
         for t in range(out_ref.shape[1] // LANES):
             cols = slice(t * LANES, (t + 1) * LANES)
-            place = jnp.broadcast_to(place_ref[0, :, cols], (group, LANES)).astype(jnp.int16)
-            total = jnp.zeros((group, LANES), bf16)
-            for name in names:
-                total = total + jnp.where(name == place, one, zero)
-            out_ref[rows, cols] = total
+            place = jnp.broadcast_to(place_ref[0, :, cols], (part, LANES)).astype(jnp.int16)
+            totals = []
+            for part_names in names:
+                total = jnp.zeros((part, LANES), bf16)
+                for name in part_names:
+                    total = total + jnp.where(name == place, one, zero)
+                totals.append(total)
+            out_ref[rows, cols] = jnp.concatenate(totals, axis=0).astype(out_ref.dtype)
         return carry
 
     lax.fori_loop(0, out_ref.shape[0] // group, step, 0)
@@ -92,7 +101,7 @@
     return pl.pallas_call(
         count_kernel,
         grid=(n_bags // block,),
-        out_shape=jax.ShapeDtypeStruct((n_bags, slots), bf16),
+        out_shape=jax.ShapeDtypeStruct((n_bags, slots), jnp.float8_e4m3fn),
         in_specs=[
             pl.BlockSpec((block, depth), lambda i: (i, 0)),
             pl.BlockSpec((1, 1, slots), lambda i: (i // per, 0, 0)),
@@ -101,14 +110,14 @@
         compiler_params=PARAMS,
         cost_estimate=pl.CostEstimate(
             flops=n_bags * slots * depth * 2,
-            bytes_accessed=n_bags * slots * 2,
+            bytes_accessed=n_bags * slots,
             transcendentals=0,
         ),
         name="count",
     )(bags, places)
 
 
-def top_kernel(own_ref, got_ref, w1_ref, b1_ref, w2_ref, label_ref, logit_ref, part_ref, g_ref):
+def top_kernel(order, own_ref, got_ref, w1_ref, b1_ref, w2_ref, label_ref, logit_ref, part_ref, g_ref):
     batch = label_ref.shape[0]
     feats = own_ref.shape[0] // batch
     spans = [slice(f * batch, (f + 1) * batch) for f in range(feats)]
@@ -132,25 +141,25 @@
     part_w1 = lax.dot_general(
         pooled, grad_pre, (((0,), (0,)), ((), ())), preferred_element_type=f32
     )
-    chunks = part_ref.shape[0]
-    depth, blocks = part_w1.shape[0] // chunks, part_w1.shape[1] // LANES
-    for j in range(blocks):
-        block = part_w1[:, j * LANES : (j + 1) * LANES].astype(bf16)
-        part_ref[:, j * depth : (j + 1) * depth, :] = block.reshape(chunks, depth, LANES)
-    part_ref[:, blocks * depth :, :] = jnp.zeros((chunks, 16, LANES), bf16)
+    depth, blocks = part_w1.shape[0] // len(order), part_w1.shape[1] // LANES
     tail = [part_w2[:, j * LANES : (j + 1) * LANES] for j in range(blocks)]
     tail = jnp.concatenate(tail + [jnp.zeros((16 - blocks, LANES), f32)], axis=0)
-    part_ref[0, blocks * depth :, :] = tail.astype(bf16)
-
-
-def top(own, got, w1, b1, w2, labels, chunks):
+    for c, place in enumerate(order):
+        rows = part_w1[c * depth : (c + 1) * depth, :]
+        for j in range(blocks):
+            part_ref[place, j * depth : (j + 1) * depth, :] = rows[:, j * LANES : (j + 1) * LANES]
+        part_ref[place, blocks * depth :, :] = tail if c == 0 else jnp.zeros_like(tail)
+
+
+def top(own, got, w1, b1, w2, labels, order):
     batch = labels.shape[0]
+    chunks = len(order)
     depth = w1.size // chunks // LANES + 16
     return pl.pallas_call(
-        top_kernel,
+        functools.partial(top_kernel, order),
         out_shape=(
             jax.ShapeDtypeStruct((batch, 1), f32),
-            jax.ShapeDtypeStruct((chunks, depth, LANES), bf16),
+            jax.ShapeDtypeStruct((chunks, depth, LANES), f32),
             jax.ShapeDtypeStruct(own.shape, bf16),
         ),
         in_specs=[VMEM] * 6,
@@ -160,12 +169,103 @@
     )(own, got, w1, b1, w2, labels)
 
 
+def update_kernel(
+    parity_ref,
+    mine_ref,
+    other_ref,
+    table_ref,
+    accum_ref,
+    accum_col_ref,
+    new_table_ref,
+    new_accum_ref,
+    row_grad_ref,
+    w1_grad_ref,
+    w2_grad_ref,
+):
+    chips, depth, _ = mine_ref.shape
+    rows, hidden = table_ref.shape[0], w1_grad_ref.shape[1]
+    size, blocks = rows // (2 * chips), hidden // LANES
+    chunk = w1_grad_ref.shape[0] // (2 * chips)
+    first = parity_ref[0] == 0
+    for y in range(chips):
+        mine, other = mine_ref[y].astype(f32), other_ref[y].astype(f32)
+        for c in range(2):
+            got = jnp.where(first, mine, other) if c == 0 else jnp.where(first, other, mine)
+            base = (chips * c + y) * chunk
+            for j in range(blocks):
+                w1_grad_ref[base : base + chunk, j * LANES : (j + 1) * LANES] = got[
+                    j * chunk : (j + 1) * chunk, :
+                ]
+            if y == 0 and c == 0:
+                w2_grad_ref[...] = got[blocks * chunk : blocks * chunk + blocks, :]
+            base = (2 * y + c) * size
+            row_grad_ref[base : base + size, :] = got[depth - size :, :]
+    grad = row_grad_ref[...]
+    square = grad * grad
+    means = []
+    for i in range(rows // LANES):
+        spread = lax.dot_general(
+            jnp.full((8, LANES), 1.0 / LANES, f32),
+            square[i * LANES : (i + 1) * LANES, :],
+            (((1,), (1,)), ((), ())),
+            precision=lax.Precision.HIGHEST,
+            preferred_element_type=f32,
+        )
+        means.append(spread[:1, :])
+    new_accum_ref[...] = accum_ref[...] + jnp.concatenate(means, axis=0)
+    scale = accum_col_ref[...] + jnp.mean(square, axis=1, keepdims=True)
+    new_table_ref[...] = table_ref[...] - LEARN_RATE * grad / jnp.sqrt(scale)
+
+
+def update(mine, other, parity, table, accum, w1_shape):
+    rows, width = table.shape
+    blocks = w1_shape[1] // LANES
+    smem = pl.BlockSpec(memory_space=pltpu.SMEM)
+    new_table, new_accum, row_grad, w1_grad, w2_grad = pl.pallas_call(
+        update_kernel,
+        out_shape=(
+            jax.ShapeDtypeStruct(table.shape, f32),
+            jax.ShapeDtypeStruct((rows // LANES, LANES), f32),
+            jax.ShapeDtypeStruct(table.shape, f32),
+            jax.ShapeDtypeStruct(w1_shape, f32),
+            jax.ShapeDtypeStruct((blocks, LANES), f32),
+        ),
+        in_specs=[smem] + [VMEM] * 5,
+        out_specs=(VMEM,) * 5,
+        compiler_params=PARAMS,
+        name="update",
+    )(parity.reshape(1), mine, other, table, accum.reshape(-1, LANES), accum[:, None])
+    return new_table, new_accum.reshape(-1), row_grad, w1_grad, w2_grad.reshape(-1)
+
+
+def bit_reversed(i, bits):
+    return sum((i >> b & 1) << (bits - 1 - b) for b in range(bits))
+
+
+def swap(shard, stride):
+    pairs = [(i, i ^ stride) for i in range(lax.axis_size("reader"))]
+    return lax.ppermute(shard, "reader", pairs)
+
+
+def halve(blocks, sent_type, strides):
+    me = lax.axis_index("reader")
+    for stride in strides:
+        half = blocks.shape[0] // 2
+        side = me // stride % 2
+        kept = lax.dynamic_slice_in_dim(blocks, side * half, half, 0)
+        sent = lax.dynamic_slice_in_dim(blocks, (1 - side) * half, half, 0)
+        blocks = kept + swap(sent.astype(sent_type), stride).astype(f32)
+    return blocks
+
+
 def partner(shard):
-    return lax.ppermute(shard, "reader", [(i, i ^ 1) for i in range(lax.axis_size("reader"))])
-
-
-def exchange(blocks, axis):
-    return lax.all_to_all(blocks, axis, split_axis=0, concat_axis=0, tiled=True)
+    return swap(shard, 1)
+
+
+def exchange(blocks, axis, groups=None):
+    return lax.all_to_all(
+        blocks, axis, split_axis=0, concat_axis=0, tiled=True, axis_index_groups=groups
+    )
 
 
 def on_device(table, accum, serve, counts, slot_map, bag_rows, bag_len, labels, w1, b1, w2):
@@ -175,6 +275,8 @@
     rows, width = table.shape
     half = slots // 2
     readers = lax.axis_size("reader")
+    chips, bits = readers // 2, readers.bit_length() - 1
+    strides = [1 << b for b in range(bits)]
     parity = lax.axis_index("reader") % 2
     own_lists = lax.dynamic_slice_in_dim(lists, parity * half, half, 1)
     own_slots = jnp.arange(half, dtype=jnp.int32)[None, :] + parity * half
@@ -198,7 +300,7 @@
         jnp.stack([own_places, came_places])[:, None, :],
     )
 
-    pooled = jnp.dot(counted, fetched, preferred_element_type=f32)
+    pooled = jnp.dot(counted.astype(bf16), fetched, preferred_element_type=f32)
     own_pooled, other_pooled = pooled[: batch * feats], pooled[batch * feats :]
     logits, part, grad_bags = top(
         own_pooled,
@@ -207,34 +309,39 @@
         b1[None, :],
         w2[None, :],
         labels[:, None],
-        readers,
+        [c // chips * chips + bit_reversed(c % chips, bits - 1) for c in range(readers)],
     )
     grad_both = jnp.concatenate([grad_bags, partner(grad_bags)], axis=0)
     slot_grad = lax.dot_general(
-        counted, grad_both, (((0,), (0,)), ((), ())), preferred_element_type=f32
+        counted.astype(bf16), grad_both, (((0,), (0,)), ((), ())), preferred_element_type=f32
     ).astype(bf16)
 
-    part = jnp.sum(exchange(part, "reader").astype(f32), axis=0)
+    part = halve(part, bf16, strides[:1])
+    part, slot_grad = lax.optimization_barrier((part, slot_grad))
+    returned = exchange(slot_grad.reshape(n_peers, half, width), "owner").reshape(-1, width)
+    part = halve(part, bf16, strides[1:])[0]
+    part, returned = lax.optimization_barrier((part, returned))
+    order = [bit_reversed(b, bits) for b in range(readers)]
+    local_grad = row_sum(slot_rows, returned, rows, order)
+    block = local_grad.reshape(readers, rows // readers, width)
+
     piece = 8
-    chunk = jnp.zeros((n_peers * piece, LANES), f32).at[: part.shape[0]].set(part)
-    chunk = jnp.sum(exchange(chunk.reshape(n_peers, piece, LANES), "owner"), axis=0)
+    depth_w = part.shape[0]
+    chunk = jnp.zeros((n_peers * piece, LANES), bf16).at[:depth_w].set(part.astype(bf16))
+    chunk = exchange(chunk.reshape(n_peers, piece, LANES), "owner")
+    chunk = jnp.sum(chunk.astype(f32), axis=0).astype(bf16)
+    block = halve(block, f32, strides[:2])
+    chunk, block = lax.optimization_barrier((chunk, block))
     chunk = exchange(jnp.broadcast_to(chunk[None], (n_peers, piece, LANES)), "owner")
-    chunk = chunk.reshape(-1, LANES)[: part.shape[0]].astype(bf16)
-
-    returned = exchange(slot_grad.reshape(n_peers, half, width), "owner").reshape(-1, width)
-    local_grad = row_sum(slot_rows, returned, rows)
-    block = exchange(local_grad.reshape(readers, rows // readers, width), "reader")
-    block = jnp.sum(block.astype(f32), axis=0)
-    row_grad = lax.all_gather(block, "reader", axis=0, tiled=True)
-    new_accum = accum + jnp.mean(row_grad * row_grad, axis=1)
-    new_table = table - LEARN_RATE * row_grad / jnp.sqrt(new_accum)[:, None]
-
-    every = exchange(jnp.broadcast_to(chunk[None], (readers,) + chunk.shape), "reader")
-    hidden = w1.shape[1]
-    blocks = hidden // LANES
-    w1_grad = every[:, : -16, :].reshape(readers, blocks, -1, LANES).transpose(0, 2, 1, 3)
-    w1_grad = w1_grad.reshape(w1.shape).astype(f32)
-    w2_grad = every[0, -16 : blocks - 16, :].reshape(-1).astype(f32)
+    chunk = chunk.reshape(-1, LANES)[:depth_w]
+    block = halve(block, f32, strides[2:])
+    same_core = [list(range(c, readers, 2)) for c in range(2)]
+    mine = jnp.concatenate([chunk, block[0].astype(bf16)], axis=0)
+    mine = jnp.broadcast_to(mine[None], (chips,) + mine.shape)
+    mine = exchange(mine, "reader", same_core)
+    new_table, new_accum, row_grad, w1_grad, w2_grad = update(
+        mine, partner(mine), parity, table, accum, w1.shape
+    )
     return (new_table, new_accum, row_grad, w1_grad, w2_grad, logits.reshape(-1))
 
 

time: 258 us -> 208 us (0.81)
  waiting for transfers between devices: 93.3 us -> 44.9 us
  starting transfers between devices: 63.9 us -> 90.6 us
  blocking collectives: 38.7 us -> 21 us
  Pallas kernels: 29.5 us -> 25.5 us
  other arithmetic: 5.75 us -> 3.17 us
    all_to_all x7 -> x4, waiting for transfers between devices: 91.2 us -> 23.3 us  [exchange(): lax.all_to_all(blocks, axis, split_axis=0, concat_axis=0, tiled=True, axi...]
    ppermute x3 -> x12, starting transfers between devices: 10 us -> 48.9 us  [swap(): return lax.ppermute(shard, 'reader', pairs)]
    all_gather x1 -> x0, blocking collectives: 38.7 us -> none  [on_device(): row_grad = lax.all_gather(block, 'reader', axis=0, tiled=True)]
    all_to_all x0 -> x1, blocking collectives: none -> 21 us  [exchange(): lax.all_to_all(blocks, axis, split_axis=0, concat_axis=0, tiled=True, axi...]
    ppermute x3 -> x12, waiting for transfers between devices: 2.11 us -> 21.6 us  [swap(): return lax.ppermute(shard, 'reader', pairs)]
    all_to_all x7 -> x4, starting transfers between devices: 53.9 us -> 41.7 us  [exchange(): lax.all_to_all(blocks, axis, split_axis=0, concat_axis=0, tiled=True, axi...]
    pallas_call x1, Pallas kernels: 21.5 us -> 16.3 us  [count(): pl.pallas_call(count_kernel, grid=(n_bags // block,), out_shape=jax.Shape...]
    pallas_call x2 -> x3, Pallas kernels: 5.04 us -> 6.31 us  [the longest x1 2.52 us: update(): pl.pallas_call(update_kernel, out_shape=(jax.ShapeDtypeStruct(table.shape...]
  transfers between devices with their start and end apart: 10 -> 16, of which waited for: 8 -> 11; matrix products, arithmetic and copies ran while one was open for 5% -> 6% of each run, Pallas kernels for 9% -> 8%
where the time goes in v2:
time: 208 us; the launch traced here: 207 us
  starting transfers between devices  90.6 us (44%)
  waiting for transfers between devices  44.9 us (22%)
  Pallas kernels  25.5 us (12%)
  blocking collectives  21 us (10%)
  matrix products  12.7 us (6%)
  local copies, waits for them, and re-layouts  7.92 us (4%)
  other arithmetic  3.17 us (2%)
    ppermute x12, starting transfers between devices, swap(): return lax.ppermute(shard, 'reader', pairs)  48.9 us
    all_to_all x4, starting transfers between devices, exchange(): lax.all_to_all(blocks, axis, split_axis=0, concat_axis=0, tiled=True, axi...  41.7 us
    all_to_all x4, waiting for transfers between devices, exchange(): lax.all_to_all(blocks, axis, split_axis=0, concat_axis=0, tiled=True, axi...  23.3 us
    ppermute x12, waiting for transfers between devices, swap(): return lax.ppermute(shard, 'reader', pairs)  21.6 us
    all_to_all x1, blocking collectives, exchange(): lax.all_to_all(blocks, axis, split_axis=0, concat_axis=0, tiled=True, axi...  21 us
    pallas_call x1, Pallas kernels, count(): pl.pallas_call(count_kernel, grid=(n_bags // block,), out_shape=jax.Shape...  16.3 us
    dot_general x1, matrix products, on_device(): lax.dot_general(counted.astype(bf16), grad_both, (((0,), (0,)), ((), ()))...  7.21 us
    dot_general x1, matrix products, on_device(): pooled = jnp.dot(counted.astype(bf16), fetched, preferred_element_type=f32)  5.48 us
  transfers between devices with their start and end apart: 16, of which 11 were waited for; matrix products, arithmetic and copies ran while one was open for 6% of the time, Pallas kernels for 8%

profile of v2, /device:TPU:1, one launch (start us, length us, event | category | flops | bytes accessed | tf_op | source)
XLA Modules:
  0.0 207.1 jit_solution(387045868097779155)
XLA Ops:
  4.9 2.9 %fetch.1 = bf16[3072,128]{1,0:T(8,128)(2,1)} custom-call(s32[128,24]{1,0:T(8,128)S(1)} %copy.36.slot_ref, f32[1024,128]{1,0:T(8,128)S(1)} %copy-done.1), custom_call_target="tpu_custom_call" | custom-call | tf_op jit(solution)/shard_map/fetch/pallas_call | solution.py:29
  7.8 18.8 %all-to-all-start = ((bf16[48,64,128]{2,1,0:T(8,128)(2,1)}), bf16[48,64,128]{2,1,0:T(8,128)(2,1)S(1)}, u32[]{:S(2)}, u32[]{:S(2)}) async-start(bf16[48,64,128]{2,1,0:T(8,128)(2,1)} %bitcast.6), calls=%async_computation | async-start | bytes 1572864 | tf_op jit(solution)/shard_map/all_to_all | solution.py:266
  28.1 2.9 %collective-permute-start = (s32[88,128]{1,0:T(8,128)S(1)}, s32[88,128]{1,0:T(8,128)S(1)}, u32[]{:S(2)}, u32[]{:S(2)}) collective-permute-start(s32[88,128]{1,0:T(8,128)S(1)} %add_bitcast_fusion.1), channel_id=1, source_target_pairs={{0,1},{1,0},{2,3},{3,2},{4,5},{5,4},{6,7},{7,6},{8,9},{9,8},{10,11... | collective-permute-start | bytes 135176 | tf_op jit(solution)/shard_map/ppermute | solution.py:247
  32.3 16.3 %count.1 = f8e4m3fn[2048,3072]{1,0:T(32,128)(4,1)} custom-call(s32[2048,8]{1,0:T(8,128)S(1)} %pad_add_fusion.bag_ref, s32[2,1,3072]{2,1,0:T(1,128)S(1)} %broadcast_in_dim.40.place_ref), custom_call_target="tpu_custom_call" | custom-call | flops 100663296 | bytes 6291456 | tf_op jit(solution)/shard_map/count/pallas_call | solution.py:101
  48.6 9.7 %all-to-all-done = bf16[48,64,128]{2,1,0:T(8,128)(2,1)S(1)} async-done(((bf16[48,64,128]{2,1,0:T(8,128)(2,1)}), bf16[48,64,128]{2,1,0:T(8,128)(2,1)S(1)}, u32[]{:S(2)}, u32[]{:S(2)}) %all-to-all-start) | async-done | bytes 786464 | tf_op jit(solution)/shard_map/all_to_all | solution.py:266
  58.3 5.5 %fusion.2 = f32[2048,128]{1,0:T(8,128)S(1)} fusion(bf16[3072,128]{1,0:T(8,128)(2,1)S(1)} %bitcast.42, f8e4m3fn[2048,3072]{1,0:T(32,128)(4,1)} %count.1), kind=kOutput, calls=%fused_computation.2 | convolution fusion | flops 1616904192 | bytes 8126464 | tf_op jit(solution)/shard_map/dot_general | solution.py:303
  63.9 5.0 %collective-permute-start.1 = (f32[1024,128]{1,0:T(8,128)S(1)}, f32[1024,128]{1,0:T(8,128)S(1)}, u32[]{:S(2)}, u32[]{:S(2)}) collective-permute-start(f32[1024,128]{1,0:T(8,128)S(1)} %get-tuple-element.46), channel_id=1, source_target_pairs={{0,1},{1,0},{2,3},{3,2},{4,5},{5,4},{6,7},{7,6},{8,9},{9,8},{10,11... | collective-permute-start | bytes 1572872 | tf_op jit(solution)/shard_map/ppermute | solution.py:247
  71.6 2.0 top.1
  74.3 2.3 %collective-permute-start.3 = (bf16[1024,128]{1,0:T(8,128)(2,1)}, bf16[1024,128]{1,0:T(8,128)(2,1)S(1)}, u32[]{:S(2)}, u32[]{:S(2)}) collective-permute-start(bf16[1024,128]{1,0:T(8,128)(2,1)} %get-tuple-element.33), channel_id=1, source_target_pairs={{0,1},{1,0},{2,3},{3,2},{4,5},{5,4},{6,7},{7,6},{8,9},{9,8},{10,11... | collective-permute-start | bytes 786440 | tf_op jit(solution)/shard_map/ppermute | solution.py:247
  76.6 2.1 collective-permute-start.2
  78.7 7.2 %fusion.4 = bf16[3072,128]{1,0:T(8,128)(2,1)} fusion(f8e4m3fn[2048,3072]{1,0:T(32,128)(4,1)} %count.1, bf16[1024,128]{1,0:T(8,128)(2,1)S(1)} %collective-permute-done.3, bf16[1024,128]{1,0:T(8,128)(2,1)} %get-tuple-element.33), kind=kOutput, calls=%fused_computation.4 | convolution fusion | flops 1618345984 | bytes 7602176 | tf_op jit(solution)/shard_map/dot_general | solution.py:315
  86.0 5.7 %all-to-all-start.1 = ((bf16[48,64,128]{2,1,0:T(8,128)(2,1)}), bf16[48,64,128]{2,1,0:T(8,128)(2,1)S(1)}, u32[]{:S(2)}, u32[]{:S(2)}) async-start(bf16[48,64,128]{2,1,0:T(8,128)(2,1)} %bitcast.41), calls=%async_computation.1 | async-start | bytes 1572864 | tf_op jit(solution)/shard_map/all_to_all | solution.py:266
  91.8 3.2 %collective-permute-start.4 = (bf16[4,272,128]{2,1,0:T(8,128)(2,1)S(1)}, bf16[4,272,128]{2,1,0:T(8,128)(2,1)S(1)}, u32[]{:S(2)}, u32[]{:S(2)}) collective-permute-start(bf16[4,272,128]{2,1,0:T(8,128)(2,1)S(1)} %dynamic-slice_convert_fusion.1), channel_id=1, source_target_pairs={{0,2},{1,3},{2,0},{3,1},{4,6},{5,7},{6,4},{7,5},{8,10},{9,11},{10,... | collective-permute-start | bytes 835592 | tf_op jit(solution)/shard_map/ppermute | solution.py:247
  95.1 6.2 %collective-permute-done.4 = bf16[4,272,128]{2,1,0:T(8,128)(2,1)S(1)} collective-permute-done((bf16[4,272,128]{2,1,0:T(8,128)(2,1)S(1)}, bf16[4,272,128]{2,1,0:T(8,128)(2,1)S(1)}, u32[]{:S(2)}, u32[]{:S(2)}) %collective-permute-start.4) | collective-permute-done | bytes 278560 | tf_op jit(solution)/shard_map/ppermute | solution.py:247
  101.4 4.2 %collective-permute-start.5 = (bf16[2,272,128]{2,1,0:T(8,128)(2,1)S(1)}, bf16[2,272,128]{2,1,0:T(8,128)(2,1)S(1)}, u32[]{:S(2)}, u32[]{:S(2)}) collective-permute-start(bf16[2,272,128]{2,1,0:T(8,128)(2,1)S(1)} %dynamic-slice_convert_fusion.2), channel_id=1, source_target_pairs={{0,4},{1,5},{2,6},{3,7},{4,0},{5,1},{6,2},{7,3},{8,12},{9,13},{10,... | collective-permute-start | bytes 417800 | tf_op jit(solution)/shard_map/ppermute | solution.py:247
  105.6 6.0 %collective-permute-done.5 = bf16[2,272,128]{2,1,0:T(8,128)(2,1)S(1)} collective-permute-done((bf16[2,272,128]{2,1,0:T(8,128)(2,1)S(1)}, bf16[2,272,128]{2,1,0:T(8,128)(2,1)S(1)}, u32[]{:S(2)}, u32[]{:S(2)}) %collective-permute-start.5) | collective-permute-done | bytes 139296 | tf_op jit(solution)/shard_map/ppermute | solution.py:247
  111.7 8.1 %collective-permute-start.6 = (bf16[1,272,128]{2,1,0:T(8,128)(2,1)S(1)}, bf16[1,272,128]{2,1,0:T(8,128)(2,1)S(1)}, u32[]{:S(2)}, u32[]{:S(2)}) collective-permute-start(bf16[1,272,128]{2,1,0:T(8,128)(2,1)S(1)} %dynamic-slice_convert_fusion.3), channel_id=1, source_target_pairs={{0,8},{1,9},{2,10},{3,11},{4,12},{5,13},{6,14},{7,15},{8,0},{9,1},... | collective-permute-start | bytes 208904 | tf_op jit(solution)/shard_map/ppermute | solution.py:247
  119.8 2.0 collective-permute-done.6
  121.8 1.6 all-to-all-done.1
  123.4 1.8 row_sum.1
  125.3 4.6 %collective-permute-start.7 = (f32[8,64,128]{2,1,0:T(8,128)S(1)}, f32[8,64,128]{2,1,0:T(8,128)S(1)}, u32[]{:S(2)}, u32[]{:S(2)}) collective-permute-start(f32[8,64,128]{2,1,0:T(8,128)S(1)} %constant_dynamic-slice_fusion.3), channel_id=1, source_target_pairs={{0,1},{1,0},{2,3},{3,2},{4,5},{5,4},{6,7},{7,6},{8,9},{9,8},{10,11... | collective-permute-start | bytes 786440 | tf_op jit(solution)/shard_map/ppermute | solution.py:247
  130.5 8.9 %all-to-all-start.2 = ((bf16[48,8,128]{2,1,0:T(8,128)(2,1)}), bf16[48,8,128]{2,1,0:T(8,128)(2,1)S(1)}, u32[]{:S(2)}, u32[]{:S(2)}) async-start(bf16[48,8,128]{2,1,0:T(8,128)(2,1)} %pad_bitcast_fusion), calls=%async_computation.2 | async-start | bytes 196608 | tf_op jit(solution)/shard_map/all_to_all | solution.py:266
  139.5 2.4 %collective-permute-start.8 = (f32[4,64,128]{2,1,0:T(8,128)S(1)}, f32[4,64,128]{2,1,0:T(8,128)S(1)}, u32[]{:S(2)}, u32[]{:S(2)}) collective-permute-start(f32[4,64,128]{2,1,0:T(8,128)S(1)} %constant_dynamic-slice_fusion.2), channel_id=1, source_target_pairs={{0,2},{1,3},{2,0},{3,1},{4,6},{5,7},{6,4},{7,5},{8,10},{9,11},{10,... | collective-permute-start | bytes 393224 | tf_op jit(solution)/shard_map/ppermute | solution.py:247
  141.9 9.5 %all-to-all-done.2 = bf16[48,8,128]{2,1,0:T(8,128)(2,1)S(1)} async-done(((bf16[48,8,128]{2,1,0:T(8,128)(2,1)}), bf16[48,8,128]{2,1,0:T(8,128)(2,1)S(1)}, u32[]{:S(2)}, u32[]{:S(2)}) %all-to-all-start.2) | async-done | bytes 98336 | tf_op jit(solution)/shard_map/all_to_all | solution.py:266
  151.6 3.0 %collective-permute-start.9 = (f32[2,64,128]{2,1,0:T(8,128)S(1)}, f32[2,64,128]{2,1,0:T(8,128)S(1)}, u32[]{:S(2)}, u32[]{:S(2)}) collective-permute-start(f32[2,64,128]{2,1,0:T(8,128)S(1)} %constant_dynamic-slice_fusion.1), channel_id=1, source_target_pairs={{0,4},{1,5},{2,6},{3,7},{4,0},{5,1},{6,2},{7,3},{8,12},{9,13},{10,... | collective-permute-start | bytes 196616 | tf_op jit(solution)/shard_map/ppermute | solution.py:247
  155.2 8.3 %all-to-all-start.3 = ((bf16[48,8,128]{2,1,0:T(8,128)(2,1)}), bf16[48,8,128]{2,1,0:T(8,128)(2,1)S(1)}, u32[]{:S(2)}, u32[]{:S(2)}) async-start(bf16[48,8,128]{2,1,0:T(8,128)(2,1)} %broadcast_in_dim.45), calls=%async_computation.3 | async-start | bytes 196608 | tf_op jit(solution)/shard_map/all_to_all | solution.py:266
  163.6 4.4 %collective-permute-start.10 = (f32[1,64,128]{2,1,0:T(8,128)S(1)}, f32[1,64,128]{2,1,0:T(8,128)S(1)}, u32[]{:S(2)}, u32[]{:S(2)}) collective-permute-start(f32[1,64,128]{2,1,0:T(8,128)S(1)} %constant_dynamic-slice_fusion), channel_id=1, source_target_pairs={{0,8},{1,9},{2,10},{3,11},{4,12},{5,13},{6,14},{7,15},{8,0},{9,1},... | collective-permute-start | bytes 98312 | tf_op jit(solution)/shard_map/ppermute | solution.py:247
  168.0 4.4 %collective-permute-done.10 = f32[1,64,128]{2,1,0:T(8,128)S(1)} collective-permute-done((f32[1,64,128]{2,1,0:T(8,128)S(1)}, f32[1,64,128]{2,1,0:T(8,128)S(1)}, u32[]{:S(2)}, u32[]{:S(2)}) %collective-permute-start.10) | collective-permute-done | bytes 32800 | tf_op jit(solution)/shard_map/ppermute | solution.py:247
  172.5 2.5 %all-to-all-done.3 = bf16[48,8,128]{2,1,0:T(8,128)(2,1)S(1)} async-done(((bf16[48,8,128]{2,1,0:T(8,128)(2,1)}), bf16[48,8,128]{2,1,0:T(8,128)(2,1)S(1)}, u32[]{:S(2)}, u32[]{:S(2)}) %all-to-all-start.3) | async-done | bytes 98336 | tf_op jit(solution)/shard_map/all_to_all | solution.py:266
  175.0 21.0 %all_to_all.25.mine_ref = bf16[8,336,128]{2,1,0:T(8,128)(2,1)S(1)} all-to-all(bf16[8,336,128]{2,1,0:T(8,128)(2,1)S(1)} %broadcast_in_dim.46), channel_id=1, replica_groups={{0,2,4,6,8,10,12,14},{1,3,5,7,9,11,13,15},{16,18,20,22,24,26,28,30},{17..., dimensions={0} | all-to-all | bytes 1376256 | tf_op jit(solution)/shard_map/all_to_all | solution.py:266
  196.0 6.8 %collective-permute-start.11 = (bf16[8,336,128]{2,1,0:T(8,128)(2,1)S(1)}, bf16[8,336,128]{2,1,0:T(8,128)(2,1)S(1)}, u32[]{:S(2)}, u32[]{:S(2)}) collective-permute-start(bf16[8,336,128]{2,1,0:T(8,128)(2,1)S(1)} %all_to_all.25.mine_ref), channel_id=1, source_target_pairs={{0,1},{1,0},{2,3},{3,2},{4,5},{5,4},{6,7},{7,6},{8,9},{9,8},{10,11... | collective-permute-start | bytes 2064392 | tf_op jit(solution)/shard_map/ppermute | solution.py:247
  204.5 2.5 %update.1 = (f32[1024,128]{1,0:T(8,128)}, f32[8,128]{1,0:T(8,128)}, f32[1024,128]{1,0:T(8,128)}, f32[512,1024]{1,0:T(8,128)}, f32[8,128]{1,0:T(8,128)}) custom-call(s32[1]{0:T(128)} %bitcast.parity_ref, bf16[8,336,128]{2,1,0:T(8,128)(2,1)S(1)} %all_to_all.25.mine_ref, bf16[8,336,128]{2,1,0:T(8,128)(2,1)S(1)} %collective-permute-done.11.other_ref, ...), custom_call_target="tpu_custom_call" | custom-call | tf_op jit(solution)/shard_map/update/pallas_call | solution.py:224
  (88 shorter events, 14.0 us)
Async XLA Ops:
  0.6 0.7 copy-start
  0.6 26.0 %copy-start.9 = (s32[1,1,6144]{2,1,0:T(1,128)S(1)}, s32[1,1,6144]{2,1,0:T(1,128)}, u32[]{:S(2)}) copy-start(s32[1,1,6144]{2,1,0:T(1,128)} %param.17) | copy-start | bytes 73732
  0.7 27.0 %copy-start.8 = (s32[256,4,8]{0,2,1:T(8,128)S(1)}, s32[256,4,8]{0,2,1:T(8,128)}, u32[]{:S(2)}) copy-start(s32[256,4,8]{0,2,1:T(8,128)} %param.18) | copy-start | bytes 98308
  0.7 27.0 %copy-start.10 = (s32[256,4]{0,1:T(4,128)S(1)}, s32[256,4]{0,1:T(4,128)}, u32[]{:S(2)}) copy-start(s32[256,4]{0,1:T(4,128)} %param.19) | copy-start | bytes 12292
  3.8 1.0 copy-start.1
  7.8 50.5 %all-to-all-start = ((bf16[48,64,128]{2,1,0:T(8,128)(2,1)}), bf16[48,64,128]{2,1,0:T(8,128)(2,1)S(1)}, u32[]{:S(2)}, u32[]{:S(2)}) async-start(bf16[48,64,128]{2,1,0:T(8,128)(2,1)} %bitcast.6), calls=%async_computation | async-start | bytes 1572864 | tf_op jit(solution)/shard_map/all_to_all | solution.py:266
  28.1 3.7 %collective-permute-start = (s32[88,128]{1,0:T(8,128)S(1)}, s32[88,128]{1,0:T(8,128)S(1)}, u32[]{:S(2)}, u32[]{:S(2)}) collective-permute-start(s32[88,128]{1,0:T(8,128)S(1)} %add_bitcast_fusion.1), channel_id=1, source_target_pairs={{0,1},{1,0},{2,3},{3,2},{4,5},{5,4},{6,7},{7,6},{8,9},{9,8},{10,11... | collective-permute-start | bytes 135176 | tf_op jit(solution)/shard_map/ppermute | solution.py:247
  58.3 10.6 %copy-start.12 = (s32[256]{0:T(256)S(1)}, s32[256]{0:T(256)}, u32[]{:S(2)}) copy-start(s32[256]{0:T(256)} %param.20) | copy-start | bytes 3076
  63.8 5.3 %copy-start.11 = (bf16[1024]{0:T(1024)(128)(2,1)S(1)}, bf16[1024]{0:T(1024)(128)(2,1)}, u32[]{:S(2)}) copy-start(bf16[1024]{0:T(1024)(128)(2,1)} %param.23) | copy-start | bytes 6148
  63.8 6.6 %copy-start.7 = (f32[1024]{0:T(1024)S(1)}, f32[1024]{0:T(1024)}, u32[]{:S(2)}) copy-start(f32[1024]{0:T(1024)} %param.22) | copy-start | bytes 12292
  63.9 6.5 %collective-permute-start.1 = (f32[1024,128]{1,0:T(8,128)S(1)}, f32[1024,128]{1,0:T(8,128)S(1)}, u32[]{:S(2)}, u32[]{:S(2)}) collective-permute-start(f32[1024,128]{1,0:T(8,128)S(1)} %get-tuple-element.46), channel_id=1, source_target_pairs={{0,1},{1,0},{2,3},{3,2},{4,5},{5,4},{6,7},{7,6},{8,9},{9,8},{10,11... | collective-permute-start | bytes 1572872 | tf_op jit(solution)/shard_map/ppermute | solution.py:247
  70.4 1.2 copy-start.3
  73.6 0.7 copy-start.4
  74.3 4.4 %collective-permute-start.3 = (bf16[1024,128]{1,0:T(8,128)(2,1)}, bf16[1024,128]{1,0:T(8,128)(2,1)S(1)}, u32[]{:S(2)}, u32[]{:S(2)}) collective-permute-start(bf16[1024,128]{1,0:T(8,128)(2,1)} %get-tuple-element.33), channel_id=1, source_target_pairs={{0,1},{1,0},{2,3},{3,2},{4,5},{5,4},{6,7},{7,6},{8,9},{9,8},{10,11... | collective-permute-start | bytes 786440 | tf_op jit(solution)/shard_map/ppermute | solution.py:247
  76.6 9.3 %collective-permute-start.2 = (bf16[8,272,128]{2,1,0:T(8,128)(2,1)S(1)}, bf16[8,272,128]{2,1,0:T(8,128)(2,1)S(1)}, u32[]{:S(2)}, u32[]{:S(2)}) collective-permute-start(bf16[8,272,128]{2,1,0:T(8,128)(2,1)S(1)} %dynamic-slice_convert_fusion), channel_id=1, source_target_pairs={{0,1},{1,0},{2,3},{3,2},{4,5},{5,4},{6,7},{7,6},{8,9},{9,8},{10,11... | collective-permute-start | bytes 1671176 | tf_op jit(solution)/shard_map/ppermute | solution.py:247
  86.0 37.4 %all-to-all-start.1 = ((bf16[48,64,128]{2,1,0:T(8,128)(2,1)}), bf16[48,64,128]{2,1,0:T(8,128)(2,1)S(1)}, u32[]{:S(2)}, u32[]{:S(2)}) async-start(bf16[48,64,128]{2,1,0:T(8,128)(2,1)} %bitcast.41), calls=%async_computation.1 | async-start | bytes 1572864 | tf_op jit(solution)/shard_map/all_to_all | solution.py:266
  91.8 9.5 %collective-permute-start.4 = (bf16[4,272,128]{2,1,0:T(8,128)(2,1)S(1)}, bf16[4,272,128]{2,1,0:T(8,128)(2,1)S(1)}, u32[]{:S(2)}, u32[]{:S(2)}) collective-permute-start(bf16[4,272,128]{2,1,0:T(8,128)(2,1)S(1)} %dynamic-slice_convert_fusion.1), channel_id=1, source_target_pairs={{0,2},{1,3},{2,0},{3,1},{4,6},{5,7},{6,4},{7,5},{8,10},{9,11},{10,... | collective-permute-start | bytes 835592 | tf_op jit(solution)/shard_map/ppermute | solution.py:247
  101.4 10.3 %collective-permute-start.5 = (bf16[2,272,128]{2,1,0:T(8,128)(2,1)S(1)}, bf16[2,272,128]{2,1,0:T(8,128)(2,1)S(1)}, u32[]{:S(2)}, u32[]{:S(2)}) collective-permute-start(bf16[2,272,128]{2,1,0:T(8,128)(2,1)S(1)} %dynamic-slice_convert_fusion.2), channel_id=1, source_target_pairs={{0,4},{1,5},{2,6},{3,7},{4,0},{5,1},{6,2},{7,3},{8,12},{9,13},{10,... | collective-permute-start | bytes 417800 | tf_op jit(solution)/shard_map/ppermute | solution.py:247
  111.7 10.1 %collective-permute-start.6 = (bf16[1,272,128]{2,1,0:T(8,128)(2,1)S(1)}, bf16[1,272,128]{2,1,0:T(8,128)(2,1)S(1)}, u32[]{:S(2)}, u32[]{:S(2)}) collective-permute-start(bf16[1,272,128]{2,1,0:T(8,128)(2,1)S(1)} %dynamic-slice_convert_fusion.3), channel_id=1, source_target_pairs={{0,8},{1,9},{2,10},{3,11},{4,12},{5,13},{6,14},{7,15},{8,0},{9,1},... | collective-permute-start | bytes 208904 | tf_op jit(solution)/shard_map/ppermute | solution.py:247
  125.3 14.1 %collective-permute-start.7 = (f32[8,64,128]{2,1,0:T(8,128)S(1)}, f32[8,64,128]{2,1,0:T(8,128)S(1)}, u32[]{:S(2)}, u32[]{:S(2)}) collective-permute-start(f32[8,64,128]{2,1,0:T(8,128)S(1)} %constant_dynamic-slice_fusion.3), channel_id=1, source_target_pairs={{0,1},{1,0},{2,3},{3,2},{4,5},{5,4},{6,7},{7,6},{8,9},{9,8},{10,11... | collective-permute-start | bytes 786440 | tf_op jit(solution)/shard_map/ppermute | solution.py:247
  130.5 21.0 %all-to-all-start.2 = ((bf16[48,8,128]{2,1,0:T(8,128)(2,1)}), bf16[48,8,128]{2,1,0:T(8,128)(2,1)S(1)}, u32[]{:S(2)}, u32[]{:S(2)}) async-start(bf16[48,8,128]{2,1,0:T(8,128)(2,1)} %pad_bitcast_fusion), calls=%async_computation.2 | async-start | bytes 196608 | tf_op jit(solution)/shard_map/all_to_all | solution.py:266
  139.4 63.4 %copy-start.6 = (f32[1024]{0:T(1024)S(1)}, f32[1024]{0:T(1024)}, u32[]{:S(2)}) copy-start(f32[1024]{0:T(1024)} %param.14) | copy-start | bytes 12292
  139.4 63.6 %copy-start.5 = (f32[256,1]{1,0:T(8,128)S(1)}, f32[256,1]{1,0:T(8,128)}, u32[]{:S(2)}) copy-start(f32[256,1]{1,0:T(8,128)} %copy-done.4) | copy-start | bytes 3076
  139.5 65.1 %copy-start.2 = (f32[1024,128]{1,0:T(8,128)S(1)}, f32[1024,128]{1,0:T(8,128)}, u32[]{:S(2)}) copy-start(f32[1024,128]{1,0:T(8,128)} %table_ref.3) | copy-start | bytes 1572868
  139.5 12.0 %collective-permute-start.8 = (f32[4,64,128]{2,1,0:T(8,128)S(1)}, f32[4,64,128]{2,1,0:T(8,128)S(1)}, u32[]{:S(2)}, u32[]{:S(2)}) collective-permute-start(f32[4,64,128]{2,1,0:T(8,128)S(1)} %constant_dynamic-slice_fusion.2), channel_id=1, source_target_pairs={{0,2},{1,3},{2,0},{3,1},{4,6},{5,7},{6,4},{7,5},{8,10},{9,11},{10,... | collective-permute-start | bytes 393224 | tf_op jit(solution)/shard_map/ppermute | solution.py:247
  151.6 12.0 %collective-permute-start.9 = (f32[2,64,128]{2,1,0:T(8,128)S(1)}, f32[2,64,128]{2,1,0:T(8,128)S(1)}, u32[]{:S(2)}, u32[]{:S(2)}) collective-permute-start(f32[2,64,128]{2,1,0:T(8,128)S(1)} %constant_dynamic-slice_fusion.1), channel_id=1, source_target_pairs={{0,4},{1,5},{2,6},{3,7},{4,0},{5,1},{6,2},{7,3},{8,12},{9,13},{10,... | collective-permute-start | bytes 196616 | tf_op jit(solution)/shard_map/ppermute | solution.py:247
  155.2 19.7 %all-to-all-start.3 = ((bf16[48,8,128]{2,1,0:T(8,128)(2,1)}), bf16[48,8,128]{2,1,0:T(8,128)(2,1)S(1)}, u32[]{:S(2)}, u32[]{:S(2)}) async-start(bf16[48,8,128]{2,1,0:T(8,128)(2,1)} %broadcast_in_dim.45), calls=%async_computation.3 | async-start | bytes 196608 | tf_op jit(solution)/shard_map/all_to_all | solution.py:266
  163.6 8.9 %collective-permute-start.10 = (f32[1,64,128]{2,1,0:T(8,128)S(1)}, f32[1,64,128]{2,1,0:T(8,128)S(1)}, u32[]{:S(2)}, u32[]{:S(2)}) collective-permute-start(f32[1,64,128]{2,1,0:T(8,128)S(1)} %constant_dynamic-slice_fusion), channel_id=1, source_target_pairs={{0,8},{1,9},{2,10},{3,11},{4,12},{5,13},{6,14},{7,15},{8,0},{9,1},... | collective-permute-start | bytes 98312 | tf_op jit(solution)/shard_map/ppermute | solution.py:247
  196.0 8.5 %collective-permute-start.11 = (bf16[8,336,128]{2,1,0:T(8,128)(2,1)S(1)}, bf16[8,336,128]{2,1,0:T(8,128)(2,1)S(1)}, u32[]{:S(2)}, u32[]{:S(2)}) collective-permute-start(bf16[8,336,128]{2,1,0:T(8,128)(2,1)S(1)} %all_to_all.25.mine_ref), channel_id=1, source_target_pairs={{0,1},{1,0},{2,3},{3,2},{4,5},{5,4},{6,7},{7,6},{8,9},{9,8},{10,11... | collective-permute-start | bytes 2064392 | tf_op jit(solution)/shard_map/ppermute | solution.py:247

commit v3 on v2

--- a/solution.py
+++ b/solution.py
@@ -9,31 +9,43 @@
 
 LEARN_RATE = 0.05
 LANES = 128
+NEAR = 4
 bf16 = jnp.bfloat16
 f32 = jnp.float32
 VMEM = pl.BlockSpec(memory_space=pltpu.VMEM)
 PARAMS = pltpu.CompilerParams(vmem_limit_bytes=48 * 1024 * 1024)
 
 
-def fetch_kernel(slot_ref, table_ref, out_ref):
+def fetch_kernel(side_ref, list_ref, limit_ref, table_ref, out_ref):
     table = table_ref[...].astype(bf16)
-    rows = lax.broadcasted_iota(jnp.int32, (LANES, table.shape[0]), 1)
-    for k in range(slot_ref.shape[1]):
-        hot = jnp.where(slot_ref[:, k : k + 1] == rows, 1.0, 0.0).astype(bf16)
+    peers = list_ref.shape[0]
+    half = list_ref.shape[1] // 2
+    lists = list_ref[...].T
+    side = side_ref[0]
+    lists = jnp.where(side == 0, lists[:half], lists[half:])
+    slots = lax.broadcasted_iota(jnp.int32, (half, peers), 0) + side * half
+    lists = jnp.where(slots < limit_ref[...], lists, -1)
+    rows = lax.broadcasted_iota(jnp.int32, (half, table.shape[0]), 1)
+    for p in range(0, peers, 2):
+        hot = jnp.concatenate(
+            [jnp.where(lists[:, q : q + 1] == rows, 1.0, 0.0).astype(bf16) for q in (p, p + 1)],
+            axis=0,
+        )
         picked = jnp.dot(hot, table, preferred_element_type=f32)
-        out_ref[k * LANES : (k + 1) * LANES, :] = picked.astype(bf16)
-
-
-def fetch(slot_cols, table):
-    slots = slot_cols.shape[1] * LANES
+        out_ref[p * half : (p + 2) * half, :] = picked.astype(bf16)
+
+
+def fetch(side, lists, limits, table):
+    slots = lists.size // 2
+    smem = pl.BlockSpec(memory_space=pltpu.SMEM)
     return pl.pallas_call(
         fetch_kernel,
         out_shape=jax.ShapeDtypeStruct((slots, table.shape[1]), bf16),
-        in_specs=[VMEM] * 2,
+        in_specs=[smem] + [VMEM] * 3,
         out_specs=VMEM,
         compiler_params=PARAMS,
         name="fetch",
-    )(slot_cols, table)
+    )(side.reshape(1), lists, limits[None, :], table)
 
 
 def row_sum_kernel(order, slot_ref, value_ref, out_ref):
@@ -117,18 +129,34 @@
     )(bags, places)
 
 
-def top_kernel(order, own_ref, got_ref, w1_ref, b1_ref, w2_ref, label_ref, logit_ref, part_ref, g_ref):
-    batch = label_ref.shape[0]
-    feats = own_ref.shape[0] // batch
-    spans = [slice(f * batch, (f + 1) * batch) for f in range(feats)]
-    pooled = jnp.concatenate([(own_ref[s, :] + got_ref[s, :]).astype(bf16) for s in spans], axis=1)
+def top_kernel(
+    order,
+    side_ref,
+    here_ref,
+    came_ref,
+    w1_ref,
+    b1_ref,
+    w2_ref,
+    label_ref,
+    logit_ref,
+    part_ref,
+    g_ref,
+):
+    batch = logit_ref.shape[0]
+    bags = here_ref.shape[0] // 2
+    spans = [slice(f * batch, (f + 1) * batch) for f in range(bags // batch)]
+    pooled = []
+    for s in range(2):
+        total = here_ref[s * bags : (s + 1) * bags, :] + came_ref[(1 - s) * bags : (2 - s) * bags, :]
+        pooled.append(jnp.concatenate([total[span].astype(bf16) for span in spans], axis=1))
+    pooled = jnp.concatenate(pooled, axis=0)
     w1 = w1_ref[...]
     pre = jnp.dot(pooled, w1, preferred_element_type=f32) + b1_ref[...]
     sig_pre = jax.nn.sigmoid(pre)
     active = pre * sig_pre
     w2 = w2_ref[...].astype(f32)
     logits = jnp.sum(active * w2, axis=1, keepdims=True)
-    logit_ref[...] = logits
+    logit_ref[...] = logits[:batch]
     error = jax.nn.sigmoid(logits) - label_ref[...].astype(f32)
     part_w2 = jnp.sum(error * active, axis=0, keepdims=True)
     slope = sig_pre * (1.0 + pre * (1.0 - sig_pre))
@@ -136,37 +164,49 @@
     grad_pooled = lax.dot_general(
         grad_pre, w1, (((1,), (1,)), ((), ())), preferred_element_type=f32
     )
-    for f, s in enumerate(spans):
-        g_ref[s, :] = grad_pooled[:, f * LANES : (f + 1) * LANES].astype(bf16)
+    for s in range(2):
+        for f, span in enumerate(spans):
+            block = grad_pooled[s * batch : (s + 1) * batch, f * LANES : (f + 1) * LANES]
+            g_ref[s * bags + span.start : s * bags + span.stop, :] = block.astype(bf16)
+    half = pooled.shape[1] // 2
+    chosen = jnp.where(side_ref[0] == 0, pooled[:, :half], pooled[:, half:])
     part_w1 = lax.dot_general(
-        pooled, grad_pre, (((0,), (0,)), ((), ())), preferred_element_type=f32
+        chosen, grad_pre, (((0,), (0,)), ((), ())), preferred_element_type=f32
     )
     depth, blocks = part_w1.shape[0] // len(order), part_w1.shape[1] // LANES
-    tail = [part_w2[:, j * LANES : (j + 1) * LANES] for j in range(blocks)]
-    tail = jnp.concatenate(tail + [jnp.zeros((16 - blocks, LANES), f32)], axis=0)
+    pieces = part_ref.shape[1]
+    each = blocks // pieces
     for c, place in enumerate(order):
         rows = part_w1[c * depth : (c + 1) * depth, :]
         for j in range(blocks):
-            part_ref[place, j * depth : (j + 1) * depth, :] = rows[:, j * LANES : (j + 1) * LANES]
-        part_ref[place, blocks * depth :, :] = tail if c == 0 else jnp.zeros_like(tail)
-
-
-def top(own, got, w1, b1, w2, labels, order):
-    batch = labels.shape[0]
+            base = j % each * depth
+            block = rows[:, j * LANES : (j + 1) * LANES]
+            part_ref[place, j // each, base : base + depth, :] = block
+        for p in range(pieces):
+            part_ref[place, p, each * depth :, :] = jnp.zeros((blocks, LANES), f32)
+    for j in range(blocks):
+        row = each * depth + j
+        part_ref[order[0], 0, row : row + 1, :] = part_w2[:, j * LANES : (j + 1) * LANES]
+
+
+def top(side, here, came, w1, b1, w2, labels, order, pieces):
+    batch = labels.shape[0] // 2
     chunks = len(order)
-    depth = w1.size // chunks // LANES + 16
+    blocks = w1.shape[1] // LANES
+    depth = w1.size // 2 // chunks // pieces // LANES + blocks
+    smem = pl.BlockSpec(memory_space=pltpu.SMEM)
     return pl.pallas_call(
         functools.partial(top_kernel, order),
         out_shape=(
             jax.ShapeDtypeStruct((batch, 1), f32),
-            jax.ShapeDtypeStruct((chunks, depth, LANES), f32),
-            jax.ShapeDtypeStruct(own.shape, bf16),
+            jax.ShapeDtypeStruct((chunks, pieces, depth, LANES), f32),
+            jax.ShapeDtypeStruct(here.shape, bf16),
         ),
-        in_specs=[VMEM] * 6,
+        in_specs=[smem] + [VMEM] * 6,
         out_specs=(VMEM,) * 3,
         compiler_params=PARAMS,
         name="top",
-    )(own, got, w1, b1, w2, labels)
+    )(side.reshape(1), here, came, w1, b1, w2, labels)
 
 
 def update_kernel(
@@ -185,6 +225,7 @@
     chips, depth, _ = mine_ref.shape
     rows, hidden = table_ref.shape[0], w1_grad_ref.shape[1]
     size, blocks = rows // (2 * chips), hidden // LANES
+    each = blocks // NEAR
     chunk = w1_grad_ref.shape[0] // (2 * chips)
     first = parity_ref[0] == 0
     for y in range(chips):
@@ -193,11 +234,11 @@
             got = jnp.where(first, mine, other) if c == 0 else jnp.where(first, other, mine)
             base = (chips * c + y) * chunk
             for j in range(blocks):
-                w1_grad_ref[base : base + chunk, j * LANES : (j + 1) * LANES] = got[
-                    j * chunk : (j + 1) * chunk, :
-                ]
+                at = j // each * (each * chunk + blocks) + j % each * chunk
+                cols = slice(j * LANES, (j + 1) * LANES)
+                w1_grad_ref[base : base + chunk, cols] = got[at : at + chunk, :]
             if y == 0 and c == 0:
-                w2_grad_ref[...] = got[blocks * chunk : blocks * chunk + blocks, :]
+                w2_grad_ref[...] = got[each * chunk : each * chunk + blocks, :]
             base = (2 * y + c) * size
             row_grad_ref[base : base + size, :] = got[depth - size :, :]
     grad = row_grad_ref[...]
@@ -242,19 +283,29 @@
     return sum((i >> b & 1) << (bits - 1 - b) for b in range(bits))
 
 
-def swap(shard, stride):
-    pairs = [(i, i ^ stride) for i in range(lax.axis_size("reader"))]
-    return lax.ppermute(shard, "reader", pairs)
-
-
-def halve(blocks, sent_type, strides):
-    me = lax.axis_index("reader")
+def swap(shard, stride, axis="reader"):
+    pairs = [(i, i ^ stride) for i in range(lax.axis_size(axis))]
+    return lax.ppermute(shard, axis, pairs)
+
+
+def halve(blocks, sent_type, strides, axis="reader"):
+    me = lax.axis_index(axis)
     for stride in strides:
         half = blocks.shape[0] // 2
         side = me // stride % 2
         kept = lax.dynamic_slice_in_dim(blocks, side * half, half, 0)
         sent = lax.dynamic_slice_in_dim(blocks, (1 - side) * half, half, 0)
-        blocks = kept + swap(sent.astype(sent_type), stride).astype(f32)
+        blocks = kept + swap(sent.astype(sent_type), stride, axis).astype(f32)
+    return blocks
+
+
+def double(blocks, strides, axis):
+    me = lax.axis_index(axis)
+    for stride in strides:
+        came = swap(blocks, stride, axis)
+        low = me // stride % 2 == 0
+        first, second = jnp.where(low, blocks, came), jnp.where(low, came, blocks)
+        blocks = jnp.concatenate([first, second], axis=0)
     return blocks
 
 
@@ -282,7 +333,7 @@
     own_slots = jnp.arange(half, dtype=jnp.int32)[None, :] + parity * half
     own_lists = jnp.where(own_slots < limits[:, None], own_lists, -1)
     slot_rows = own_lists.reshape(-1, LANES)
-    picked = fetch(slot_rows.T, table)
+    picked = fetch(parity, lists, limits, table)
     fetched = exchange(picked.reshape(n_peers, half, width), "owner").reshape(-1, width)
 
     batch, feats, depth = bag_rows.shape
@@ -291,52 +342,52 @@
     places = slot_map.reshape(n_peers, 2, half)
     own_places = lax.dynamic_slice_in_dim(places, parity, 1, 1).reshape(-1)
     other_places = lax.dynamic_slice_in_dim(places, 1 - parity, 1, 1).reshape(-1)
-    sent = jnp.concatenate([bags.reshape(-1), other_places]).reshape(-1, LANES)
+    sent = jnp.concatenate([bags.reshape(-1), other_places, labels]).reshape(-1, LANES)
     came = partner(sent).reshape(-1)
     came_bags = came[: bags.size].reshape(bags.shape)
-    came_places = came[bags.size :]
+    came_places = came[bags.size : -batch]
+    both_labels = jnp.concatenate([labels, came[-batch:]])
     counted = count(
         jnp.concatenate([bags, came_bags], axis=0),
         jnp.stack([own_places, came_places])[:, None, :],
     )
 
     pooled = jnp.dot(counted.astype(bf16), fetched, preferred_element_type=f32)
-    own_pooled, other_pooled = pooled[: batch * feats], pooled[batch * feats :]
-    logits, part, grad_bags = top(
-        own_pooled,
-        partner(other_pooled),
+    logits, part, grad_both = top(
+        parity,
+        pooled,
+        partner(pooled),
         w1,
         b1[None, :],
         w2[None, :],
-        labels[:, None],
-        [c // chips * chips + bit_reversed(c % chips, bits - 1) for c in range(readers)],
-    )
-    grad_both = jnp.concatenate([grad_bags, partner(grad_bags)], axis=0)
+        both_labels[:, None],
+        [bit_reversed(c, bits - 1) for c in range(chips)],
+        NEAR,
+    )
     slot_grad = lax.dot_general(
         counted.astype(bf16), grad_both, (((0,), (0,)), ((), ())), preferred_element_type=f32
     ).astype(bf16)
 
-    part = halve(part, bf16, strides[:1])
+    part = halve(part, bf16, strides[1:2])
     part, slot_grad = lax.optimization_barrier((part, slot_grad))
     returned = exchange(slot_grad.reshape(n_peers, half, width), "owner").reshape(-1, width)
-    part = halve(part, bf16, strides[1:])[0]
+    part = halve(part, bf16, strides[2:])[0]
+    part = halve(part, f32, [1, 2], "owner")[0].astype(bf16)
     part, returned = lax.optimization_barrier((part, returned))
-    order = [bit_reversed(b, bits) for b in range(readers)]
+    order = [b % 2 * chips + b // 2 for b in range(readers)]
     local_grad = row_sum(slot_rows, returned, rows, order)
     block = local_grad.reshape(readers, rows // readers, width)
 
-    piece = 8
-    depth_w = part.shape[0]
-    chunk = jnp.zeros((n_peers * piece, LANES), bf16).at[:depth_w].set(part.astype(bf16))
-    chunk = exchange(chunk.reshape(n_peers, piece, LANES), "owner")
-    chunk = jnp.sum(chunk.astype(f32), axis=0).astype(bf16)
-    block = halve(block, f32, strides[:2])
+    far = n_peers // NEAR
+    part = jnp.broadcast_to(part[None], (far,) + part.shape)
+    part = exchange(part, "owner", [list(range(x, n_peers, NEAR)) for x in range(NEAR)])
+    chunk = jnp.sum(part.astype(f32), axis=0, keepdims=True).astype(bf16)
+    block = halve(block, f32, strides[:1])
     chunk, block = lax.optimization_barrier((chunk, block))
-    chunk = exchange(jnp.broadcast_to(chunk[None], (n_peers, piece, LANES)), "owner")
-    chunk = chunk.reshape(-1, LANES)[:depth_w]
-    block = halve(block, f32, strides[2:])
     same_core = [list(range(c, readers, 2)) for c in range(2)]
-    mine = jnp.concatenate([chunk, block[0].astype(bf16)], axis=0)
+    block = jnp.sum(exchange(block, "reader", same_core), axis=0)
+    chunk = double(chunk, [2, 1], "owner").reshape(-1, LANES)
+    mine = jnp.concatenate([chunk, block.astype(bf16)], axis=0)
     mine = jnp.broadcast_to(mine[None], (chips,) + mine.shape)
     mine = exchange(mine, "reader", same_core)
     new_table, new_accum, row_grad, w1_grad, w2_grad = update(

time: 208 us -> 195 us (0.938)
  waiting for transfers between devices: 44.9 us -> 34 us
  blocking collectives: 21 us -> 16.6 us
  starting transfers between devices: 90.6 us -> 93.1 us
  other arithmetic: 3.17 us -> 5.32 us
    all_to_all x4, waiting for transfers between devices: 23.3 us -> 13.9 us  [exchange(): lax.all_to_all(blocks, axis, split_axis=0, concat_axis=0, tiled=True, axi...]
    all_to_all x1, blocking collectives: 21 us -> 16.6 us  [exchange(): lax.all_to_all(blocks, axis, split_axis=0, concat_axis=0, tiled=True, axi...]
    ppermute x12 -> x11, starting transfers between devices: 48.9 us -> 52.9 us  [swap(): return lax.ppermute(shard, axis, pairs)]
    ppermute x12 -> x11, waiting for transfers between devices: 21.6 us -> 20.2 us  [swap(): return lax.ppermute(shard, axis, pairs)]
  transfers between devices with their start and end apart: 16 -> 15, of which waited for: 11 -> 13; matrix products, arithmetic and copies ran while one was open for 6% -> 7% of each run, Pallas kernels for 8% -> 9%
where the time goes in v3:
time: 195 us; the launch traced here: 194 us
  starting transfers between devices  93.1 us (48%)
  waiting for transfers between devices  34 us (17%)
  Pallas kernels  25.7 us (13%)
  blocking collectives  16.6 us (9%)
  matrix products  12.1 us (6%)
  local copies, waits for them, and re-layouts  5.91 us (3%)
  other arithmetic  5.32 us (3%)
    ppermute x11, starting transfers between devices, swap(): return lax.ppermute(shard, axis, pairs)  52.9 us
    all_to_all x4, starting transfers between devices, exchange(): lax.all_to_all(blocks, axis, split_axis=0, concat_axis=0, tiled=True, axi...  40.2 us
    ppermute x11, waiting for transfers between devices, swap(): return lax.ppermute(shard, axis, pairs)  20.2 us
    all_to_all x1, blocking collectives, exchange(): lax.all_to_all(blocks, axis, split_axis=0, concat_axis=0, tiled=True, axi...  16.6 us
    pallas_call x1, Pallas kernels, count(): pl.pallas_call(count_kernel, grid=(n_bags // block,), out_shape=jax.Shape...  16.3 us
    all_to_all x4, waiting for transfers between devices, exchange(): lax.all_to_all(blocks, axis, split_axis=0, concat_axis=0, tiled=True, axi...  13.9 us
    dot_general x1, matrix products, on_device(): lax.dot_general(counted.astype(bf16), grad_both, (((0,), (0,)), ((), ()))...  6.52 us
    dot_general x1, matrix products, on_device(): pooled = jnp.dot(counted.astype(bf16), fetched, preferred_element_type=f32)  5.57 us
  transfers between devices with their start and end apart: 15, of which 13 were waited for; matrix products, arithmetic and copies ran while one was open for 7% of the time, Pallas kernels for 9%

profile of v3, /device:TPU:1, one launch (start us, length us, event | category | flops | bytes accessed | tf_op | source)
XLA Modules:
  0.0 194.2 jit_solution(459146549237512632)
XLA Ops:
  3.1 2.8 %fetch.1 = bf16[3072,128]{1,0:T(8,128)(2,1)} custom-call(s32[1]{0:T(128)} %bitcast.side_ref.parity_ref, s32[48,128]{1,0:T(8,128)S(1)} %bitcast.40, s32[1,48]{1,0:T(1,128)S(1)} %bitcast.44, f32[1024,128]{1,0:T(8,128)S(1)} %copy-done), custom_call_target="tpu_custom_call" | custom-call | tf_op jit(solution)/shard_map/fetch/pallas_call | solution.py:41
  5.9 18.8 %all-to-all-start = ((bf16[48,64,128]{2,1,0:T(8,128)(2,1)}), bf16[48,64,128]{2,1,0:T(8,128)(2,1)S(1)}, u32[]{:S(2)}, u32[]{:S(2)}) async-start(bf16[48,64,128]{2,1,0:T(8,128)(2,1)} %bitcast.7), calls=%async_computation | async-start | bytes 1572864 | tf_op jit(solution)/shard_map/all_to_all | solution.py:317
  28.9 2.8 %collective-permute-start = (s32[90,128]{1,0:T(8,128)S(1)}, s32[90,128]{1,0:T(8,128)S(1)}, u32[]{:S(2)}, u32[]{:S(2)}) collective-permute-start(s32[90,128]{1,0:T(8,128)S(1)} %add_bitcast_fusion), channel_id=1, source_target_pairs={{0,1},{1,0},{2,3},{3,2},{4,5},{5,4},{6,7},{7,6},{8,9},{9,8},{10,11... | collective-permute-start | bytes 138248 | tf_op jit(solution)/shard_map/ppermute | solution.py:288
  33.1 16.3 %count.1 = f8e4m3fn[2048,3072]{1,0:T(32,128)(4,1)} custom-call(s32[2048,8]{1,0:T(8,128)S(1)} %pad_add_fusion.bag_ref, s32[2,1,3072]{2,1,0:T(1,128)S(1)} %broadcast_in_dim.40.place_ref), custom_call_target="tpu_custom_call" | custom-call | flops 100663296 | bytes 6291456 | tf_op jit(solution)/shard_map/count/pallas_call | solution.py:113
  49.4 7.0 %all-to-all-done = bf16[48,64,128]{2,1,0:T(8,128)(2,1)S(1)} async-done(((bf16[48,64,128]{2,1,0:T(8,128)(2,1)}), bf16[48,64,128]{2,1,0:T(8,128)(2,1)S(1)}, u32[]{:S(2)}, u32[]{:S(2)}) %all-to-all-start) | async-done | bytes 786464 | tf_op jit(solution)/shard_map/all_to_all | solution.py:317
  56.4 5.6 %fusion.2.here_ref = f32[2048,128]{1,0:T(8,128)S(1)} fusion(bf16[3072,128]{1,0:T(8,128)(2,1)S(1)} %bitcast.46, f8e4m3fn[2048,3072]{1,0:T(32,128)(4,1)} %count.1), kind=kOutput, calls=%fused_computation.2 | convolution fusion | flops 1616904192 | bytes 8126464 | tf_op jit(solution)/shard_map/dot_general | solution.py:355
  62.0 5.0 %collective-permute-start.1 = (f32[2048,128]{1,0:T(8,128)S(1)}, f32[2048,128]{1,0:T(8,128)S(1)}, u32[]{:S(2)}, u32[]{:S(2)}) collective-permute-start(f32[2048,128]{1,0:T(8,128)S(1)} %fusion.2.here_ref), channel_id=1, source_target_pairs={{0,1},{1,0},{2,3},{3,2},{4,5},{5,4},{6,7},{7,6},{8,9},{9,8},{10,11... | collective-permute-start | bytes 3145736 | tf_op jit(solution)/shard_map/ppermute | solution.py:288
  67.2 2.0 %collective-permute-done.1.came_ref = f32[2048,128]{1,0:T(8,128)S(1)} collective-permute-done((f32[2048,128]{1,0:T(8,128)S(1)}, f32[2048,128]{1,0:T(8,128)S(1)}, u32[]{:S(2)}, u32[]{:S(2)}) %collective-permute-start.1) | collective-permute-done | bytes 1048608 | tf_op jit(solution)/shard_map/ppermute | solution.py:288
  69.2 2.3 %top.1 = (f32[256,1]{1,0:T(8,128)S(1)}, f32[8,4,72,128]{3,2,1,0:T(8,128)S(1)}, bf16[2048,128]{1,0:T(8,128)(2,1)S(1)}) custom-call(s32[1]{0:T(128)} %bitcast.side_ref.parity_ref, f32[2048,128]{1,0:T(8,128)S(1)} %fusion.2.here_ref, f32[2048,128]{1,0:T(8,128)S(1)} %collective-permute-done.1.came_ref, bf16[512,1024]{1,0:T(8,128)(2,1)S(1)} %copy-done.2, ...), custom_call_target="tpu_custom_call" | custom-call | tf_op jit(solution)/shard_map/top/pallas_call | solution.py:198
  71.6 3.2 %collective-permute-start.2 = (bf16[4,4,72,128]{3,2,1,0:T(8,128)(2,1)S(1)}, bf16[4,4,72,128]{3,2,1,0:T(8,128)(2,1)S(1)}, u32[]{:S(2)}, u32[]{:S(2)}) collective-permute-start(bf16[4,4,72,128]{3,2,1,0:T(8,128)(2,1)S(1)} %dynamic-slice_convert_fusion), channel_id=1, source_target_pairs={{0,2},{1,3},{2,0},{3,1},{4,6},{5,7},{6,4},{7,5},{8,10},{9,11},{10,... | collective-permute-start | bytes 884744 | tf_op jit(solution)/shard_map/ppermute | solution.py:288
  74.8 6.5 %fusion.4 = bf16[3072,128]{1,0:T(8,128)(2,1)} fusion(bf16[2048,128]{1,0:T(8,128)(2,1)S(1)} %get-tuple-element.21, f8e4m3fn[2048,3072]{1,0:T(32,128)(4,1)} %count.1), kind=kOutput, calls=%fused_computation.4 | convolution fusion | flops 1617297408 | bytes 7602176 | tf_op jit(solution)/shard_map/dot_general | solution.py:367
  81.8 5.8 %all-to-all-start.1 = ((bf16[48,64,128]{2,1,0:T(8,128)(2,1)}), bf16[48,64,128]{2,1,0:T(8,128)(2,1)S(1)}, u32[]{:S(2)}, u32[]{:S(2)}) async-start(bf16[48,64,128]{2,1,0:T(8,128)(2,1)} %bitcast.15), calls=%async_computation.1 | async-start | bytes 1572864 | tf_op jit(solution)/shard_map/all_to_all | solution.py:317
  87.7 4.2 %collective-permute-start.3 = (bf16[2,4,72,128]{3,2,1,0:T(8,128)(2,1)S(1)}, bf16[2,4,72,128]{3,2,1,0:T(8,128)(2,1)S(1)}, u32[]{:S(2)}, u32[]{:S(2)}) collective-permute-start(bf16[2,4,72,128]{3,2,1,0:T(8,128)(2,1)S(1)} %dynamic-slice_convert_fusion.1), channel_id=1, source_target_pairs={{0,4},{1,5},{2,6},{3,7},{4,0},{5,1},{6,2},{7,3},{8,12},{9,13},{10,... | collective-permute-start | bytes 442376 | tf_op jit(solution)/shard_map/ppermute | solution.py:288
  92.7 5.6 %collective-permute-done.3 = bf16[2,4,72,128]{3,2,1,0:T(8,128)(2,1)S(1)} collective-permute-done((bf16[2,4,72,128]{3,2,1,0:T(8,128)(2,1)S(1)}, bf16[2,4,72,128]{3,2,1,0:T(8,128)(2,1)S(1)}, u32[]{:S(2)}, u32[]{:S(2)}) %collective-permute-start.3) | collective-permute-done | bytes 147488 | tf_op jit(solution)/shard_map/ppermute | solution.py:288
  98.4 8.2 %collective-permute-start.4 = (bf16[1,4,72,128]{3,2,1,0:T(8,128)(2,1)S(1)}, bf16[1,4,72,128]{3,2,1,0:T(8,128)(2,1)S(1)}, u32[]{:S(2)}, u32[]{:S(2)}) collective-permute-start(bf16[1,4,72,128]{3,2,1,0:T(8,128)(2,1)S(1)} %dynamic-slice_convert_fusion.2), channel_id=1, source_target_pairs={{0,8},{1,9},{2,10},{3,11},{4,12},{5,13},{6,14},{7,15},{8,0},{9,1},... | collective-permute-start | bytes 221192 | tf_op jit(solution)/shard_map/ppermute | solution.py:288
  106.7 1.9 collective-permute-done.4
  108.6 2.7 %collective-permute-start.5 = (f32[2,72,128]{2,1,0:T(8,128)S(1)}, f32[2,72,128]{2,1,0:T(8,128)S(1)}, u32[]{:S(2)}, u32[]{:S(2)}) collective-permute-start(f32[2,72,128]{2,1,0:T(8,128)S(1)} %dynamic-slice_bitcast_fusion), channel_id=1, source_target_pairs={{0,16},{16,0},{32,48},{48,32},{64,80},{80,64},{96,112},{112,96},{1... | collective-permute-start | bytes 221192 | tf_op jit(solution)/shard_map/ppermute | solution.py:288
  111.8 2.6 %collective-permute-done.5 = f32[2,72,128]{2,1,0:T(8,128)S(1)} collective-permute-done((f32[2,72,128]{2,1,0:T(8,128)S(1)}, f32[2,72,128]{2,1,0:T(8,128)S(1)}, u32[]{:S(2)}, u32[]{:S(2)}) %collective-permute-start.5) | collective-permute-done | bytes 73760 | tf_op jit(solution)/shard_map/ppermute | solution.py:288
  114.5 4.3 %collective-permute-start.6 = (f32[1,72,128]{2,1,0:T(8,128)S(1)}, f32[1,72,128]{2,1,0:T(8,128)S(1)}, u32[]{:S(2)}, u32[]{:S(2)}) collective-permute-start(f32[1,72,128]{2,1,0:T(8,128)S(1)} %constant_dynamic-slice_fusion.2), channel_id=1, source_target_pairs={{0,32},{16,48},{32,0},{48,16},{64,96},{80,112},{96,64},{112,80},{1... | collective-permute-start | bytes 110600 | tf_op jit(solution)/shard_map/ppermute | solution.py:288
  118.8 2.1 %collective-permute-done.6 = f32[1,72,128]{2,1,0:T(8,128)S(1)} collective-permute-done((f32[1,72,128]{2,1,0:T(8,128)S(1)}, f32[1,72,128]{2,1,0:T(8,128)S(1)}, u32[]{:S(2)}, u32[]{:S(2)}) %collective-permute-start.6) | collective-permute-done | bytes 36896 | tf_op jit(solution)/shard_map/ppermute | solution.py:288
  121.7 8.7 %all-to-all-start.2 = ((bf16[12,72,128]{2,1,0:T(8,128)(2,1)}), bf16[12,72,128]{2,1,0:T(8,128)(2,1)S(1)}, u32[]{:S(2)}, u32[]{:S(2)}) async-start(bf16[12,72,128]{2,1,0:T(8,128)(2,1)} %broadcast_in_dim.44), calls=%async_computation.2 | async-start | bytes 442368 | tf_op jit(solution)/shard_map/all_to_all | solution.py:317
  130.4 1.8 row_sum.1
  132.3 5.4 %collective-permute-start.7 = (f32[8,64,128]{2,1,0:T(8,128)S(1)}, f32[8,64,128]{2,1,0:T(8,128)S(1)}, u32[]{:S(2)}, u32[]{:S(2)}) collective-permute-start(f32[8,64,128]{2,1,0:T(8,128)S(1)} %constant_dynamic-slice_fusion), channel_id=1, source_target_pairs={{0,1},{1,0},{2,3},{3,2},{4,5},{5,4},{6,7},{7,6},{8,9},{9,8},{10,11... | collective-permute-start | bytes 786440 | tf_op jit(solution)/shard_map/ppermute | solution.py:288
  139.5 2.3 %all-to-all-done.2 = bf16[12,72,128]{2,1,0:T(8,128)(2,1)S(1)} async-done(((bf16[12,72,128]{2,1,0:T(8,128)(2,1)}), bf16[12,72,128]{2,1,0:T(8,128)(2,1)S(1)}, u32[]{:S(2)}, u32[]{:S(2)}) %all-to-all-start.2) | async-done | bytes 221216 | tf_op jit(solution)/shard_map/all_to_all | solution.py:317
  141.9 4.6 %collective-permute-start.8 = (bf16[1,72,128]{2,1,0:T(8,128)(2,1)S(1)}, bf16[1,72,128]{2,1,0:T(8,128)(2,1)S(1)}, u32[]{:S(2)}, u32[]{:S(2)}) collective-permute-start(bf16[1,72,128]{2,1,0:T(8,128)(2,1)S(1)} %bitcast.49), channel_id=1, source_target_pairs={{0,32},{16,48},{32,0},{48,16},{64,96},{80,112},{96,64},{112,80},{1... | collective-permute-start | bytes 55304 | tf_op jit(solution)/shard_map/ppermute | solution.py:288
  146.5 6.8 %all-to-all-start.3 = ((f32[8,64,128]{2,1,0:T(8,128)}), f32[8,64,128]{2,1,0:T(8,128)S(1)}, u32[]{:S(2)}, u32[]{:S(2)}) async-start(f32[8,64,128]{2,1,0:T(8,128)} %dynamic-slice_add_fusion), calls=%async_computation.3 | async-start | bytes 524288 | tf_op jit(solution)/shard_map/all_to_all | solution.py:317
  153.4 1.9 collective-permute-start.9
  155.3 2.8 %collective-permute-done.9 = bf16[2,72,128]{2,1,0:T(8,128)(2,1)S(1)} collective-permute-done((bf16[2,72,128]{2,1,0:T(8,128)(2,1)S(1)}, bf16[2,72,128]{2,1,0:T(8,128)(2,1)S(1)}, u32[]{:S(2)}, u32[]{:S(2)}) %collective-permute-start.9) | collective-permute-done | bytes 36896 | tf_op jit(solution)/shard_map/ppermute | solution.py:288
  158.1 4.6 %all-to-all-done.3 = f32[8,64,128]{2,1,0:T(8,128)S(1)} async-done(((f32[8,64,128]{2,1,0:T(8,128)}), f32[8,64,128]{2,1,0:T(8,128)S(1)}, u32[]{:S(2)}, u32[]{:S(2)}) %all-to-all-start.3) | async-done | bytes 262176 | tf_op jit(solution)/shard_map/all_to_all | solution.py:317
  162.8 16.6 %all_to_all.25.mine_ref = bf16[8,352,128]{2,1,0:T(8,128)(2,1)S(1)} all-to-all(bf16[8,352,128]{2,1,0:T(8,128)(2,1)S(1)} %broadcast_in_dim.46), channel_id=1, replica_groups={{0,2,4,6,8,10,12,14},{1,3,5,7,9,11,13,15},{16,18,20,22,24,26,28,30},{17..., dimensions={0} | all-to-all | bytes 1441792 | tf_op jit(solution)/shard_map/all_to_all | solution.py:317
  179.4 10.4 %collective-permute-start.10 = (bf16[8,352,128]{2,1,0:T(8,128)(2,1)S(1)}, bf16[8,352,128]{2,1,0:T(8,128)(2,1)S(1)}, u32[]{:S(2)}, u32[]{:S(2)}) collective-permute-start(bf16[8,352,128]{2,1,0:T(8,128)(2,1)S(1)} %all_to_all.25.mine_ref), channel_id=1, source_target_pairs={{0,1},{1,0},{2,3},{3,2},{4,5},{5,4},{6,7},{7,6},{8,9},{9,8},{10,11... | collective-permute-start | bytes 2162696 | tf_op jit(solution)/shard_map/ppermute | solution.py:288
  191.7 2.5 %update.1 = (f32[1024,128]{1,0:T(8,128)}, f32[8,128]{1,0:T(8,128)}, f32[1024,128]{1,0:T(8,128)}, f32[512,1024]{1,0:T(8,128)}, f32[8,128]{1,0:T(8,128)}) custom-call(s32[1]{0:T(128)} %bitcast.side_ref.parity_ref, bf16[8,352,128]{2,1,0:T(8,128)(2,1)S(1)} %all_to_all.25.mine_ref, bf16[8,352,128]{2,1,0:T(8,128)(2,1)S(1)} %collective-permute-done.10.other_ref, ...), custom_call_target="tpu_custom_call" | custom-call | tf_op jit(solution)/shard_map/update/pallas_call | solution.py:265
  (81 shorter events, 14.4 us)
Async XLA Ops:
  0.6 1.0 copy-start
  1.7 0.7 copy-start.3
  2.4 0.7 copy-start.7
  5.9 50.5 %all-to-all-start = ((bf16[48,64,128]{2,1,0:T(8,128)(2,1)}), bf16[48,64,128]{2,1,0:T(8,128)(2,1)S(1)}, u32[]{:S(2)}, u32[]{:S(2)}) async-start(bf16[48,64,128]{2,1,0:T(8,128)(2,1)} %bitcast.7), calls=%async_computation | async-start | bytes 1572864 | tf_op jit(solution)/shard_map/all_to_all | solution.py:317
  28.9 3.7 %collective-permute-start = (s32[90,128]{1,0:T(8,128)S(1)}, s32[90,128]{1,0:T(8,128)S(1)}, u32[]{:S(2)}, u32[]{:S(2)}) collective-permute-start(s32[90,128]{1,0:T(8,128)S(1)} %add_bitcast_fusion), channel_id=1, source_target_pairs={{0,1},{1,0},{2,3},{3,2},{4,5},{5,4},{6,7},{7,6},{8,9},{9,8},{10,11... | collective-permute-start | bytes 138248 | tf_op jit(solution)/shard_map/ppermute | solution.py:288
  56.4 10.6 %copy-start.10 = (bf16[1024]{0:T(1024)(128)(2,1)S(1)}, bf16[1024]{0:T(1024)(128)(2,1)}, u32[]{:S(2)}) copy-start(bf16[1024]{0:T(1024)(128)(2,1)} %param.21) | copy-start | bytes 6148
  56.4 10.7 %copy-start.9 = (s32[256]{0:T(256)S(1)}, s32[256]{0:T(256)}, u32[]{:S(2)}) copy-start(s32[256]{0:T(256)} %param.18) | copy-start | bytes 3076
  56.4 12.9 %copy-start.2 = (bf16[512,1024]{1,0:T(8,128)(2,1)S(1)}, bf16[512,1024]{1,0:T(8,128)(2,1)}, u32[]{:S(2)}) copy-start(bf16[512,1024]{1,0:T(8,128)(2,1)} %w1_ref.1) | copy-start | bytes 3145732
  56.4 12.9 %copy-start.6 = (f32[1024]{0:T(1024)S(1)}, f32[1024]{0:T(1024)}, u32[]{:S(2)}) copy-start(f32[1024]{0:T(1024)} %param.20) | copy-start | bytes 12292
  62.0 7.3 %collective-permute-start.1 = (f32[2048,128]{1,0:T(8,128)S(1)}, f32[2048,128]{1,0:T(8,128)S(1)}, u32[]{:S(2)}, u32[]{:S(2)}) collective-permute-start(f32[2048,128]{1,0:T(8,128)S(1)} %fusion.2.here_ref), channel_id=1, source_target_pairs={{0,1},{1,0},{2,3},{3,2},{4,5},{5,4},{6,7},{7,6},{8,9},{9,8},{10,11... | collective-permute-start | bytes 3145736 | tf_op jit(solution)/shard_map/ppermute | solution.py:288
  71.6 10.1 %collective-permute-start.2 = (bf16[4,4,72,128]{3,2,1,0:T(8,128)(2,1)S(1)}, bf16[4,4,72,128]{3,2,1,0:T(8,128)(2,1)S(1)}, u32[]{:S(2)}, u32[]{:S(2)}) collective-permute-start(bf16[4,4,72,128]{3,2,1,0:T(8,128)(2,1)S(1)} %dynamic-slice_convert_fusion), channel_id=1, source_target_pairs={{0,2},{1,3},{2,0},{3,1},{4,6},{5,7},{6,4},{7,5},{8,10},{9,11},{10,... | collective-permute-start | bytes 884744 | tf_op jit(solution)/shard_map/ppermute | solution.py:288
  74.8 17.2 %copy-start.8 = (s32[1,1,48]{2,1,0:T(1,128)S(1)}, s32[1,1,48]{2,1,0:T(1,128)}, u32[]{:S(2)}) copy-start(s32[1,1,48]{2,1,0:T(1,128)} %param.14) | copy-start | bytes 580
  74.8 31.8 %copy-start.4 = (s32[1,1,48,128]{3,2,1,0:T(8,128)S(1)}, s32[1,1,48,128]{3,2,1,0:T(8,128)}, u32[]{:S(2)}) copy-start(s32[1,1,48,128]{3,2,1,0:T(8,128)} %param.13) | copy-start | bytes 73732
  81.4 108.5 %copy-start.5 = (f32[1024]{0:T(1024)S(1)}, f32[1024]{0:T(1024)}, u32[]{:S(2)}) copy-start(f32[1024]{0:T(1024)} %param.12) | copy-start | bytes 12292
  81.8 109.9 %copy-start.1 = (f32[1024,128]{1,0:T(8,128)S(1)}, f32[1024,128]{1,0:T(8,128)}, u32[]{:S(2)}) copy-start(f32[1024,128]{1,0:T(8,128)} %table_ref.3) | copy-start | bytes 1572868
  81.8 39.2 %all-to-all-start.1 = ((bf16[48,64,128]{2,1,0:T(8,128)(2,1)}), bf16[48,64,128]{2,1,0:T(8,128)(2,1)S(1)}, u32[]{:S(2)}, u32[]{:S(2)}) async-start(bf16[48,64,128]{2,1,0:T(8,128)(2,1)} %bitcast.15), calls=%async_computation.1 | async-start | bytes 1572864 | tf_op jit(solution)/shard_map/all_to_all | solution.py:317
  87.7 10.6 %collective-permute-start.3 = (bf16[2,4,72,128]{3,2,1,0:T(8,128)(2,1)S(1)}, bf16[2,4,72,128]{3,2,1,0:T(8,128)(2,1)S(1)}, u32[]{:S(2)}, u32[]{:S(2)}) collective-permute-start(bf16[2,4,72,128]{3,2,1,0:T(8,128)(2,1)S(1)} %dynamic-slice_convert_fusion.1), channel_id=1, source_target_pairs={{0,4},{1,5},{2,6},{3,7},{4,0},{5,1},{6,2},{7,3},{8,12},{9,13},{10,... | collective-permute-start | bytes 442376 | tf_op jit(solution)/shard_map/ppermute | solution.py:288
  98.4 10.3 %collective-permute-start.4 = (bf16[1,4,72,128]{3,2,1,0:T(8,128)(2,1)S(1)}, bf16[1,4,72,128]{3,2,1,0:T(8,128)(2,1)S(1)}, u32[]{:S(2)}, u32[]{:S(2)}) collective-permute-start(bf16[1,4,72,128]{3,2,1,0:T(8,128)(2,1)S(1)} %dynamic-slice_convert_fusion.2), channel_id=1, source_target_pairs={{0,8},{1,9},{2,10},{3,11},{4,12},{5,13},{6,14},{7,15},{8,0},{9,1},... | collective-permute-start | bytes 221192 | tf_op jit(solution)/shard_map/ppermute | solution.py:288
  108.6 5.8 %collective-permute-start.5 = (f32[2,72,128]{2,1,0:T(8,128)S(1)}, f32[2,72,128]{2,1,0:T(8,128)S(1)}, u32[]{:S(2)}, u32[]{:S(2)}) collective-permute-start(f32[2,72,128]{2,1,0:T(8,128)S(1)} %dynamic-slice_bitcast_fusion), channel_id=1, source_target_pairs={{0,16},{16,0},{32,48},{48,32},{64,80},{80,64},{96,112},{112,96},{1... | collective-permute-start | bytes 221192 | tf_op jit(solution)/shard_map/ppermute | solution.py:288
  114.5 6.5 %collective-permute-start.6 = (f32[1,72,128]{2,1,0:T(8,128)S(1)}, f32[1,72,128]{2,1,0:T(8,128)S(1)}, u32[]{:S(2)}, u32[]{:S(2)}) collective-permute-start(f32[1,72,128]{2,1,0:T(8,128)S(1)} %constant_dynamic-slice_fusion.2), channel_id=1, source_target_pairs={{0,32},{16,48},{32,0},{48,16},{64,96},{80,112},{96,64},{112,80},{1... | collective-permute-start | bytes 110600 | tf_op jit(solution)/shard_map/ppermute | solution.py:288
  121.7 20.2 %all-to-all-start.2 = ((bf16[12,72,128]{2,1,0:T(8,128)(2,1)}), bf16[12,72,128]{2,1,0:T(8,128)(2,1)S(1)}, u32[]{:S(2)}, u32[]{:S(2)}) async-start(bf16[12,72,128]{2,1,0:T(8,128)(2,1)} %broadcast_in_dim.44), calls=%async_computation.2 | async-start | bytes 442368 | tf_op jit(solution)/shard_map/all_to_all | solution.py:317
  132.3 6.5 %collective-permute-start.7 = (f32[8,64,128]{2,1,0:T(8,128)S(1)}, f32[8,64,128]{2,1,0:T(8,128)S(1)}, u32[]{:S(2)}, u32[]{:S(2)}) collective-permute-start(f32[8,64,128]{2,1,0:T(8,128)S(1)} %constant_dynamic-slice_fusion), channel_id=1, source_target_pairs={{0,1},{1,0},{2,3},{3,2},{4,5},{5,4},{6,7},{7,6},{8,9},{9,8},{10,11... | collective-permute-start | bytes 786440 | tf_op jit(solution)/shard_map/ppermute | solution.py:288
  141.9 11.4 %collective-permute-start.8 = (bf16[1,72,128]{2,1,0:T(8,128)(2,1)S(1)}, bf16[1,72,128]{2,1,0:T(8,128)(2,1)S(1)}, u32[]{:S(2)}, u32[]{:S(2)}) collective-permute-start(bf16[1,72,128]{2,1,0:T(8,128)(2,1)S(1)} %bitcast.49), channel_id=1, source_target_pairs={{0,32},{16,48},{32,0},{48,16},{64,96},{80,112},{96,64},{112,80},{1... | collective-permute-start | bytes 55304 | tf_op jit(solution)/shard_map/ppermute | solution.py:288
  146.5 16.2 %all-to-all-start.3 = ((f32[8,64,128]{2,1,0:T(8,128)}), f32[8,64,128]{2,1,0:T(8,128)S(1)}, u32[]{:S(2)}, u32[]{:S(2)}) async-start(f32[8,64,128]{2,1,0:T(8,128)} %dynamic-slice_add_fusion), calls=%async_computation.3 | async-start | bytes 524288 | tf_op jit(solution)/shard_map/all_to_all | solution.py:317
  153.4 4.7 %collective-permute-start.9 = (bf16[2,72,128]{2,1,0:T(8,128)(2,1)S(1)}, bf16[2,72,128]{2,1,0:T(8,128)(2,1)S(1)}, u32[]{:S(2)}, u32[]{:S(2)}) collective-permute-start(bf16[2,72,128]{2,1,0:T(8,128)(2,1)S(1)} %pad_maximum_fusion.2), channel_id=1, source_target_pairs={{0,16},{16,0},{32,48},{48,32},{64,80},{80,64},{96,112},{112,96},{1... | collective-permute-start | bytes 110600 | tf_op jit(solution)/shard_map/ppermute | solution.py:288
  179.4 12.3 %collective-permute-start.10 = (bf16[8,352,128]{2,1,0:T(8,128)(2,1)S(1)}, bf16[8,352,128]{2,1,0:T(8,128)(2,1)S(1)}, u32[]{:S(2)}, u32[]{:S(2)}) collective-permute-start(bf16[8,352,128]{2,1,0:T(8,128)(2,1)S(1)} %all_to_all.25.mine_ref), channel_id=1, source_target_pairs={{0,1},{1,0},{2,3},{3,2},{4,5},{5,4},{6,7},{7,6},{8,9},{9,8},{10,11... | collective-permute-start | bytes 2162696 | tf_op jit(solution)/shard_map/ppermute | solution.py:288

commit v4 on v3

--- a/solution.py
+++ b/solution.py
@@ -279,34 +279,50 @@
     return new_table, new_accum.reshape(-1), row_grad, w1_grad, w2_grad.reshape(-1)
 
 
-def bit_reversed(i, bits):
-    return sum((i >> b & 1) << (bits - 1 - b) for b in range(bits))
-
-
-def swap(shard, stride, axis="reader"):
-    pairs = [(i, i ^ stride) for i in range(lax.axis_size(axis))]
+def side_of(index, bits):
+    side = 0
+    for b in bits:
+        side = side ^ (index >> b & 1)
+    return side
+
+
+def swap(shard, mask, axis="reader"):
+    pairs = [(i, i ^ mask) for i in range(lax.axis_size(axis))]
     return lax.ppermute(shard, axis, pairs)
 
 
-def halve(blocks, sent_type, strides, axis="reader"):
+def halve(blocks, sent_type, steps, axis="reader"):
     me = lax.axis_index(axis)
-    for stride in strides:
+    for mask, bits in steps:
         half = blocks.shape[0] // 2
-        side = me // stride % 2
+        side = side_of(me, bits)
         kept = lax.dynamic_slice_in_dim(blocks, side * half, half, 0)
         sent = lax.dynamic_slice_in_dim(blocks, (1 - side) * half, half, 0)
-        blocks = kept + swap(sent.astype(sent_type), stride, axis).astype(f32)
+        blocks = kept + swap(sent.astype(sent_type), mask, axis).astype(f32)
     return blocks
 
 
-def double(blocks, strides, axis):
+def double(blocks, steps, axis):
     me = lax.axis_index(axis)
-    for stride in strides:
-        came = swap(blocks, stride, axis)
-        low = me // stride % 2 == 0
+    for mask, bits in reversed(steps):
+        came = swap(blocks, mask, axis)
+        low = side_of(me, bits) == 0
         first, second = jnp.where(low, blocks, came), jnp.where(low, came, blocks)
         blocks = jnp.concatenate([first, second], axis=0)
     return blocks
+
+
+def ring_steps(low, n):
+    last = low + n - 1
+    steps = [(1 << b, (b, last)) for b in range(low, last)]
+    return steps + [(sum(1 << b for b in range(low, last + 1)), (last,))]
+
+
+def places(steps, count):
+    return [
+        sum(side_of(i, bits) << (len(steps) - 1 - k) for k, (_, bits) in enumerate(steps))
+        for i in range(count)
+    ]
 
 
 def partner(shard):
@@ -326,8 +342,10 @@
     rows, width = table.shape
     half = slots // 2
     readers = lax.axis_size("reader")
-    chips, bits = readers // 2, readers.bit_length() - 1
-    strides = [1 << b for b in range(bits)]
+    chips = readers // 2
+    chip_bits = chips.bit_length() - 1
+    chip_steps = ring_steps(1, chip_bits)
+    near_steps = ring_steps(0, NEAR.bit_length() - 1)
     parity = lax.axis_index("reader") % 2
     own_lists = lax.dynamic_slice_in_dim(lists, parity * half, half, 1)
     own_slots = jnp.arange(half, dtype=jnp.int32)[None, :] + parity * half
@@ -339,9 +357,9 @@
     batch, feats, depth = bag_rows.shape
     inside = jnp.arange(depth, dtype=jnp.int32)[None, None, :] < bag_len[:, :, None]
     bags = jnp.where(inside, bag_rows, -1).transpose(1, 0, 2).reshape(-1, depth)
-    places = slot_map.reshape(n_peers, 2, half)
-    own_places = lax.dynamic_slice_in_dim(places, parity, 1, 1).reshape(-1)
-    other_places = lax.dynamic_slice_in_dim(places, 1 - parity, 1, 1).reshape(-1)
+    cached = slot_map.reshape(n_peers, 2, half)
+    own_places = lax.dynamic_slice_in_dim(cached, parity, 1, 1).reshape(-1)
+    other_places = lax.dynamic_slice_in_dim(cached, 1 - parity, 1, 1).reshape(-1)
     sent = jnp.concatenate([bags.reshape(-1), other_places, labels]).reshape(-1, LANES)
     came = partner(sent).reshape(-1)
     came_bags = came[: bags.size].reshape(bags.shape)
@@ -361,18 +379,18 @@
         b1[None, :],
         w2[None, :],
         both_labels[:, None],
-        [bit_reversed(c, bits - 1) for c in range(chips)],
+        places(ring_steps(0, chip_bits), chips),
         NEAR,
     )
     slot_grad = lax.dot_general(
         counted.astype(bf16), grad_both, (((0,), (0,)), ((), ())), preferred_element_type=f32
     ).astype(bf16)
 
-    part = halve(part, bf16, strides[1:2])
+    part = halve(part, bf16, chip_steps[:1])
     part, slot_grad = lax.optimization_barrier((part, slot_grad))
     returned = exchange(slot_grad.reshape(n_peers, half, width), "owner").reshape(-1, width)
-    part = halve(part, bf16, strides[2:])[0]
-    part = halve(part, f32, [1, 2], "owner")[0].astype(bf16)
+    part = halve(part, bf16, chip_steps[1:])[0]
+    part = halve(part, f32, near_steps, "owner")[0].astype(bf16)
     part, returned = lax.optimization_barrier((part, returned))
     order = [b % 2 * chips + b // 2 for b in range(readers)]
     local_grad = row_sum(slot_rows, returned, rows, order)
@@ -382,11 +400,11 @@
     part = jnp.broadcast_to(part[None], (far,) + part.shape)
     part = exchange(part, "owner", [list(range(x, n_peers, NEAR)) for x in range(NEAR)])
     chunk = jnp.sum(part.astype(f32), axis=0, keepdims=True).astype(bf16)
-    block = halve(block, f32, strides[:1])
+    block = halve(block, f32, [(1, (0,))])
     chunk, block = lax.optimization_barrier((chunk, block))
     same_core = [list(range(c, readers, 2)) for c in range(2)]
     block = jnp.sum(exchange(block, "reader", same_core), axis=0)
-    chunk = double(chunk, [2, 1], "owner").reshape(-1, LANES)
+    chunk = double(chunk, near_steps, "owner").reshape(-1, LANES)
     mine = jnp.concatenate([chunk, block.astype(bf16)], axis=0)
     mine = jnp.broadcast_to(mine[None], (chips,) + mine.shape)
     mine = exchange(mine, "reader", same_core)

time: 195 us -> 193 us (0.990)
  transfers between devices with their start and end apart: 15 -> 15, of which waited for: 13 -> 14; matrix products, arithmetic and copies ran while one was open for 7% -> 7% of each run, Pallas kernels for 9% -> 9%
where the time goes in v4:
time: 193 us; the launch traced here: 192 us
  starting transfers between devices  91.3 us (47%)
  waiting for transfers between devices  33.1 us (17%)
  Pallas kernels  25.7 us (13%)
  blocking collectives  17.1 us (9%)
  matrix products  12.1 us (6%)
  local copies, waits for them, and re-layouts  5.91 us (3%)
  other arithmetic  5.32 us (3%)
    ppermute x11, starting transfers between devices, swap(): return lax.ppermute(shard, axis, pairs)  51.1 us
    all_to_all x4, starting transfers between devices, exchange(): lax.all_to_all(blocks, axis, split_axis=0, concat_axis=0, tiled=True, axi...  40.1 us
    ppermute x11, waiting for transfers between devices, swap(): return lax.ppermute(shard, axis, pairs)  19.3 us
    all_to_all x1, blocking collectives, exchange(): lax.all_to_all(blocks, axis, split_axis=0, concat_axis=0, tiled=True, axi...  17.1 us
    pallas_call x1, Pallas kernels, count(): pl.pallas_call(count_kernel, grid=(n_bags // block,), out_shape=jax.Shape...  16.3 us
    all_to_all x4, waiting for transfers between devices, exchange(): lax.all_to_all(blocks, axis, split_axis=0, concat_axis=0, tiled=True, axi...  13.8 us
    dot_general x1, matrix products, on_device(): lax.dot_general(counted.astype(bf16), grad_both, (((0,), (0,)), ((), ()))...  6.52 us
    dot_general x1, matrix products, on_device(): pooled = jnp.dot(counted.astype(bf16), fetched, preferred_element_type=f32)  5.57 us
  transfers between devices with their start and end apart: 15, of which 14 were waited for; matrix products, arithmetic and copies ran while one was open for 7% of the time, Pallas kernels for 9%

profile of v4, /device:TPU:1, one launch (start us, length us, event | category | flops | bytes accessed | tf_op | source)
XLA Modules:
  0.0 191.8 jit_solution(4322164048374476435)
XLA Ops:
  3.1 2.8 %fetch.1 = bf16[3072,128]{1,0:T(8,128)(2,1)} custom-call(s32[1]{0:T(128)} %bitcast.side_ref.parity_ref, s32[48,128]{1,0:T(8,128)S(1)} %bitcast.40, s32[1,48]{1,0:T(1,128)S(1)} %bitcast.44, f32[1024,128]{1,0:T(8,128)S(1)} %copy-done), custom_call_target="tpu_custom_call" | custom-call | tf_op jit(solution)/shard_map/fetch/pallas_call | solution.py:41
  5.9 18.8 %all-to-all-start = ((bf16[48,64,128]{2,1,0:T(8,128)(2,1)}), bf16[48,64,128]{2,1,0:T(8,128)(2,1)S(1)}, u32[]{:S(2)}, u32[]{:S(2)}) async-start(bf16[48,64,128]{2,1,0:T(8,128)(2,1)} %bitcast.7), calls=%async_computation | async-start | bytes 1572864 | tf_op jit(solution)/shard_map/all_to_all | solution.py:333
  28.9 2.8 %collective-permute-start = (s32[90,128]{1,0:T(8,128)S(1)}, s32[90,128]{1,0:T(8,128)S(1)}, u32[]{:S(2)}, u32[]{:S(2)}) collective-permute-start(s32[90,128]{1,0:T(8,128)S(1)} %add_bitcast_fusion), channel_id=1, source_target_pairs={{0,1},{1,0},{2,3},{3,2},{4,5},{5,4},{6,7},{7,6},{8,9},{9,8},{10,11... | collective-permute-start | bytes 138248 | tf_op jit(solution)/shard_map/ppermute | solution.py:291
  33.1 16.3 %count.1 = f8e4m3fn[2048,3072]{1,0:T(32,128)(4,1)} custom-call(s32[2048,8]{1,0:T(8,128)S(1)} %pad_add_fusion.bag_ref, s32[2,1,3072]{2,1,0:T(1,128)S(1)} %broadcast_in_dim.40.place_ref), custom_call_target="tpu_custom_call" | custom-call | flops 100663296 | bytes 6291456 | tf_op jit(solution)/shard_map/count/pallas_call | solution.py:113
  49.4 7.0 %all-to-all-done = bf16[48,64,128]{2,1,0:T(8,128)(2,1)S(1)} async-done(((bf16[48,64,128]{2,1,0:T(8,128)(2,1)}), bf16[48,64,128]{2,1,0:T(8,128)(2,1)S(1)}, u32[]{:S(2)}, u32[]{:S(2)}) %all-to-all-start) | async-done | bytes 786464 | tf_op jit(solution)/shard_map/all_to_all | solution.py:333
  56.4 5.6 %fusion.2.here_ref = f32[2048,128]{1,0:T(8,128)S(1)} fusion(bf16[3072,128]{1,0:T(8,128)(2,1)S(1)} %bitcast.46, f8e4m3fn[2048,3072]{1,0:T(32,128)(4,1)} %count.1), kind=kOutput, calls=%fused_computation.2 | convolution fusion | flops 1616904192 | bytes 8126464 | tf_op jit(solution)/shard_map/dot_general | solution.py:373
  62.0 5.0 %collective-permute-start.1 = (f32[2048,128]{1,0:T(8,128)S(1)}, f32[2048,128]{1,0:T(8,128)S(1)}, u32[]{:S(2)}, u32[]{:S(2)}) collective-permute-start(f32[2048,128]{1,0:T(8,128)S(1)} %fusion.2.here_ref), channel_id=1, source_target_pairs={{0,1},{1,0},{2,3},{3,2},{4,5},{5,4},{6,7},{7,6},{8,9},{9,8},{10,11... | collective-permute-start | bytes 3145736 | tf_op jit(solution)/shard_map/ppermute | solution.py:291
  67.2 2.0 %collective-permute-done.1.came_ref = f32[2048,128]{1,0:T(8,128)S(1)} collective-permute-done((f32[2048,128]{1,0:T(8,128)S(1)}, f32[2048,128]{1,0:T(8,128)S(1)}, u32[]{:S(2)}, u32[]{:S(2)}) %collective-permute-start.1) | collective-permute-done | bytes 1048608 | tf_op jit(solution)/shard_map/ppermute | solution.py:291
  69.2 2.3 %top.1 = (f32[256,1]{1,0:T(8,128)S(1)}, f32[8,4,72,128]{3,2,1,0:T(8,128)S(1)}, bf16[2048,128]{1,0:T(8,128)(2,1)S(1)}) custom-call(s32[1]{0:T(128)} %bitcast.side_ref.parity_ref, f32[2048,128]{1,0:T(8,128)S(1)} %fusion.2.here_ref, f32[2048,128]{1,0:T(8,128)S(1)} %collective-permute-done.1.came_ref, bf16[512,1024]{1,0:T(8,128)(2,1)S(1)} %copy-done.2, ...), custom_call_target="tpu_custom_call" | custom-call | tf_op jit(solution)/shard_map/top/pallas_call | solution.py:198
  71.6 3.2 %collective-permute-start.2 = (bf16[4,4,72,128]{3,2,1,0:T(8,128)(2,1)S(1)}, bf16[4,4,72,128]{3,2,1,0:T(8,128)(2,1)S(1)}, u32[]{:S(2)}, u32[]{:S(2)}) collective-permute-start(bf16[4,4,72,128]{3,2,1,0:T(8,128)(2,1)S(1)} %dynamic-slice_convert_fusion), channel_id=1, source_target_pairs={{0,2},{1,3},{2,0},{3,1},{4,6},{5,7},{6,4},{7,5},{8,10},{9,11},{10,... | collective-permute-start | bytes 884744 | tf_op jit(solution)/shard_map/ppermute | solution.py:291
  74.9 6.5 %fusion.4 = bf16[3072,128]{1,0:T(8,128)(2,1)} fusion(bf16[2048,128]{1,0:T(8,128)(2,1)S(1)} %get-tuple-element.21, f8e4m3fn[2048,3072]{1,0:T(32,128)(4,1)} %count.1), kind=kOutput, calls=%fused_computation.4 | convolution fusion | flops 1617297408 | bytes 7602176 | tf_op jit(solution)/shard_map/dot_general | solution.py:385
  81.8 5.8 %all-to-all-start.1 = ((bf16[48,64,128]{2,1,0:T(8,128)(2,1)}), bf16[48,64,128]{2,1,0:T(8,128)(2,1)S(1)}, u32[]{:S(2)}, u32[]{:S(2)}) async-start(bf16[48,64,128]{2,1,0:T(8,128)(2,1)} %bitcast.15), calls=%async_computation.1 | async-start | bytes 1572864 | tf_op jit(solution)/shard_map/all_to_all | solution.py:333
  87.7 4.2 %collective-permute-start.3 = (bf16[2,4,72,128]{3,2,1,0:T(8,128)(2,1)S(1)}, bf16[2,4,72,128]{3,2,1,0:T(8,128)(2,1)S(1)}, u32[]{:S(2)}, u32[]{:S(2)}) collective-permute-start(bf16[2,4,72,128]{3,2,1,0:T(8,128)(2,1)S(1)} %dynamic-slice_convert_fusion.1), channel_id=1, source_target_pairs={{0,4},{1,5},{2,6},{3,7},{4,0},{5,1},{6,2},{7,3},{8,12},{9,13},{10,... | collective-permute-start | bytes 442376 | tf_op jit(solution)/shard_map/ppermute | solution.py:291
  92.6 5.7 %collective-permute-done.3 = bf16[2,4,72,128]{3,2,1,0:T(8,128)(2,1)S(1)} collective-permute-done((bf16[2,4,72,128]{3,2,1,0:T(8,128)(2,1)S(1)}, bf16[2,4,72,128]{3,2,1,0:T(8,128)(2,1)S(1)}, u32[]{:S(2)}, u32[]{:S(2)}) %collective-permute-start.3) | collective-permute-done | bytes 147488 | tf_op jit(solution)/shard_map/ppermute | solution.py:291
  98.4 5.4 %collective-permute-start.4 = (bf16[1,4,72,128]{3,2,1,0:T(8,128)(2,1)S(1)}, bf16[1,4,72,128]{3,2,1,0:T(8,128)(2,1)S(1)}, u32[]{:S(2)}, u32[]{:S(2)}) collective-permute-start(bf16[1,4,72,128]{3,2,1,0:T(8,128)(2,1)S(1)} %dynamic-slice_convert_fusion.2), channel_id=1, source_target_pairs={{0,14},{1,15},{2,12},{3,13},{4,10},{5,11},{6,8},{7,9},{8,6},{9,7},... | collective-permute-start | bytes 221192 | tf_op jit(solution)/shard_map/ppermute | solution.py:291
  103.9 1.9 collective-permute-done.4
  105.8 3.8 %collective-permute-start.5 = (f32[2,72,128]{2,1,0:T(8,128)S(1)}, f32[2,72,128]{2,1,0:T(8,128)S(1)}, u32[]{:S(2)}, u32[]{:S(2)}) collective-permute-start(f32[2,72,128]{2,1,0:T(8,128)S(1)} %dynamic-slice_bitcast_fusion), channel_id=1, source_target_pairs={{0,16},{16,0},{32,48},{48,32},{64,80},{80,64},{96,112},{112,96},{1... | collective-permute-start | bytes 221192 | tf_op jit(solution)/shard_map/ppermute | solution.py:291
  110.0 2.0 %collective-permute-done.5 = f32[2,72,128]{2,1,0:T(8,128)S(1)} collective-permute-done((f32[2,72,128]{2,1,0:T(8,128)S(1)}, f32[2,72,128]{2,1,0:T(8,128)S(1)}, u32[]{:S(2)}, u32[]{:S(2)}) %collective-permute-start.5) | collective-permute-done | bytes 73760 | tf_op jit(solution)/shard_map/ppermute | solution.py:291
  112.0 4.5 %collective-permute-start.6 = (f32[1,72,128]{2,1,0:T(8,128)S(1)}, f32[1,72,128]{2,1,0:T(8,128)S(1)}, u32[]{:S(2)}, u32[]{:S(2)}) collective-permute-start(f32[1,72,128]{2,1,0:T(8,128)S(1)} %constant_dynamic-slice_fusion.2), channel_id=1, source_target_pairs={{0,48},{16,32},{32,16},{48,0},{64,112},{80,96},{96,80},{112,64},{1... | collective-permute-start | bytes 110600 | tf_op jit(solution)/shard_map/ppermute | solution.py:291
  116.5 1.9 collective-permute-done.6
  119.5 8.8 %all-to-all-start.2 = ((bf16[12,72,128]{2,1,0:T(8,128)(2,1)}), bf16[12,72,128]{2,1,0:T(8,128)(2,1)S(1)}, u32[]{:S(2)}, u32[]{:S(2)}) async-start(bf16[12,72,128]{2,1,0:T(8,128)(2,1)} %broadcast_in_dim.44), calls=%async_computation.2 | async-start | bytes 442368 | tf_op jit(solution)/shard_map/all_to_all | solution.py:333
  128.3 1.8 row_sum.1
  130.1 5.9 %collective-permute-start.7 = (f32[8,64,128]{2,1,0:T(8,128)S(1)}, f32[8,64,128]{2,1,0:T(8,128)S(1)}, u32[]{:S(2)}, u32[]{:S(2)}) collective-permute-start(f32[8,64,128]{2,1,0:T(8,128)S(1)} %constant_dynamic-slice_fusion), channel_id=1, source_target_pairs={{0,1},{1,0},{2,3},{3,2},{4,5},{5,4},{6,7},{7,6},{8,9},{9,8},{10,11... | collective-permute-start | bytes 786440 | tf_op jit(solution)/shard_map/ppermute | solution.py:291
  137.9 1.8 all-to-all-done.2
  139.7 4.6 %collective-permute-start.8 = (bf16[1,72,128]{2,1,0:T(8,128)(2,1)S(1)}, bf16[1,72,128]{2,1,0:T(8,128)(2,1)S(1)}, u32[]{:S(2)}, u32[]{:S(2)}) collective-permute-start(bf16[1,72,128]{2,1,0:T(8,128)(2,1)S(1)} %bitcast.49), channel_id=1, source_target_pairs={{0,48},{16,32},{32,16},{48,0},{64,112},{80,96},{96,80},{112,64},{1... | collective-permute-start | bytes 55304 | tf_op jit(solution)/shard_map/ppermute | solution.py:291
  144.3 6.7 %all-to-all-start.3 = ((f32[8,64,128]{2,1,0:T(8,128)}), f32[8,64,128]{2,1,0:T(8,128)S(1)}, u32[]{:S(2)}, u32[]{:S(2)}) async-start(f32[8,64,128]{2,1,0:T(8,128)} %dynamic-slice_add_fusion), calls=%async_computation.3 | async-start | bytes 524288 | tf_op jit(solution)/shard_map/all_to_all | solution.py:333
  151.0 1.9 %collective-permute-start.9 = (bf16[2,72,128]{2,1,0:T(8,128)(2,1)S(1)}, bf16[2,72,128]{2,1,0:T(8,128)(2,1)S(1)}, u32[]{:S(2)}, u32[]{:S(2)}) collective-permute-start(bf16[2,72,128]{2,1,0:T(8,128)(2,1)S(1)} %pad_maximum_fusion.2), channel_id=1, source_target_pairs={{0,16},{16,0},{32,48},{48,32},{64,80},{80,64},{96,112},{112,96},{1... | collective-permute-start | bytes 110600 | tf_op jit(solution)/shard_map/ppermute | solution.py:291
  153.0 2.8 %collective-permute-done.9 = bf16[2,72,128]{2,1,0:T(8,128)(2,1)S(1)} collective-permute-done((bf16[2,72,128]{2,1,0:T(8,128)(2,1)S(1)}, bf16[2,72,128]{2,1,0:T(8,128)(2,1)S(1)}, u32[]{:S(2)}, u32[]{:S(2)}) %collective-permute-start.9) | collective-permute-done | bytes 36896 | tf_op jit(solution)/shard_map/ppermute | solution.py:291
  155.8 4.6 %all-to-all-done.3 = f32[8,64,128]{2,1,0:T(8,128)S(1)} async-done(((f32[8,64,128]{2,1,0:T(8,128)}), f32[8,64,128]{2,1,0:T(8,128)S(1)}, u32[]{:S(2)}, u32[]{:S(2)}) %all-to-all-start.3) | async-done | bytes 262176 | tf_op jit(solution)/shard_map/all_to_all | solution.py:333
  160.5 17.1 %all_to_all.25.mine_ref = bf16[8,352,128]{2,1,0:T(8,128)(2,1)S(1)} all-to-all(bf16[8,352,128]{2,1,0:T(8,128)(2,1)S(1)} %broadcast_in_dim.46), channel_id=1, replica_groups={{0,2,4,6,8,10,12,14},{1,3,5,7,9,11,13,15},{16,18,20,22,24,26,28,30},{17..., dimensions={0} | all-to-all | bytes 1441792 | tf_op jit(solution)/shard_map/all_to_all | solution.py:333
  177.6 9.8 %collective-permute-start.10 = (bf16[8,352,128]{2,1,0:T(8,128)(2,1)S(1)}, bf16[8,352,128]{2,1,0:T(8,128)(2,1)S(1)}, u32[]{:S(2)}, u32[]{:S(2)}) collective-permute-start(bf16[8,352,128]{2,1,0:T(8,128)(2,1)S(1)} %all_to_all.25.mine_ref), channel_id=1, source_target_pairs={{0,1},{1,0},{2,3},{3,2},{4,5},{5,4},{6,7},{7,6},{8,9},{9,8},{10,11... | collective-permute-start | bytes 2162696 | tf_op jit(solution)/shard_map/ppermute | solution.py:291
  189.2 2.5 %update.1 = (f32[1024,128]{1,0:T(8,128)}, f32[8,128]{1,0:T(8,128)}, f32[1024,128]{1,0:T(8,128)}, f32[512,1024]{1,0:T(8,128)}, f32[8,128]{1,0:T(8,128)}) custom-call(s32[1]{0:T(128)} %bitcast.side_ref.parity_ref, bf16[8,352,128]{2,1,0:T(8,128)(2,1)S(1)} %all_to_all.25.mine_ref, bf16[8,352,128]{2,1,0:T(8,128)(2,1)S(1)} %collective-permute-done.10.other_ref, ...), custom_call_target="tpu_custom_call" | custom-call | tf_op jit(solution)/shard_map/update/pallas_call | solution.py:265
  (81 shorter events, 14.7 us)
Async XLA Ops:
  0.6 1.0 copy-start
  1.7 0.7 copy-start.3
  2.4 0.7 copy-start.7
  5.9 50.5 %all-to-all-start = ((bf16[48,64,128]{2,1,0:T(8,128)(2,1)}), bf16[48,64,128]{2,1,0:T(8,128)(2,1)S(1)}, u32[]{:S(2)}, u32[]{:S(2)}) async-start(bf16[48,64,128]{2,1,0:T(8,128)(2,1)} %bitcast.7), calls=%async_computation | async-start | bytes 1572864 | tf_op jit(solution)/shard_map/all_to_all | solution.py:333
  28.9 3.7 %collective-permute-start = (s32[90,128]{1,0:T(8,128)S(1)}, s32[90,128]{1,0:T(8,128)S(1)}, u32[]{:S(2)}, u32[]{:S(2)}) collective-permute-start(s32[90,128]{1,0:T(8,128)S(1)} %add_bitcast_fusion), channel_id=1, source_target_pairs={{0,1},{1,0},{2,3},{3,2},{4,5},{5,4},{6,7},{7,6},{8,9},{9,8},{10,11... | collective-permute-start | bytes 138248 | tf_op jit(solution)/shard_map/ppermute | solution.py:291
  56.4 10.6 %copy-start.10 = (bf16[1024]{0:T(1024)(128)(2,1)S(1)}, bf16[1024]{0:T(1024)(128)(2,1)}, u32[]{:S(2)}) copy-start(bf16[1024]{0:T(1024)(128)(2,1)} %param.21) | copy-start | bytes 6148
  56.4 10.6 %copy-start.9 = (s32[256]{0:T(256)S(1)}, s32[256]{0:T(256)}, u32[]{:S(2)}) copy-start(s32[256]{0:T(256)} %param.18) | copy-start | bytes 3076
  56.4 12.8 %copy-start.2 = (bf16[512,1024]{1,0:T(8,128)(2,1)S(1)}, bf16[512,1024]{1,0:T(8,128)(2,1)}, u32[]{:S(2)}) copy-start(bf16[512,1024]{1,0:T(8,128)(2,1)} %w1_ref.1) | copy-start | bytes 3145732
  56.4 12.8 %copy-start.6 = (f32[1024]{0:T(1024)S(1)}, f32[1024]{0:T(1024)}, u32[]{:S(2)}) copy-start(f32[1024]{0:T(1024)} %param.20) | copy-start | bytes 12292
  62.0 7.3 %collective-permute-start.1 = (f32[2048,128]{1,0:T(8,128)S(1)}, f32[2048,128]{1,0:T(8,128)S(1)}, u32[]{:S(2)}, u32[]{:S(2)}) collective-permute-start(f32[2048,128]{1,0:T(8,128)S(1)} %fusion.2.here_ref), channel_id=1, source_target_pairs={{0,1},{1,0},{2,3},{3,2},{4,5},{5,4},{6,7},{7,6},{8,9},{9,8},{10,11... | collective-permute-start | bytes 3145736 | tf_op jit(solution)/shard_map/ppermute | solution.py:291
  71.6 10.1 %collective-permute-start.2 = (bf16[4,4,72,128]{3,2,1,0:T(8,128)(2,1)S(1)}, bf16[4,4,72,128]{3,2,1,0:T(8,128)(2,1)S(1)}, u32[]{:S(2)}, u32[]{:S(2)}) collective-permute-start(bf16[4,4,72,128]{3,2,1,0:T(8,128)(2,1)S(1)} %dynamic-slice_convert_fusion), channel_id=1, source_target_pairs={{0,2},{1,3},{2,0},{3,1},{4,6},{5,7},{6,4},{7,5},{8,10},{9,11},{10,... | collective-permute-start | bytes 884744 | tf_op jit(solution)/shard_map/ppermute | solution.py:291
  74.8 17.1 %copy-start.8 = (s32[1,1,48]{2,1,0:T(1,128)S(1)}, s32[1,1,48]{2,1,0:T(1,128)}, u32[]{:S(2)}) copy-start(s32[1,1,48]{2,1,0:T(1,128)} %param.14) | copy-start | bytes 580
  74.9 28.9 %copy-start.4 = (s32[1,1,48,128]{3,2,1,0:T(8,128)S(1)}, s32[1,1,48,128]{3,2,1,0:T(8,128)}, u32[]{:S(2)}) copy-start(s32[1,1,48,128]{3,2,1,0:T(8,128)} %param.13) | copy-start | bytes 73732
  81.4 106.1 %copy-start.5 = (f32[1024]{0:T(1024)S(1)}, f32[1024]{0:T(1024)}, u32[]{:S(2)}) copy-start(f32[1024]{0:T(1024)} %param.12) | copy-start | bytes 12292
  81.8 107.5 %copy-start.1 = (f32[1024,128]{1,0:T(8,128)S(1)}, f32[1024,128]{1,0:T(8,128)}, u32[]{:S(2)}) copy-start(f32[1024,128]{1,0:T(8,128)} %table_ref.3) | copy-start | bytes 1572868
  81.8 37.0 %all-to-all-start.1 = ((bf16[48,64,128]{2,1,0:T(8,128)(2,1)}), bf16[48,64,128]{2,1,0:T(8,128)(2,1)S(1)}, u32[]{:S(2)}, u32[]{:S(2)}) async-start(bf16[48,64,128]{2,1,0:T(8,128)(2,1)} %bitcast.15), calls=%async_computation.1 | async-start | bytes 1572864 | tf_op jit(solution)/shard_map/all_to_all | solution.py:333
  87.7 10.6 %collective-permute-start.3 = (bf16[2,4,72,128]{3,2,1,0:T(8,128)(2,1)S(1)}, bf16[2,4,72,128]{3,2,1,0:T(8,128)(2,1)S(1)}, u32[]{:S(2)}, u32[]{:S(2)}) collective-permute-start(bf16[2,4,72,128]{3,2,1,0:T(8,128)(2,1)S(1)} %dynamic-slice_convert_fusion.1), channel_id=1, source_target_pairs={{0,4},{1,5},{2,6},{3,7},{4,0},{5,1},{6,2},{7,3},{8,12},{9,13},{10,... | collective-permute-start | bytes 442376 | tf_op jit(solution)/shard_map/ppermute | solution.py:291
  98.4 7.4 %collective-permute-start.4 = (bf16[1,4,72,128]{3,2,1,0:T(8,128)(2,1)S(1)}, bf16[1,4,72,128]{3,2,1,0:T(8,128)(2,1)S(1)}, u32[]{:S(2)}, u32[]{:S(2)}) collective-permute-start(bf16[1,4,72,128]{3,2,1,0:T(8,128)(2,1)S(1)} %dynamic-slice_convert_fusion.2), channel_id=1, source_target_pairs={{0,14},{1,15},{2,12},{3,13},{4,10},{5,11},{6,8},{7,9},{8,6},{9,7},... | collective-permute-start | bytes 221192 | tf_op jit(solution)/shard_map/ppermute | solution.py:291
  105.8 6.2 %collective-permute-start.5 = (f32[2,72,128]{2,1,0:T(8,128)S(1)}, f32[2,72,128]{2,1,0:T(8,128)S(1)}, u32[]{:S(2)}, u32[]{:S(2)}) collective-permute-start(f32[2,72,128]{2,1,0:T(8,128)S(1)} %dynamic-slice_bitcast_fusion), channel_id=1, source_target_pairs={{0,16},{16,0},{32,48},{48,32},{64,80},{80,64},{96,112},{112,96},{1... | collective-permute-start | bytes 221192 | tf_op jit(solution)/shard_map/ppermute | solution.py:291
  112.0 6.4 %collective-permute-start.6 = (f32[1,72,128]{2,1,0:T(8,128)S(1)}, f32[1,72,128]{2,1,0:T(8,128)S(1)}, u32[]{:S(2)}, u32[]{:S(2)}) collective-permute-start(f32[1,72,128]{2,1,0:T(8,128)S(1)} %constant_dynamic-slice_fusion.2), channel_id=1, source_target_pairs={{0,48},{16,32},{32,16},{48,0},{64,112},{80,96},{96,80},{112,64},{1... | collective-permute-start | bytes 110600 | tf_op jit(solution)/shard_map/ppermute | solution.py:291
  119.5 20.2 %all-to-all-start.2 = ((bf16[12,72,128]{2,1,0:T(8,128)(2,1)}), bf16[12,72,128]{2,1,0:T(8,128)(2,1)S(1)}, u32[]{:S(2)}, u32[]{:S(2)}) async-start(bf16[12,72,128]{2,1,0:T(8,128)(2,1)} %broadcast_in_dim.44), calls=%async_computation.2 | async-start | bytes 442368 | tf_op jit(solution)/shard_map/all_to_all | solution.py:333
  130.1 7.0 %collective-permute-start.7 = (f32[8,64,128]{2,1,0:T(8,128)S(1)}, f32[8,64,128]{2,1,0:T(8,128)S(1)}, u32[]{:S(2)}, u32[]{:S(2)}) collective-permute-start(f32[8,64,128]{2,1,0:T(8,128)S(1)} %constant_dynamic-slice_fusion), channel_id=1, source_target_pairs={{0,1},{1,0},{2,3},{3,2},{4,5},{5,4},{6,7},{7,6},{8,9},{9,8},{10,11... | collective-permute-start | bytes 786440 | tf_op jit(solution)/shard_map/ppermute | solution.py:291
  139.7 11.3 %collective-permute-start.8 = (bf16[1,72,128]{2,1,0:T(8,128)(2,1)S(1)}, bf16[1,72,128]{2,1,0:T(8,128)(2,1)S(1)}, u32[]{:S(2)}, u32[]{:S(2)}) collective-permute-start(bf16[1,72,128]{2,1,0:T(8,128)(2,1)S(1)} %bitcast.49), channel_id=1, source_target_pairs={{0,48},{16,32},{32,16},{48,0},{64,112},{80,96},{96,80},{112,64},{1... | collective-permute-start | bytes 55304 | tf_op jit(solution)/shard_map/ppermute | solution.py:291
  144.3 16.0 %all-to-all-start.3 = ((f32[8,64,128]{2,1,0:T(8,128)}), f32[8,64,128]{2,1,0:T(8,128)S(1)}, u32[]{:S(2)}, u32[]{:S(2)}) async-start(f32[8,64,128]{2,1,0:T(8,128)} %dynamic-slice_add_fusion), calls=%async_computation.3 | async-start | bytes 524288 | tf_op jit(solution)/shard_map/all_to_all | solution.py:333
  151.0 4.7 %collective-permute-start.9 = (bf16[2,72,128]{2,1,0:T(8,128)(2,1)S(1)}, bf16[2,72,128]{2,1,0:T(8,128)(2,1)S(1)}, u32[]{:S(2)}, u32[]{:S(2)}) collective-permute-start(bf16[2,72,128]{2,1,0:T(8,128)(2,1)S(1)} %pad_maximum_fusion.2), channel_id=1, source_target_pairs={{0,16},{16,0},{32,48},{48,32},{64,80},{80,64},{96,112},{112,96},{1... | collective-permute-start | bytes 110600 | tf_op jit(solution)/shard_map/ppermute | solution.py:291
  177.6 11.6 %collective-permute-start.10 = (bf16[8,352,128]{2,1,0:T(8,128)(2,1)S(1)}, bf16[8,352,128]{2,1,0:T(8,128)(2,1)S(1)}, u32[]{:S(2)}, u32[]{:S(2)}) collective-permute-start(bf16[8,352,128]{2,1,0:T(8,128)(2,1)S(1)} %all_to_all.25.mine_ref), channel_id=1, source_target_pairs={{0,1},{1,0},{2,3},{3,2},{4,5},{5,4},{6,7},{7,6},{8,9},{9,8},{10,11... | collective-permute-start | bytes 2162696 | tf_op jit(solution)/shard_map/ppermute | solution.py:291

commit v5 on v4

--- a/solution.py
+++ b/solution.py
@@ -48,7 +48,7 @@
     )(side.reshape(1), lists, limits[None, :], table)
 
 
-def row_sum_kernel(order, slot_ref, value_ref, out_ref):
+def row_sum_kernel(slot_ref, value_ref, out_ref):
     n = out_ref.shape[0]
     iota = lax.broadcasted_iota(jnp.int32, (n, LANES), 0)
     total = jnp.zeros(out_ref.shape, f32)
@@ -59,15 +59,12 @@
         )
         values = value_ref[k * LANES : (k + 2) * LANES, :]
         total = total + jnp.dot(hot, values, preferred_element_type=f32)
-    blocks = len(order)
-    size = n // blocks
-    for b, place in enumerate(order):
-        out_ref[place * size : (place + 1) * size, :] = total[b * size : (b + 1) * size, :]
-
-
-def row_sum(slot_rows, values, n, order):
+    out_ref[...] = total
+
+
+def row_sum(slot_rows, values, n):
     return pl.pallas_call(
-        functools.partial(row_sum_kernel, order),
+        row_sum_kernel,
         out_shape=jax.ShapeDtypeStruct((n, values.shape[1]), f32),
         in_specs=[VMEM] * 2,
         out_specs=VMEM,
@@ -392,18 +389,16 @@
     part = halve(part, bf16, chip_steps[1:])[0]
     part = halve(part, f32, near_steps, "owner")[0].astype(bf16)
     part, returned = lax.optimization_barrier((part, returned))
-    order = [b % 2 * chips + b // 2 for b in range(readers)]
-    local_grad = row_sum(slot_rows, returned, rows, order)
+    local_grad = row_sum(slot_rows, returned, rows)
     block = local_grad.reshape(readers, rows // readers, width)
 
     far = n_peers // NEAR
     part = jnp.broadcast_to(part[None], (far,) + part.shape)
     part = exchange(part, "owner", [list(range(x, n_peers, NEAR)) for x in range(NEAR)])
     chunk = jnp.sum(part.astype(f32), axis=0, keepdims=True).astype(bf16)
-    block = halve(block, f32, [(1, (0,))])
     chunk, block = lax.optimization_barrier((chunk, block))
     same_core = [list(range(c, readers, 2)) for c in range(2)]
-    block = jnp.sum(exchange(block, "reader", same_core), axis=0)
+    block = jnp.sum(exchange(block, "reader"), axis=0)
     chunk = double(chunk, near_steps, "owner").reshape(-1, LANES)
     mine = jnp.concatenate([chunk, block.astype(bf16)], axis=0)
     mine = jnp.broadcast_to(mine[None], (chips,) + mine.shape)

time: 193 us -> 202 us (1.047)
  waiting for transfers between devices: 33.1 us -> 42.8 us
  starting transfers between devices: 91.3 us -> 82.8 us
  blocking collectives: 17.1 us -> 24.6 us
    ppermute x11 -> x10, starting transfers between devices: 51.1 us -> 37.4 us  [swap(): return lax.ppermute(shard, axis, pairs)]
    all_to_all x1, blocking collectives: 17.1 us -> 24.6 us  [exchange(): lax.all_to_all(blocks, axis, split_axis=0, concat_axis=0, tiled=True, axi...]
    all_to_all x4, waiting for transfers between devices: 13.8 us -> 21.2 us  [exchange(): lax.all_to_all(blocks, axis, split_axis=0, concat_axis=0, tiled=True, axi...]
    all_to_all x4, starting transfers between devices: 40.1 us -> 45.4 us  [exchange(): lax.all_to_all(blocks, axis, split_axis=0, concat_axis=0, tiled=True, axi...]
    ppermute x11 -> x10, waiting for transfers between devices: 19.3 us -> 21.6 us  [swap(): return lax.ppermute(shard, axis, pairs)]
  transfers between devices with their start and end apart: 15 -> 14, of which waited for: 14 -> 14; matrix products, arithmetic and copies ran while one was open for 7% -> 7% of each run, Pallas kernels for 9% -> 9%
where the time goes in v5:
time: 202 us; the launch traced here: 200 us
  starting transfers between devices  82.8 us (41%)
  waiting for transfers between devices  42.8 us (21%)
  Pallas kernels  26.5 us (13%)
  blocking collectives  24.6 us (12%)
  matrix products  12.1 us (6%)
  local copies, waits for them, and re-layouts  5.89 us (3%)
  other arithmetic  4.6 us (2%)
    all_to_all x4, starting transfers between devices, exchange(): lax.all_to_all(blocks, axis, split_axis=0, concat_axis=0, tiled=True, axi...  45.4 us
    ppermute x10, starting transfers between devices, swap(): return lax.ppermute(shard, axis, pairs)  37.4 us
    all_to_all x1, blocking collectives, exchange(): lax.all_to_all(blocks, axis, split_axis=0, concat_axis=0, tiled=True, axi...  24.6 us
    ppermute x10, waiting for transfers between devices, swap(): return lax.ppermute(shard, axis, pairs)  21.6 us
    all_to_all x4, waiting for transfers between devices, exchange(): lax.all_to_all(blocks, axis, split_axis=0, concat_axis=0, tiled=True, axi...  21.2 us
    pallas_call x1, Pallas kernels, count(): pl.pallas_call(count_kernel, grid=(n_bags // block,), out_shape=jax.Shape...  16.3 us
    dot_general x1, matrix products, on_device(): lax.dot_general(counted.astype(bf16), grad_both, (((0,), (0,)), ((), ()))...  6.52 us
    dot_general x1, matrix products, on_device(): pooled = jnp.dot(counted.astype(bf16), fetched, preferred_element_type=f32)  5.57 us
  transfers between devices with their start and end apart: 14, of which 14 were waited for; matrix products, arithmetic and copies ran while one was open for 7% of the time, Pallas kernels for 9%

profile of v5, /device:TPU:1, one launch (start us, length us, event | category | flops | bytes accessed | tf_op | source)
XLA Modules:
  0.0 200.4 jit_solution(1517301838070023963)
XLA Ops:
  3.1 2.8 %fetch.1 = bf16[3072,128]{1,0:T(8,128)(2,1)} custom-call(s32[1]{0:T(128)} %bitcast.side_ref.parity_ref, s32[48,128]{1,0:T(8,128)S(1)} %bitcast.38, s32[1,48]{1,0:T(1,128)S(1)} %bitcast.42, f32[1024,128]{1,0:T(8,128)S(1)} %copy-done), custom_call_target="tpu_custom_call" | custom-call | tf_op jit(solution)/shard_map/fetch/pallas_call | solution.py:41
  5.9 18.8 %all-to-all-start = ((bf16[48,64,128]{2,1,0:T(8,128)(2,1)}), bf16[48,64,128]{2,1,0:T(8,128)(2,1)S(1)}, u32[]{:S(2)}, u32[]{:S(2)}) async-start(bf16[48,64,128]{2,1,0:T(8,128)(2,1)} %bitcast.7), calls=%async_computation | async-start | bytes 1572864 | tf_op jit(solution)/shard_map/all_to_all | solution.py:330
  28.9 2.8 %collective-permute-start = (s32[90,128]{1,0:T(8,128)S(1)}, s32[90,128]{1,0:T(8,128)S(1)}, u32[]{:S(2)}, u32[]{:S(2)}) collective-permute-start(s32[90,128]{1,0:T(8,128)S(1)} %add_bitcast_fusion), channel_id=1, source_target_pairs={{0,1},{1,0},{2,3},{3,2},{4,5},{5,4},{6,7},{7,6},{8,9},{9,8},{10,11... | collective-permute-start | bytes 138248 | tf_op jit(solution)/shard_map/ppermute | solution.py:288
  33.1 16.3 %count.1 = f8e4m3fn[2048,3072]{1,0:T(32,128)(4,1)} custom-call(s32[2048,8]{1,0:T(8,128)S(1)} %pad_add_fusion.bag_ref, s32[2,1,3072]{2,1,0:T(1,128)S(1)} %broadcast_in_dim.40.place_ref), custom_call_target="tpu_custom_call" | custom-call | flops 100663296 | bytes 6291456 | tf_op jit(solution)/shard_map/count/pallas_call | solution.py:110
  49.4 7.0 %all-to-all-done = bf16[48,64,128]{2,1,0:T(8,128)(2,1)S(1)} async-done(((bf16[48,64,128]{2,1,0:T(8,128)(2,1)}), bf16[48,64,128]{2,1,0:T(8,128)(2,1)S(1)}, u32[]{:S(2)}, u32[]{:S(2)}) %all-to-all-start) | async-done | bytes 786464 | tf_op jit(solution)/shard_map/all_to_all | solution.py:330
  56.4 5.6 %fusion.2.here_ref = f32[2048,128]{1,0:T(8,128)S(1)} fusion(bf16[3072,128]{1,0:T(8,128)(2,1)S(1)} %bitcast.44, f8e4m3fn[2048,3072]{1,0:T(32,128)(4,1)} %count.1), kind=kOutput, calls=%fused_computation.2 | convolution fusion | flops 1616904192 | bytes 8126464 | tf_op jit(solution)/shard_map/dot_general | solution.py:370
  62.0 5.0 %collective-permute-start.1 = (f32[2048,128]{1,0:T(8,128)S(1)}, f32[2048,128]{1,0:T(8,128)S(1)}, u32[]{:S(2)}, u32[]{:S(2)}) collective-permute-start(f32[2048,128]{1,0:T(8,128)S(1)} %fusion.2.here_ref), channel_id=1, source_target_pairs={{0,1},{1,0},{2,3},{3,2},{4,5},{5,4},{6,7},{7,6},{8,9},{9,8},{10,11... | collective-permute-start | bytes 3145736 | tf_op jit(solution)/shard_map/ppermute | solution.py:288
  67.2 2.0 %collective-permute-done.1.came_ref = f32[2048,128]{1,0:T(8,128)S(1)} collective-permute-done((f32[2048,128]{1,0:T(8,128)S(1)}, f32[2048,128]{1,0:T(8,128)S(1)}, u32[]{:S(2)}, u32[]{:S(2)}) %collective-permute-start.1) | collective-permute-done | bytes 1048608 | tf_op jit(solution)/shard_map/ppermute | solution.py:288
  69.2 2.3 %top.1 = (f32[256,1]{1,0:T(8,128)S(1)}, f32[8,4,72,128]{3,2,1,0:T(8,128)S(1)}, bf16[2048,128]{1,0:T(8,128)(2,1)S(1)}) custom-call(s32[1]{0:T(128)} %bitcast.side_ref.parity_ref, f32[2048,128]{1,0:T(8,128)S(1)} %fusion.2.here_ref, f32[2048,128]{1,0:T(8,128)S(1)} %collective-permute-done.1.came_ref, bf16[512,1024]{1,0:T(8,128)(2,1)S(1)} %copy-done.2, ...), custom_call_target="tpu_custom_call" | custom-call | tf_op jit(solution)/shard_map/top/pallas_call | solution.py:195
  71.6 3.2 %collective-permute-start.2 = (bf16[4,4,72,128]{3,2,1,0:T(8,128)(2,1)S(1)}, bf16[4,4,72,128]{3,2,1,0:T(8,128)(2,1)S(1)}, u32[]{:S(2)}, u32[]{:S(2)}) collective-permute-start(bf16[4,4,72,128]{3,2,1,0:T(8,128)(2,1)S(1)} %dynamic-slice_convert_fusion), channel_id=1, source_target_pairs={{0,2},{1,3},{2,0},{3,1},{4,6},{5,7},{6,4},{7,5},{8,10},{9,11},{10,... | collective-permute-start | bytes 884744 | tf_op jit(solution)/shard_map/ppermute | solution.py:288
  74.9 6.5 %fusion.4 = bf16[3072,128]{1,0:T(8,128)(2,1)} fusion(bf16[2048,128]{1,0:T(8,128)(2,1)S(1)} %get-tuple-element.21, f8e4m3fn[2048,3072]{1,0:T(32,128)(4,1)} %count.1), kind=kOutput, calls=%fused_computation.4 | convolution fusion | flops 1617297408 | bytes 7602176 | tf_op jit(solution)/shard_map/dot_general | solution.py:382
  81.8 5.7 %all-to-all-start.1 = ((bf16[48,64,128]{2,1,0:T(8,128)(2,1)}), bf16[48,64,128]{2,1,0:T(8,128)(2,1)S(1)}, u32[]{:S(2)}, u32[]{:S(2)}) async-start(bf16[48,64,128]{2,1,0:T(8,128)(2,1)} %bitcast.15), calls=%async_computation.1 | async-start | bytes 1572864 | tf_op jit(solution)/shard_map/all_to_all | solution.py:330
  87.5 4.2 %collective-permute-start.3 = (bf16[2,4,72,128]{3,2,1,0:T(8,128)(2,1)S(1)}, bf16[2,4,72,128]{3,2,1,0:T(8,128)(2,1)S(1)}, u32[]{:S(2)}, u32[]{:S(2)}) collective-permute-start(bf16[2,4,72,128]{3,2,1,0:T(8,128)(2,1)S(1)} %dynamic-slice_convert_fusion.1), channel_id=1, source_target_pairs={{0,4},{1,5},{2,6},{3,7},{4,0},{5,1},{6,2},{7,3},{8,12},{9,13},{10,... | collective-permute-start | bytes 442376 | tf_op jit(solution)/shard_map/ppermute | solution.py:288
  91.8 6.4 %collective-permute-done.3 = bf16[2,4,72,128]{3,2,1,0:T(8,128)(2,1)S(1)} collective-permute-done((bf16[2,4,72,128]{3,2,1,0:T(8,128)(2,1)S(1)}, bf16[2,4,72,128]{3,2,1,0:T(8,128)(2,1)S(1)}, u32[]{:S(2)}, u32[]{:S(2)}) %collective-permute-start.3) | collective-permute-done | bytes 147488 | tf_op jit(solution)/shard_map/ppermute | solution.py:288
  98.2 5.4 %collective-permute-start.4 = (bf16[1,4,72,128]{3,2,1,0:T(8,128)(2,1)S(1)}, bf16[1,4,72,128]{3,2,1,0:T(8,128)(2,1)S(1)}, u32[]{:S(2)}, u32[]{:S(2)}) collective-permute-start(bf16[1,4,72,128]{3,2,1,0:T(8,128)(2,1)S(1)} %dynamic-slice_convert_fusion.2), channel_id=1, source_target_pairs={{0,14},{1,15},{2,12},{3,13},{4,10},{5,11},{6,8},{7,9},{8,6},{9,7},... | collective-permute-start | bytes 221192 | tf_op jit(solution)/shard_map/ppermute | solution.py:288
  103.6 2.0 collective-permute-done.4
  105.6 3.8 %collective-permute-start.5 = (f32[2,72,128]{2,1,0:T(8,128)S(1)}, f32[2,72,128]{2,1,0:T(8,128)S(1)}, u32[]{:S(2)}, u32[]{:S(2)}) collective-permute-start(f32[2,72,128]{2,1,0:T(8,128)S(1)} %dynamic-slice_bitcast_fusion), channel_id=1, source_target_pairs={{0,16},{16,0},{32,48},{48,32},{64,80},{80,64},{96,112},{112,96},{1... | collective-permute-start | bytes 221192 | tf_op jit(solution)/shard_map/ppermute | solution.py:288
  109.5 2.3 %collective-permute-done.5 = f32[2,72,128]{2,1,0:T(8,128)S(1)} collective-permute-done((f32[2,72,128]{2,1,0:T(8,128)S(1)}, f32[2,72,128]{2,1,0:T(8,128)S(1)}, u32[]{:S(2)}, u32[]{:S(2)}) %collective-permute-start.5) | collective-permute-done | bytes 73760 | tf_op jit(solution)/shard_map/ppermute | solution.py:288
  111.8 4.4 %collective-permute-start.6 = (f32[1,72,128]{2,1,0:T(8,128)S(1)}, f32[1,72,128]{2,1,0:T(8,128)S(1)}, u32[]{:S(2)}, u32[]{:S(2)}) collective-permute-start(f32[1,72,128]{2,1,0:T(8,128)S(1)} %constant_dynamic-slice_fusion.1), channel_id=1, source_target_pairs={{0,48},{16,32},{32,16},{48,0},{64,112},{80,96},{96,80},{112,64},{1... | collective-permute-start | bytes 110600 | tf_op jit(solution)/shard_map/ppermute | solution.py:288
  116.3 1.9 collective-permute-done.6
  119.3 8.8 %all-to-all-start.2 = ((bf16[12,72,128]{2,1,0:T(8,128)(2,1)}), bf16[12,72,128]{2,1,0:T(8,128)(2,1)S(1)}, u32[]{:S(2)}, u32[]{:S(2)}) async-start(bf16[12,72,128]{2,1,0:T(8,128)(2,1)} %broadcast_in_dim.44), calls=%async_computation.2 | async-start | bytes 442368 | tf_op jit(solution)/shard_map/all_to_all | solution.py:330
  129.4 2.6 %row_sum.1 = f32[1024,128]{1,0:T(8,128)} custom-call(s32[24,128]{1,0:T(8,128)S(1)} %compare_select_fusion.slot_ref, bf16[3072,128]{1,0:T(8,128)(2,1)S(1)} %bitcast.37), custom_call_target="tpu_custom_call" | custom-call | tf_op jit(solution)/shard_map/row_sum/pallas_call | solution.py:66
  131.9 7.6 %all-to-all-done.2 = bf16[12,72,128]{2,1,0:T(8,128)(2,1)S(1)} async-done(((bf16[12,72,128]{2,1,0:T(8,128)(2,1)}), bf16[12,72,128]{2,1,0:T(8,128)(2,1)S(1)}, u32[]{:S(2)}, u32[]{:S(2)}) %all-to-all-start.2) | async-done | bytes 221216 | tf_op jit(solution)/shard_map/all_to_all | solution.py:330
  139.6 12.1 %all-to-all-start.3 = ((f32[16,64,128]{2,1,0:T(8,128)}), f32[16,64,128]{2,1,0:T(8,128)S(1)}, u32[]{:S(2)}, u32[]{:S(2)}) async-start(f32[16,64,128]{2,1,0:T(8,128)} %bitcast.18), calls=%async_computation.3 | async-start | bytes 1048576 | tf_op jit(solution)/shard_map/all_to_all | solution.py:330
  151.7 4.1 %collective-permute-start.7 = (bf16[1,72,128]{2,1,0:T(8,128)(2,1)S(1)}, bf16[1,72,128]{2,1,0:T(8,128)(2,1)S(1)}, u32[]{:S(2)}, u32[]{:S(2)}) collective-permute-start(bf16[1,72,128]{2,1,0:T(8,128)(2,1)S(1)} %bitcast.47), channel_id=1, source_target_pairs={{0,48},{16,32},{32,16},{48,0},{64,112},{80,96},{96,80},{112,64},{1... | collective-permute-start | bytes 55304 | tf_op jit(solution)/shard_map/ppermute | solution.py:288
  155.8 1.9 collective-permute-done.7
  157.7 1.9 collective-permute-start.8
  159.7 3.1 %collective-permute-done.8 = bf16[2,72,128]{2,1,0:T(8,128)(2,1)S(1)} collective-permute-done((bf16[2,72,128]{2,1,0:T(8,128)(2,1)S(1)}, bf16[2,72,128]{2,1,0:T(8,128)(2,1)S(1)}, u32[]{:S(2)}, u32[]{:S(2)}) %collective-permute-start.8) | collective-permute-done | bytes 36896 | tf_op jit(solution)/shard_map/ppermute | solution.py:288
  162.8 6.2 %all-to-all-done.3 = f32[16,64,128]{2,1,0:T(8,128)S(1)} async-done(((f32[16,64,128]{2,1,0:T(8,128)}), f32[16,64,128]{2,1,0:T(8,128)S(1)}, u32[]{:S(2)}, u32[]{:S(2)}) %all-to-all-start.3) | async-done | bytes 524320 | tf_op jit(solution)/shard_map/all_to_all | solution.py:330
  169.2 24.6 %all_to_all.25.mine_ref = bf16[8,352,128]{2,1,0:T(8,128)(2,1)S(1)} all-to-all(bf16[8,352,128]{2,1,0:T(8,128)(2,1)S(1)} %broadcast_in_dim.46), channel_id=1, replica_groups={{0,2,4,6,8,10,12,14},{1,3,5,7,9,11,13,15},{16,18,20,22,24,26,28,30},{17..., dimensions={0} | all-to-all | bytes 1441792 | tf_op jit(solution)/shard_map/all_to_all | solution.py:330
  193.8 2.4 %collective-permute-start.9 = (bf16[8,352,128]{2,1,0:T(8,128)(2,1)S(1)}, bf16[8,352,128]{2,1,0:T(8,128)(2,1)S(1)}, u32[]{:S(2)}, u32[]{:S(2)}) collective-permute-start(bf16[8,352,128]{2,1,0:T(8,128)(2,1)S(1)} %all_to_all.25.mine_ref), channel_id=1, source_target_pairs={{0,1},{1,0},{2,3},{3,2},{4,5},{5,4},{6,7},{7,6},{8,9},{9,8},{10,11... | collective-permute-start | bytes 2162696 | tf_op jit(solution)/shard_map/ppermute | solution.py:288
  197.9 2.5 %update.1 = (f32[1024,128]{1,0:T(8,128)}, f32[8,128]{1,0:T(8,128)}, f32[1024,128]{1,0:T(8,128)}, f32[512,1024]{1,0:T(8,128)}, f32[8,128]{1,0:T(8,128)}) custom-call(s32[1]{0:T(128)} %bitcast.side_ref.parity_ref, bf16[8,352,128]{2,1,0:T(8,128)(2,1)S(1)} %all_to_all.25.mine_ref, bf16[8,352,128]{2,1,0:T(8,128)(2,1)S(1)} %collective-permute-done.9.other_ref, ...), custom_call_target="tpu_custom_call" | custom-call | tf_op jit(solution)/shard_map/update/pallas_call | solution.py:262
  (77 shorter events, 12.8 us)
Async XLA Ops:
  0.6 1.0 copy-start
  1.7 0.7 copy-start.3
  2.4 0.7 copy-start.7
  5.9 50.5 %all-to-all-start = ((bf16[48,64,128]{2,1,0:T(8,128)(2,1)}), bf16[48,64,128]{2,1,0:T(8,128)(2,1)S(1)}, u32[]{:S(2)}, u32[]{:S(2)}) async-start(bf16[48,64,128]{2,1,0:T(8,128)(2,1)} %bitcast.7), calls=%async_computation | async-start | bytes 1572864 | tf_op jit(solution)/shard_map/all_to_all | solution.py:330
  28.9 3.7 %collective-permute-start = (s32[90,128]{1,0:T(8,128)S(1)}, s32[90,128]{1,0:T(8,128)S(1)}, u32[]{:S(2)}, u32[]{:S(2)}) collective-permute-start(s32[90,128]{1,0:T(8,128)S(1)} %add_bitcast_fusion), channel_id=1, source_target_pairs={{0,1},{1,0},{2,3},{3,2},{4,5},{5,4},{6,7},{7,6},{8,9},{9,8},{10,11... | collective-permute-start | bytes 138248 | tf_op jit(solution)/shard_map/ppermute | solution.py:288
  56.4 10.6 %copy-start.10 = (bf16[1024]{0:T(1024)(128)(2,1)S(1)}, bf16[1024]{0:T(1024)(128)(2,1)}, u32[]{:S(2)}) copy-start(bf16[1024]{0:T(1024)(128)(2,1)} %param.21) | copy-start | bytes 6148
  56.4 10.6 %copy-start.9 = (s32[256]{0:T(256)S(1)}, s32[256]{0:T(256)}, u32[]{:S(2)}) copy-start(s32[256]{0:T(256)} %param.18) | copy-start | bytes 3076
  56.4 12.8 %copy-start.2 = (bf16[512,1024]{1,0:T(8,128)(2,1)S(1)}, bf16[512,1024]{1,0:T(8,128)(2,1)}, u32[]{:S(2)}) copy-start(bf16[512,1024]{1,0:T(8,128)(2,1)} %w1_ref.1) | copy-start | bytes 3145732
  56.4 12.8 %copy-start.6 = (f32[1024]{0:T(1024)S(1)}, f32[1024]{0:T(1024)}, u32[]{:S(2)}) copy-start(f32[1024]{0:T(1024)} %param.20) | copy-start | bytes 12292
  62.0 7.3 %collective-permute-start.1 = (f32[2048,128]{1,0:T(8,128)S(1)}, f32[2048,128]{1,0:T(8,128)S(1)}, u32[]{:S(2)}, u32[]{:S(2)}) collective-permute-start(f32[2048,128]{1,0:T(8,128)S(1)} %fusion.2.here_ref), channel_id=1, source_target_pairs={{0,1},{1,0},{2,3},{3,2},{4,5},{5,4},{6,7},{7,6},{8,9},{9,8},{10,11... | collective-permute-start | bytes 3145736 | tf_op jit(solution)/shard_map/ppermute | solution.py:288
  71.6 10.1 %collective-permute-start.2 = (bf16[4,4,72,128]{3,2,1,0:T(8,128)(2,1)S(1)}, bf16[4,4,72,128]{3,2,1,0:T(8,128)(2,1)S(1)}, u32[]{:S(2)}, u32[]{:S(2)}) collective-permute-start(bf16[4,4,72,128]{3,2,1,0:T(8,128)(2,1)S(1)} %dynamic-slice_convert_fusion), channel_id=1, source_target_pairs={{0,2},{1,3},{2,0},{3,1},{4,6},{5,7},{6,4},{7,5},{8,10},{9,11},{10,... | collective-permute-start | bytes 884744 | tf_op jit(solution)/shard_map/ppermute | solution.py:288
  74.8 53.3 %copy-start.8 = (s32[1,1,48]{2,1,0:T(1,128)S(1)}, s32[1,1,48]{2,1,0:T(1,128)}, u32[]{:S(2)}) copy-start(s32[1,1,48]{2,1,0:T(1,128)} %param.14) | copy-start | bytes 580
  74.9 54.0 %copy-start.4 = (s32[1,1,48,128]{3,2,1,0:T(8,128)S(1)}, s32[1,1,48,128]{3,2,1,0:T(8,128)}, u32[]{:S(2)}) copy-start(s32[1,1,48,128]{3,2,1,0:T(8,128)} %param.13) | copy-start | bytes 73732
  81.4 114.7 %copy-start.5 = (f32[1024]{0:T(1024)S(1)}, f32[1024]{0:T(1024)}, u32[]{:S(2)}) copy-start(f32[1024]{0:T(1024)} %param.12) | copy-start | bytes 12292
  81.4 116.5 %copy-start.1 = (f32[1024,128]{1,0:T(8,128)S(1)}, f32[1024,128]{1,0:T(8,128)}, u32[]{:S(2)}) copy-start(f32[1024,128]{1,0:T(8,128)} %table_ref.3) | copy-start | bytes 1572868
  81.8 36.8 %all-to-all-start.1 = ((bf16[48,64,128]{2,1,0:T(8,128)(2,1)}), bf16[48,64,128]{2,1,0:T(8,128)(2,1)S(1)}, u32[]{:S(2)}, u32[]{:S(2)}) async-start(bf16[48,64,128]{2,1,0:T(8,128)(2,1)} %bitcast.15), calls=%async_computation.1 | async-start | bytes 1572864 | tf_op jit(solution)/shard_map/all_to_all | solution.py:330
  87.5 10.6 %collective-permute-start.3 = (bf16[2,4,72,128]{3,2,1,0:T(8,128)(2,1)S(1)}, bf16[2,4,72,128]{3,2,1,0:T(8,128)(2,1)S(1)}, u32[]{:S(2)}, u32[]{:S(2)}) collective-permute-start(bf16[2,4,72,128]{3,2,1,0:T(8,128)(2,1)S(1)} %dynamic-slice_convert_fusion.1), channel_id=1, source_target_pairs={{0,4},{1,5},{2,6},{3,7},{4,0},{5,1},{6,2},{7,3},{8,12},{9,13},{10,... | collective-permute-start | bytes 442376 | tf_op jit(solution)/shard_map/ppermute | solution.py:288
  98.2 7.4 %collective-permute-start.4 = (bf16[1,4,72,128]{3,2,1,0:T(8,128)(2,1)S(1)}, bf16[1,4,72,128]{3,2,1,0:T(8,128)(2,1)S(1)}, u32[]{:S(2)}, u32[]{:S(2)}) collective-permute-start(bf16[1,4,72,128]{3,2,1,0:T(8,128)(2,1)S(1)} %dynamic-slice_convert_fusion.2), channel_id=1, source_target_pairs={{0,14},{1,15},{2,12},{3,13},{4,10},{5,11},{6,8},{7,9},{8,6},{9,7},... | collective-permute-start | bytes 221192 | tf_op jit(solution)/shard_map/ppermute | solution.py:288
  105.6 6.2 %collective-permute-start.5 = (f32[2,72,128]{2,1,0:T(8,128)S(1)}, f32[2,72,128]{2,1,0:T(8,128)S(1)}, u32[]{:S(2)}, u32[]{:S(2)}) collective-permute-start(f32[2,72,128]{2,1,0:T(8,128)S(1)} %dynamic-slice_bitcast_fusion), channel_id=1, source_target_pairs={{0,16},{16,0},{32,48},{48,32},{64,80},{80,64},{96,112},{112,96},{1... | collective-permute-start | bytes 221192 | tf_op jit(solution)/shard_map/ppermute | solution.py:288
  111.8 6.4 %collective-permute-start.6 = (f32[1,72,128]{2,1,0:T(8,128)S(1)}, f32[1,72,128]{2,1,0:T(8,128)S(1)}, u32[]{:S(2)}, u32[]{:S(2)}) collective-permute-start(f32[1,72,128]{2,1,0:T(8,128)S(1)} %constant_dynamic-slice_fusion.1), channel_id=1, source_target_pairs={{0,48},{16,32},{32,16},{48,0},{64,112},{80,96},{96,80},{112,64},{1... | collective-permute-start | bytes 110600 | tf_op jit(solution)/shard_map/ppermute | solution.py:288
  119.3 20.2 %all-to-all-start.2 = ((bf16[12,72,128]{2,1,0:T(8,128)(2,1)}), bf16[12,72,128]{2,1,0:T(8,128)(2,1)S(1)}, u32[]{:S(2)}, u32[]{:S(2)}) async-start(bf16[12,72,128]{2,1,0:T(8,128)(2,1)} %broadcast_in_dim.44), calls=%async_computation.2 | async-start | bytes 442368 | tf_op jit(solution)/shard_map/all_to_all | solution.py:330
  139.6 29.4 %all-to-all-start.3 = ((f32[16,64,128]{2,1,0:T(8,128)}), f32[16,64,128]{2,1,0:T(8,128)S(1)}, u32[]{:S(2)}, u32[]{:S(2)}) async-start(f32[16,64,128]{2,1,0:T(8,128)} %bitcast.18), calls=%async_computation.3 | async-start | bytes 1048576 | tf_op jit(solution)/shard_map/all_to_all | solution.py:330
  151.7 6.0 %collective-permute-start.7 = (bf16[1,72,128]{2,1,0:T(8,128)(2,1)S(1)}, bf16[1,72,128]{2,1,0:T(8,128)(2,1)S(1)}, u32[]{:S(2)}, u32[]{:S(2)}) collective-permute-start(bf16[1,72,128]{2,1,0:T(8,128)(2,1)S(1)} %bitcast.47), channel_id=1, source_target_pairs={{0,48},{16,32},{32,16},{48,0},{64,112},{80,96},{96,80},{112,64},{1... | collective-permute-start | bytes 55304 | tf_op jit(solution)/shard_map/ppermute | solution.py:288
  157.7 5.0 %collective-permute-start.8 = (bf16[2,72,128]{2,1,0:T(8,128)(2,1)S(1)}, bf16[2,72,128]{2,1,0:T(8,128)(2,1)S(1)}, u32[]{:S(2)}, u32[]{:S(2)}) collective-permute-start(bf16[2,72,128]{2,1,0:T(8,128)(2,1)S(1)} %pad_maximum_fusion.2), channel_id=1, source_target_pairs={{0,16},{16,0},{32,48},{48,32},{64,80},{80,64},{96,112},{112,96},{1... | collective-permute-start | bytes 110600 | tf_op jit(solution)/shard_map/ppermute | solution.py:288
  193.8 4.2 %collective-permute-start.9 = (bf16[8,352,128]{2,1,0:T(8,128)(2,1)S(1)}, bf16[8,352,128]{2,1,0:T(8,128)(2,1)S(1)}, u32[]{:S(2)}, u32[]{:S(2)}) collective-permute-start(bf16[8,352,128]{2,1,0:T(8,128)(2,1)S(1)} %all_to_all.25.mine_ref), channel_id=1, source_target_pairs={{0,1},{1,0},{2,3},{3,2},{4,5},{5,4},{6,7},{7,6},{8,9},{9,8},{10,11... | collective-permute-start | bytes 2162696 | tf_op jit(solution)/shard_map/ppermute | solution.py:288

commit v6 on v4

--- a/solution.py
+++ b/solution.py
@@ -16,15 +16,23 @@
 PARAMS = pltpu.CompilerParams(vmem_limit_bytes=48 * 1024 * 1024)
 
 
-def fetch_kernel(side_ref, list_ref, limit_ref, table_ref, out_ref):
-    table = table_ref[...].astype(bf16)
+def fetch_kernel(
+    side_ref, list_hbm, limit_ref, table_hbm, out_ref, list_ref, table_ref, list_sem, table_sem
+):
+    list_copy = pltpu.make_async_copy(list_hbm, list_ref, list_sem)
+    table_copy = pltpu.make_async_copy(table_hbm, table_ref, table_sem)
+    list_copy.start()
+    table_copy.start()
     peers = list_ref.shape[0]
     half = list_ref.shape[1] // 2
+    list_copy.wait()
     lists = list_ref[...].T
     side = side_ref[0]
     lists = jnp.where(side == 0, lists[:half], lists[half:])
     slots = lax.broadcasted_iota(jnp.int32, (half, peers), 0) + side * half
     lists = jnp.where(slots < limit_ref[...], lists, -1)
+    table_copy.wait()
+    table = table_ref[...].astype(bf16)
     rows = lax.broadcasted_iota(jnp.int32, (half, table.shape[0]), 1)
     for p in range(0, peers, 2):
         hot = jnp.concatenate(
@@ -38,11 +46,18 @@
 def fetch(side, lists, limits, table):
     slots = lists.size // 2
     smem = pl.BlockSpec(memory_space=pltpu.SMEM)
+    anywhere = pl.BlockSpec(memory_space=pl.ANY)
     return pl.pallas_call(
         fetch_kernel,
         out_shape=jax.ShapeDtypeStruct((slots, table.shape[1]), bf16),
-        in_specs=[smem] + [VMEM] * 3,
+        in_specs=[smem, anywhere, VMEM, anywhere],
         out_specs=VMEM,
+        scratch_shapes=[
+            pltpu.VMEM(lists.shape, lists.dtype),
+            pltpu.VMEM(table.shape, table.dtype),
+            pltpu.SemaphoreType.DMA(()),
+            pltpu.SemaphoreType.DMA(()),
+        ],
         compiler_params=PARAMS,
         name="fetch",
     )(side.reshape(1), lists, limits[None, :], table)

time: 193 us -> 193 us (level)
  no operation moved by 1% of the time
where the time goes in v6:
time: 193 us; the launch traced here: 192 us
  starting transfers between devices  91.3 us (47%)
  waiting for transfers between devices  33.1 us (17%)
  Pallas kernels  26 us (13%)
  blocking collectives  17.1 us (9%)
  matrix products  12.1 us (6%)
  local copies, waits for them, and re-layouts  5.91 us (3%)
  other arithmetic  5.32 us (3%)
    ppermute x11, starting transfers between devices, swap(): return lax.ppermute(shard, axis, pairs)  51.1 us
    all_to_all x4, starting transfers between devices, exchange(): lax.all_to_all(blocks, axis, split_axis=0, concat_axis=0, tiled=True, axi...  40.2 us
    ppermute x11, waiting for transfers between devices, swap(): return lax.ppermute(shard, axis, pairs)  19.3 us
    all_to_all x1, blocking collectives, exchange(): lax.all_to_all(blocks, axis, split_axis=0, concat_axis=0, tiled=True, axi...  17.1 us
    pallas_call x1, Pallas kernels, count(): pl.pallas_call(count_kernel, grid=(n_bags // block,), out_shape=jax.Shape...  16.3 us
    all_to_all x4, waiting for transfers between devices, exchange(): lax.all_to_all(blocks, axis, split_axis=0, concat_axis=0, tiled=True, axi...  13.8 us
    dot_general x1, matrix products, on_device(): lax.dot_general(counted.astype(bf16), grad_both, (((0,), (0,)), ((), ()))...  6.52 us
    dot_general x1, matrix products, on_device(): pooled = jnp.dot(counted.astype(bf16), fetched, preferred_element_type=f32)  5.57 us
  transfers between devices with their start and end apart: 15, of which 14 were waited for; matrix products, arithmetic and copies ran while one was open for 7% of the time, Pallas kernels for 9%

profile of v6, /device:TPU:1, one launch (start us, length us, event | category | flops | bytes accessed | tf_op | source)
XLA Modules:
  0.0 192.0 jit_solution(11250925477350851253)
XLA Ops:
  3.1 3.1 %fetch.1 = bf16[3072,128]{1,0:T(8,128)(2,1)} custom-call(s32[1]{0:T(128)} %bitcast.side_ref.parity_ref, s32[48,128]{1,0:T(8,128)S(1)} %bitcast.40, s32[1,48]{1,0:T(1,128)S(1)} %bitcast.44, f32[1024,128]{1,0:T(8,128)S(1)} %copy-done), custom_call_target="tpu_custom_call" | custom-call | tf_op jit(solution)/shard_map/fetch/pallas_call | solution.py:50
  6.2 18.8 %all-to-all-start = ((bf16[48,64,128]{2,1,0:T(8,128)(2,1)}), bf16[48,64,128]{2,1,0:T(8,128)(2,1)S(1)}, u32[]{:S(2)}, u32[]{:S(2)}) async-start(bf16[48,64,128]{2,1,0:T(8,128)(2,1)} %bitcast.7), calls=%async_computation | async-start | bytes 1572864 | tf_op jit(solution)/shard_map/all_to_all | solution.py:348
  29.2 2.9 %collective-permute-start = (s32[90,128]{1,0:T(8,128)S(1)}, s32[90,128]{1,0:T(8,128)S(1)}, u32[]{:S(2)}, u32[]{:S(2)}) collective-permute-start(s32[90,128]{1,0:T(8,128)S(1)} %add_bitcast_fusion), channel_id=1, source_target_pairs={{0,1},{1,0},{2,3},{3,2},{4,5},{5,4},{6,7},{7,6},{8,9},{9,8},{10,11... | collective-permute-start | bytes 138248 | tf_op jit(solution)/shard_map/ppermute | solution.py:306
  33.4 16.3 %count.1 = f8e4m3fn[2048,3072]{1,0:T(32,128)(4,1)} custom-call(s32[2048,8]{1,0:T(8,128)S(1)} %pad_add_fusion.bag_ref, s32[2,1,3072]{2,1,0:T(1,128)S(1)} %broadcast_in_dim.40.place_ref), custom_call_target="tpu_custom_call" | custom-call | flops 100663296 | bytes 6291456 | tf_op jit(solution)/shard_map/count/pallas_call | solution.py:128
  49.7 7.0 %all-to-all-done = bf16[48,64,128]{2,1,0:T(8,128)(2,1)S(1)} async-done(((bf16[48,64,128]{2,1,0:T(8,128)(2,1)}), bf16[48,64,128]{2,1,0:T(8,128)(2,1)S(1)}, u32[]{:S(2)}, u32[]{:S(2)}) %all-to-all-start) | async-done | bytes 786464 | tf_op jit(solution)/shard_map/all_to_all | solution.py:348
  56.7 5.6 %fusion.2.here_ref = f32[2048,128]{1,0:T(8,128)S(1)} fusion(bf16[3072,128]{1,0:T(8,128)(2,1)S(1)} %bitcast.46, f8e4m3fn[2048,3072]{1,0:T(32,128)(4,1)} %count.1), kind=kOutput, calls=%fused_computation.2 | convolution fusion | flops 1616904192 | bytes 8126464 | tf_op jit(solution)/shard_map/dot_general | solution.py:388
  62.3 5.0 %collective-permute-start.1 = (f32[2048,128]{1,0:T(8,128)S(1)}, f32[2048,128]{1,0:T(8,128)S(1)}, u32[]{:S(2)}, u32[]{:S(2)}) collective-permute-start(f32[2048,128]{1,0:T(8,128)S(1)} %fusion.2.here_ref), channel_id=1, source_target_pairs={{0,1},{1,0},{2,3},{3,2},{4,5},{5,4},{6,7},{7,6},{8,9},{9,8},{10,11... | collective-permute-start | bytes 3145736 | tf_op jit(solution)/shard_map/ppermute | solution.py:306
  67.5 2.0 %collective-permute-done.1.came_ref = f32[2048,128]{1,0:T(8,128)S(1)} collective-permute-done((f32[2048,128]{1,0:T(8,128)S(1)}, f32[2048,128]{1,0:T(8,128)S(1)}, u32[]{:S(2)}, u32[]{:S(2)}) %collective-permute-start.1) | collective-permute-done | bytes 1048608 | tf_op jit(solution)/shard_map/ppermute | solution.py:306
  69.5 2.3 %top.1 = (f32[256,1]{1,0:T(8,128)S(1)}, f32[8,4,72,128]{3,2,1,0:T(8,128)S(1)}, bf16[2048,128]{1,0:T(8,128)(2,1)S(1)}) custom-call(s32[1]{0:T(128)} %bitcast.side_ref.parity_ref, f32[2048,128]{1,0:T(8,128)S(1)} %fusion.2.here_ref, f32[2048,128]{1,0:T(8,128)S(1)} %collective-permute-done.1.came_ref, bf16[512,1024]{1,0:T(8,128)(2,1)S(1)} %copy-done.2, ...), custom_call_target="tpu_custom_call" | custom-call | tf_op jit(solution)/shard_map/top/pallas_call | solution.py:213
  71.9 3.2 %collective-permute-start.2 = (bf16[4,4,72,128]{3,2,1,0:T(8,128)(2,1)S(1)}, bf16[4,4,72,128]{3,2,1,0:T(8,128)(2,1)S(1)}, u32[]{:S(2)}, u32[]{:S(2)}) collective-permute-start(bf16[4,4,72,128]{3,2,1,0:T(8,128)(2,1)S(1)} %dynamic-slice_convert_fusion), channel_id=1, source_target_pairs={{0,2},{1,3},{2,0},{3,1},{4,6},{5,7},{6,4},{7,5},{8,10},{9,11},{10,... | collective-permute-start | bytes 884744 | tf_op jit(solution)/shard_map/ppermute | solution.py:306
  75.1 6.5 %fusion.4 = bf16[3072,128]{1,0:T(8,128)(2,1)} fusion(bf16[2048,128]{1,0:T(8,128)(2,1)S(1)} %get-tuple-element.21, f8e4m3fn[2048,3072]{1,0:T(32,128)(4,1)} %count.1), kind=kOutput, calls=%fused_computation.4 | convolution fusion | flops 1617297408 | bytes 7602176 | tf_op jit(solution)/shard_map/dot_general | solution.py:400
  82.1 5.8 %all-to-all-start.1 = ((bf16[48,64,128]{2,1,0:T(8,128)(2,1)}), bf16[48,64,128]{2,1,0:T(8,128)(2,1)S(1)}, u32[]{:S(2)}, u32[]{:S(2)}) async-start(bf16[48,64,128]{2,1,0:T(8,128)(2,1)} %bitcast.15), calls=%async_computation.1 | async-start | bytes 1572864 | tf_op jit(solution)/shard_map/all_to_all | solution.py:348
  87.9 4.2 %collective-permute-start.3 = (bf16[2,4,72,128]{3,2,1,0:T(8,128)(2,1)S(1)}, bf16[2,4,72,128]{3,2,1,0:T(8,128)(2,1)S(1)}, u32[]{:S(2)}, u32[]{:S(2)}) collective-permute-start(bf16[2,4,72,128]{3,2,1,0:T(8,128)(2,1)S(1)} %dynamic-slice_convert_fusion.1), channel_id=1, source_target_pairs={{0,4},{1,5},{2,6},{3,7},{4,0},{5,1},{6,2},{7,3},{8,12},{9,13},{10,... | collective-permute-start | bytes 442376 | tf_op jit(solution)/shard_map/ppermute | solution.py:306
  92.9 5.7 %collective-permute-done.3 = bf16[2,4,72,128]{3,2,1,0:T(8,128)(2,1)S(1)} collective-permute-done((bf16[2,4,72,128]{3,2,1,0:T(8,128)(2,1)S(1)}, bf16[2,4,72,128]{3,2,1,0:T(8,128)(2,1)S(1)}, u32[]{:S(2)}, u32[]{:S(2)}) %collective-permute-start.3) | collective-permute-done | bytes 147488 | tf_op jit(solution)/shard_map/ppermute | solution.py:306
  98.6 5.3 %collective-permute-start.4 = (bf16[1,4,72,128]{3,2,1,0:T(8,128)(2,1)S(1)}, bf16[1,4,72,128]{3,2,1,0:T(8,128)(2,1)S(1)}, u32[]{:S(2)}, u32[]{:S(2)}) collective-permute-start(bf16[1,4,72,128]{3,2,1,0:T(8,128)(2,1)S(1)} %dynamic-slice_convert_fusion.2), channel_id=1, source_target_pairs={{0,14},{1,15},{2,12},{3,13},{4,10},{5,11},{6,8},{7,9},{8,6},{9,7},... | collective-permute-start | bytes 221192 | tf_op jit(solution)/shard_map/ppermute | solution.py:306
  104.1 1.9 collective-permute-done.4
  106.0 3.8 %collective-permute-start.5 = (f32[2,72,128]{2,1,0:T(8,128)S(1)}, f32[2,72,128]{2,1,0:T(8,128)S(1)}, u32[]{:S(2)}, u32[]{:S(2)}) collective-permute-start(f32[2,72,128]{2,1,0:T(8,128)S(1)} %dynamic-slice_bitcast_fusion), channel_id=1, source_target_pairs={{0,16},{16,0},{32,48},{48,32},{64,80},{80,64},{96,112},{112,96},{1... | collective-permute-start | bytes 221192 | tf_op jit(solution)/shard_map/ppermute | solution.py:306
  110.2 2.0 %collective-permute-done.5 = f32[2,72,128]{2,1,0:T(8,128)S(1)} collective-permute-done((f32[2,72,128]{2,1,0:T(8,128)S(1)}, f32[2,72,128]{2,1,0:T(8,128)S(1)}, u32[]{:S(2)}, u32[]{:S(2)}) %collective-permute-start.5) | collective-permute-done | bytes 73760 | tf_op jit(solution)/shard_map/ppermute | solution.py:306
  112.2 4.5 %collective-permute-start.6 = (f32[1,72,128]{2,1,0:T(8,128)S(1)}, f32[1,72,128]{2,1,0:T(8,128)S(1)}, u32[]{:S(2)}, u32[]{:S(2)}) collective-permute-start(f32[1,72,128]{2,1,0:T(8,128)S(1)} %constant_dynamic-slice_fusion.2), channel_id=1, source_target_pairs={{0,48},{16,32},{32,16},{48,0},{64,112},{80,96},{96,80},{112,64},{1... | collective-permute-start | bytes 110600 | tf_op jit(solution)/shard_map/ppermute | solution.py:306
  116.7 1.9 collective-permute-done.6
  119.7 8.8 %all-to-all-start.2 = ((bf16[12,72,128]{2,1,0:T(8,128)(2,1)}), bf16[12,72,128]{2,1,0:T(8,128)(2,1)S(1)}, u32[]{:S(2)}, u32[]{:S(2)}) async-start(bf16[12,72,128]{2,1,0:T(8,128)(2,1)} %broadcast_in_dim.44), calls=%async_computation.2 | async-start | bytes 442368 | tf_op jit(solution)/shard_map/all_to_all | solution.py:348
  128.5 1.8 row_sum.1
  130.4 5.9 %collective-permute-start.7 = (f32[8,64,128]{2,1,0:T(8,128)S(1)}, f32[8,64,128]{2,1,0:T(8,128)S(1)}, u32[]{:S(2)}, u32[]{:S(2)}) collective-permute-start(f32[8,64,128]{2,1,0:T(8,128)S(1)} %constant_dynamic-slice_fusion), channel_id=1, source_target_pairs={{0,1},{1,0},{2,3},{3,2},{4,5},{5,4},{6,7},{7,6},{8,9},{9,8},{10,11... | collective-permute-start | bytes 786440 | tf_op jit(solution)/shard_map/ppermute | solution.py:306
  138.1 1.8 all-to-all-done.2
  140.0 4.6 %collective-permute-start.8 = (bf16[1,72,128]{2,1,0:T(8,128)(2,1)S(1)}, bf16[1,72,128]{2,1,0:T(8,128)(2,1)S(1)}, u32[]{:S(2)}, u32[]{:S(2)}) collective-permute-start(bf16[1,72,128]{2,1,0:T(8,128)(2,1)S(1)} %bitcast.49), channel_id=1, source_target_pairs={{0,48},{16,32},{32,16},{48,0},{64,112},{80,96},{96,80},{112,64},{1... | collective-permute-start | bytes 55304 | tf_op jit(solution)/shard_map/ppermute | solution.py:306
  144.6 6.7 %all-to-all-start.3 = ((f32[8,64,128]{2,1,0:T(8,128)}), f32[8,64,128]{2,1,0:T(8,128)S(1)}, u32[]{:S(2)}, u32[]{:S(2)}) async-start(f32[8,64,128]{2,1,0:T(8,128)} %dynamic-slice_add_fusion), calls=%async_computation.3 | async-start | bytes 524288 | tf_op jit(solution)/shard_map/all_to_all | solution.py:348
  151.3 1.9 %collective-permute-start.9 = (bf16[2,72,128]{2,1,0:T(8,128)(2,1)S(1)}, bf16[2,72,128]{2,1,0:T(8,128)(2,1)S(1)}, u32[]{:S(2)}, u32[]{:S(2)}) collective-permute-start(bf16[2,72,128]{2,1,0:T(8,128)(2,1)S(1)} %pad_maximum_fusion.2), channel_id=1, source_target_pairs={{0,16},{16,0},{32,48},{48,32},{64,80},{80,64},{96,112},{112,96},{1... | collective-permute-start | bytes 110600 | tf_op jit(solution)/shard_map/ppermute | solution.py:306
  153.3 2.8 %collective-permute-done.9 = bf16[2,72,128]{2,1,0:T(8,128)(2,1)S(1)} collective-permute-done((bf16[2,72,128]{2,1,0:T(8,128)(2,1)S(1)}, bf16[2,72,128]{2,1,0:T(8,128)(2,1)S(1)}, u32[]{:S(2)}, u32[]{:S(2)}) %collective-permute-start.9) | collective-permute-done | bytes 36896 | tf_op jit(solution)/shard_map/ppermute | solution.py:306
  156.1 4.6 %all-to-all-done.3 = f32[8,64,128]{2,1,0:T(8,128)S(1)} async-done(((f32[8,64,128]{2,1,0:T(8,128)}), f32[8,64,128]{2,1,0:T(8,128)S(1)}, u32[]{:S(2)}, u32[]{:S(2)}) %all-to-all-start.3) | async-done | bytes 262176 | tf_op jit(solution)/shard_map/all_to_all | solution.py:348
  160.8 17.1 %all_to_all.25.mine_ref = bf16[8,352,128]{2,1,0:T(8,128)(2,1)S(1)} all-to-all(bf16[8,352,128]{2,1,0:T(8,128)(2,1)S(1)} %broadcast_in_dim.46), channel_id=1, replica_groups={{0,2,4,6,8,10,12,14},{1,3,5,7,9,11,13,15},{16,18,20,22,24,26,28,30},{17..., dimensions={0} | all-to-all | bytes 1441792 | tf_op jit(solution)/shard_map/all_to_all | solution.py:348
  177.9 9.8 %collective-permute-start.10 = (bf16[8,352,128]{2,1,0:T(8,128)(2,1)S(1)}, bf16[8,352,128]{2,1,0:T(8,128)(2,1)S(1)}, u32[]{:S(2)}, u32[]{:S(2)}) collective-permute-start(bf16[8,352,128]{2,1,0:T(8,128)(2,1)S(1)} %all_to_all.25.mine_ref), channel_id=1, source_target_pairs={{0,1},{1,0},{2,3},{3,2},{4,5},{5,4},{6,7},{7,6},{8,9},{9,8},{10,11... | collective-permute-start | bytes 2162696 | tf_op jit(solution)/shard_map/ppermute | solution.py:306
  189.5 2.5 %update.1 = (f32[1024,128]{1,0:T(8,128)}, f32[8,128]{1,0:T(8,128)}, f32[1024,128]{1,0:T(8,128)}, f32[512,1024]{1,0:T(8,128)}, f32[8,128]{1,0:T(8,128)}) custom-call(s32[1]{0:T(128)} %bitcast.side_ref.parity_ref, bf16[8,352,128]{2,1,0:T(8,128)(2,1)S(1)} %all_to_all.25.mine_ref, bf16[8,352,128]{2,1,0:T(8,128)(2,1)S(1)} %collective-permute-done.10.other_ref, ...), custom_call_target="tpu_custom_call" | custom-call | tf_op jit(solution)/shard_map/update/pallas_call | solution.py:280
  (81 shorter events, 14.8 us)
Async XLA Ops:
  0.6 1.0 copy-start
  1.7 0.7 copy-start.3
  2.4 0.7 copy-start.7
  6.2 50.5 %all-to-all-start = ((bf16[48,64,128]{2,1,0:T(8,128)(2,1)}), bf16[48,64,128]{2,1,0:T(8,128)(2,1)S(1)}, u32[]{:S(2)}, u32[]{:S(2)}) async-start(bf16[48,64,128]{2,1,0:T(8,128)(2,1)} %bitcast.7), calls=%async_computation | async-start | bytes 1572864 | tf_op jit(solution)/shard_map/all_to_all | solution.py:348
  29.2 3.7 %collective-permute-start = (s32[90,128]{1,0:T(8,128)S(1)}, s32[90,128]{1,0:T(8,128)S(1)}, u32[]{:S(2)}, u32[]{:S(2)}) collective-permute-start(s32[90,128]{1,0:T(8,128)S(1)} %add_bitcast_fusion), channel_id=1, source_target_pairs={{0,1},{1,0},{2,3},{3,2},{4,5},{5,4},{6,7},{7,6},{8,9},{9,8},{10,11... | collective-permute-start | bytes 138248 | tf_op jit(solution)/shard_map/ppermute | solution.py:306
  56.7 10.6 %copy-start.10 = (bf16[1024]{0:T(1024)(128)(2,1)S(1)}, bf16[1024]{0:T(1024)(128)(2,1)}, u32[]{:S(2)}) copy-start(bf16[1024]{0:T(1024)(128)(2,1)} %param.21) | copy-start | bytes 6148
  56.7 10.6 %copy-start.9 = (s32[256]{0:T(256)S(1)}, s32[256]{0:T(256)}, u32[]{:S(2)}) copy-start(s32[256]{0:T(256)} %param.18) | copy-start | bytes 3076
  56.7 12.8 %copy-start.2 = (bf16[512,1024]{1,0:T(8,128)(2,1)S(1)}, bf16[512,1024]{1,0:T(8,128)(2,1)}, u32[]{:S(2)}) copy-start(bf16[512,1024]{1,0:T(8,128)(2,1)} %w1_ref.1) | copy-start | bytes 3145732
  56.7 12.8 %copy-start.6 = (f32[1024]{0:T(1024)S(1)}, f32[1024]{0:T(1024)}, u32[]{:S(2)}) copy-start(f32[1024]{0:T(1024)} %param.20) | copy-start | bytes 12292
  62.3 7.3 %collective-permute-start.1 = (f32[2048,128]{1,0:T(8,128)S(1)}, f32[2048,128]{1,0:T(8,128)S(1)}, u32[]{:S(2)}, u32[]{:S(2)}) collective-permute-start(f32[2048,128]{1,0:T(8,128)S(1)} %fusion.2.here_ref), channel_id=1, source_target_pairs={{0,1},{1,0},{2,3},{3,2},{4,5},{5,4},{6,7},{7,6},{8,9},{9,8},{10,11... | collective-permute-start | bytes 3145736 | tf_op jit(solution)/shard_map/ppermute | solution.py:306
  71.9 10.1 %collective-permute-start.2 = (bf16[4,4,72,128]{3,2,1,0:T(8,128)(2,1)S(1)}, bf16[4,4,72,128]{3,2,1,0:T(8,128)(2,1)S(1)}, u32[]{:S(2)}, u32[]{:S(2)}) collective-permute-start(bf16[4,4,72,128]{3,2,1,0:T(8,128)(2,1)S(1)} %dynamic-slice_convert_fusion), channel_id=1, source_target_pairs={{0,2},{1,3},{2,0},{3,1},{4,6},{5,7},{6,4},{7,5},{8,10},{9,11},{10,... | collective-permute-start | bytes 884744 | tf_op jit(solution)/shard_map/ppermute | solution.py:306
  75.1 17.1 %copy-start.8 = (s32[1,1,48]{2,1,0:T(1,128)S(1)}, s32[1,1,48]{2,1,0:T(1,128)}, u32[]{:S(2)}) copy-start(s32[1,1,48]{2,1,0:T(1,128)} %param.14) | copy-start | bytes 580
  75.1 28.9 %copy-start.4 = (s32[1,1,48,128]{3,2,1,0:T(8,128)S(1)}, s32[1,1,48,128]{3,2,1,0:T(8,128)}, u32[]{:S(2)}) copy-start(s32[1,1,48,128]{3,2,1,0:T(8,128)} %param.13) | copy-start | bytes 73732
  81.6 106.1 %copy-start.5 = (f32[1024]{0:T(1024)S(1)}, f32[1024]{0:T(1024)}, u32[]{:S(2)}) copy-start(f32[1024]{0:T(1024)} %param.12) | copy-start | bytes 12292
  82.0 107.5 %copy-start.1 = (f32[1024,128]{1,0:T(8,128)S(1)}, f32[1024,128]{1,0:T(8,128)}, u32[]{:S(2)}) copy-start(f32[1024,128]{1,0:T(8,128)} %table_ref.1) | copy-start | bytes 1572868
  82.1 37.0 %all-to-all-start.1 = ((bf16[48,64,128]{2,1,0:T(8,128)(2,1)}), bf16[48,64,128]{2,1,0:T(8,128)(2,1)S(1)}, u32[]{:S(2)}, u32[]{:S(2)}) async-start(bf16[48,64,128]{2,1,0:T(8,128)(2,1)} %bitcast.15), calls=%async_computation.1 | async-start | bytes 1572864 | tf_op jit(solution)/shard_map/all_to_all | solution.py:348
  87.9 10.6 %collective-permute-start.3 = (bf16[2,4,72,128]{3,2,1,0:T(8,128)(2,1)S(1)}, bf16[2,4,72,128]{3,2,1,0:T(8,128)(2,1)S(1)}, u32[]{:S(2)}, u32[]{:S(2)}) collective-permute-start(bf16[2,4,72,128]{3,2,1,0:T(8,128)(2,1)S(1)} %dynamic-slice_convert_fusion.1), channel_id=1, source_target_pairs={{0,4},{1,5},{2,6},{3,7},{4,0},{5,1},{6,2},{7,3},{8,12},{9,13},{10,... | collective-permute-start | bytes 442376 | tf_op jit(solution)/shard_map/ppermute | solution.py:306
  98.6 7.4 %collective-permute-start.4 = (bf16[1,4,72,128]{3,2,1,0:T(8,128)(2,1)S(1)}, bf16[1,4,72,128]{3,2,1,0:T(8,128)(2,1)S(1)}, u32[]{:S(2)}, u32[]{:S(2)}) collective-permute-start(bf16[1,4,72,128]{3,2,1,0:T(8,128)(2,1)S(1)} %dynamic-slice_convert_fusion.2), channel_id=1, source_target_pairs={{0,14},{1,15},{2,12},{3,13},{4,10},{5,11},{6,8},{7,9},{8,6},{9,7},... | collective-permute-start | bytes 221192 | tf_op jit(solution)/shard_map/ppermute | solution.py:306
  106.0 6.2 %collective-permute-start.5 = (f32[2,72,128]{2,1,0:T(8,128)S(1)}, f32[2,72,128]{2,1,0:T(8,128)S(1)}, u32[]{:S(2)}, u32[]{:S(2)}) collective-permute-start(f32[2,72,128]{2,1,0:T(8,128)S(1)} %dynamic-slice_bitcast_fusion), channel_id=1, source_target_pairs={{0,16},{16,0},{32,48},{48,32},{64,80},{80,64},{96,112},{112,96},{1... | collective-permute-start | bytes 221192 | tf_op jit(solution)/shard_map/ppermute | solution.py:306
  112.2 6.4 %collective-permute-start.6 = (f32[1,72,128]{2,1,0:T(8,128)S(1)}, f32[1,72,128]{2,1,0:T(8,128)S(1)}, u32[]{:S(2)}, u32[]{:S(2)}) collective-permute-start(f32[1,72,128]{2,1,0:T(8,128)S(1)} %constant_dynamic-slice_fusion.2), channel_id=1, source_target_pairs={{0,48},{16,32},{32,16},{48,0},{64,112},{80,96},{96,80},{112,64},{1... | collective-permute-start | bytes 110600 | tf_op jit(solution)/shard_map/ppermute | solution.py:306
  119.7 20.2 %all-to-all-start.2 = ((bf16[12,72,128]{2,1,0:T(8,128)(2,1)}), bf16[12,72,128]{2,1,0:T(8,128)(2,1)S(1)}, u32[]{:S(2)}, u32[]{:S(2)}) async-start(bf16[12,72,128]{2,1,0:T(8,128)(2,1)} %broadcast_in_dim.44), calls=%async_computation.2 | async-start | bytes 442368 | tf_op jit(solution)/shard_map/all_to_all | solution.py:348
  130.4 7.0 %collective-permute-start.7 = (f32[8,64,128]{2,1,0:T(8,128)S(1)}, f32[8,64,128]{2,1,0:T(8,128)S(1)}, u32[]{:S(2)}, u32[]{:S(2)}) collective-permute-start(f32[8,64,128]{2,1,0:T(8,128)S(1)} %constant_dynamic-slice_fusion), channel_id=1, source_target_pairs={{0,1},{1,0},{2,3},{3,2},{4,5},{5,4},{6,7},{7,6},{8,9},{9,8},{10,11... | collective-permute-start | bytes 786440 | tf_op jit(solution)/shard_map/ppermute | solution.py:306
  140.0 11.3 %collective-permute-start.8 = (bf16[1,72,128]{2,1,0:T(8,128)(2,1)S(1)}, bf16[1,72,128]{2,1,0:T(8,128)(2,1)S(1)}, u32[]{:S(2)}, u32[]{:S(2)}) collective-permute-start(bf16[1,72,128]{2,1,0:T(8,128)(2,1)S(1)} %bitcast.49), channel_id=1, source_target_pairs={{0,48},{16,32},{32,16},{48,0},{64,112},{80,96},{96,80},{112,64},{1... | collective-permute-start | bytes 55304 | tf_op jit(solution)/shard_map/ppermute | solution.py:306
  144.6 16.1 %all-to-all-start.3 = ((f32[8,64,128]{2,1,0:T(8,128)}), f32[8,64,128]{2,1,0:T(8,128)S(1)}, u32[]{:S(2)}, u32[]{:S(2)}) async-start(f32[8,64,128]{2,1,0:T(8,128)} %dynamic-slice_add_fusion), calls=%async_computation.3 | async-start | bytes 524288 | tf_op jit(solution)/shard_map/all_to_all | solution.py:348
  151.3 4.7 %collective-permute-start.9 = (bf16[2,72,128]{2,1,0:T(8,128)(2,1)S(1)}, bf16[2,72,128]{2,1,0:T(8,128)(2,1)S(1)}, u32[]{:S(2)}, u32[]{:S(2)}) collective-permute-start(bf16[2,72,128]{2,1,0:T(8,128)(2,1)S(1)} %pad_maximum_fusion.2), channel_id=1, source_target_pairs={{0,16},{16,0},{32,48},{48,32},{64,80},{80,64},{96,112},{112,96},{1... | collective-permute-start | bytes 110600 | tf_op jit(solution)/shard_map/ppermute | solution.py:306
  177.9 11.6 %collective-permute-start.10 = (bf16[8,352,128]{2,1,0:T(8,128)(2,1)S(1)}, bf16[8,352,128]{2,1,0:T(8,128)(2,1)S(1)}, u32[]{:S(2)}, u32[]{:S(2)}) collective-permute-start(bf16[8,352,128]{2,1,0:T(8,128)(2,1)S(1)} %all_to_all.25.mine_ref), channel_id=1, source_target_pairs={{0,1},{1,0},{2,3},{3,2},{4,5},{5,4},{6,7},{7,6},{8,9},{9,8},{10,11... | collective-permute-start | bytes 2162696 | tf_op jit(solution)/shard_map/ppermute | solution.py:306
